TPU v7x, 512 devices: a whole 4x8x8 slice. The times are simulated.
512 devices in a mesh: grp: 8 (over y), tp: 16 (over z, x_lo), rep: 4 (over x_hi, core).
Axes of the slice: x: 4 (x_hi: 2, x_lo: 2; x = x_hi * 2 + x_lo), y: 8, z: 8, core: 2. Of those that a mesh axis runs over, the one named last changes fastest.
Arguments:
- hist: bfloat16 [1024, 4096], P('grp', ('tp', 'rep')), may hold values from -6 to 6
- tower_gain: bfloat16 [1, 4096], P(None, ('tp', 'rep')), may hold values from 0.5 to 1.5
- up_w: bfloat16 [4096, 8192], P(None, ('tp', 'rep')), may hold values from -0.09375 to 0.09375
- down_w: bfloat16 [8192, 4096], P(('tp', 'rep')), may hold values from -0.0625 to 0.0625
- query: bfloat16 [4096], P(('tp', 'rep')), may hold values from -0.19921875 to 0.19921875
- proj_w: bfloat16 [4096, 2048], P(('tp', 'rep')), may hold values from -0.09375 to 0.09375
- cand: bfloat16 [16384, 2048], P(('grp', 'tp', 'rep')), may hold values from -6 to 6
- owner: int32 [16384], P(('grp', 'tp', 'rep')), may hold values from 0 to 4, as said below
- task: int32 [16384], P(('grp', 'tp', 'rep')), may hold values from 0 to 3
- cross_u: bfloat16 [2048, 128], replicated, may hold values from -0.125 to 0.125
- cross_v: bfloat16 [128, 2048], replicated, may hold values from -0.5 to 0.5
- cross_bias: bfloat16 [2048], replicated, may hold values from -3 to 3
- gate_w: bfloat16 [2048, 12], replicated, may hold values from -0.125 to 0.125
- expert_w: bfloat16 [3, 2048, 8192], P(None, None, ('tp', 'rep')), may hold values from -0.125 to 0.125
- head_w: bfloat16 [4, 3, 8192], P(None, None, ('tp', 'rep')), may hold values from -0.0625 to 0.0625
Outputs:
- score: float32 [16384], P(('grp', 'tp', 'rep'))
Inputs may be any that keep to these rules, and one draw needn't show every extreme that they name: owner is a request among the 4 of the slot's index of grp, or 4 for an empty slot; on every device the live slots come before the empty ones, and every device has an empty slot.
All inputs are finite; a program needn't handle non-finite values.
Results may differ from a plain program's by a relative error of at most 0.04.
Values may be sent and summed in bfloat16 or wider, within the bound.
No kernel may reach another device: no remote copies, remote signals or barrier semaphores. Data moves between devices by JAX's collectives and lax.ppermute only.
A program may use at most 64 MiB of HBM per device.

v0:
```python
import math

import jax
import jax.numpy as jnp
from jax import lax
from jax.sharding import PartitionSpec as P

D = 4096
EXPERTS = 3
TASKS = 4
REQ_GRP = 4
HIST = 32


epsilon = 1e-05


def expert_terms(rows, weights, heads):
    active = jnp.einsum("ne,keh->knh", rows, weights, preferred_element_type=jnp.float32)
    active = jax.nn.relu(active).astype(jnp.bfloat16)
    terms = jnp.einsum("knh,tkh->nkt", active, heads, preferred_element_type=jnp.float32)
    return terms.reshape(rows.shape[0], heads.shape[1] * heads.shape[0])


def body(
    hist,
    tower_gain,
    up_w,
    down_w,
    query,
    proj_w,
    cand,
    owner,
    task,
    cross_u,
    cross_v,
    cross_bias,
    gate_w,
    expert_w,
    head_w,
):
    slots = cand.shape[0]
    cols = lax.all_gather(hist, ("tp", "rep"), axis=1, tiled=True)
    gains = lax.all_gather(tower_gain, ("tp", "rep"), axis=1, tiled=True)
    cols_f = cols.astype(jnp.float32)
    scaled = (cols_f * gains.astype(jnp.float32)).astype(jnp.bfloat16)
    total = jnp.dot(scaled, up_w, preferred_element_type=jnp.float32)
    squares = jnp.sum(cols_f * cols_f, axis=1)
    total, squares = (total, squares)
    inverse = lax.rsqrt(squares / D + epsilon)
    hidden = jax.nn.gelu(total * inverse[:, None]).astype(jnp.bfloat16)
    summed = lax.psum_scatter(
        lax.dot_general(
            down_w, hidden, (((0,), (1,)), ((), ())), preferred_element_type=jnp.float32
        ),
        ("tp", "rep"),
        scatter_dimension=0,
        tiled=True,
    )
    tower_out = (hist.T.astype(jnp.float32) + summed).astype(jnp.bfloat16)
    out_f = tower_out.astype(jnp.float32)
    part_squares = jnp.sum(out_f * out_f, axis=0)
    part_dotted = jnp.sum(out_f * query.astype(jnp.float32)[:, None], axis=0)
    values = lax.dot_general(
        tower_out, proj_w, (((0,), (0,)), ((), ())), preferred_element_type=jnp.float32
    )
    values_all, squares_all, dotted_all = lax.psum(
        (values, part_squares, part_dotted), ("tp", "rep")
    )
    weight = jax.nn.sigmoid(dotted_all * lax.rsqrt(squares_all / D + epsilon))
    user = jnp.sum(
        (weight[:, None] * values_all).reshape(REQ_GRP, HIST, values.shape[1]), axis=1
    ) / math.sqrt(HIST)
    owner_hot = (owner[:, None] == jnp.arange(REQ_GRP)[None, :]).astype(jnp.float32)
    added = jnp.dot(
        owner_hot, user, precision=lax.Precision.HIGHEST, preferred_element_type=jnp.float32
    )
    x0 = (cand.astype(jnp.float32) + added).astype(jnp.bfloat16)
    low = jnp.dot(x0, cross_u, preferred_element_type=jnp.float32).astype(jnp.bfloat16)
    x0_f = x0.astype(jnp.float32)
    cross = (
        jnp.dot(low, cross_v, preferred_element_type=jnp.float32)
        + cross_bias.astype(jnp.float32)[None, :]
    )
    x1 = (x0_f * cross + x0_f).astype(jnp.bfloat16)
    task_hot = (task[:, None] == jnp.arange(TASKS)[None, :]).astype(jnp.float32)
    logits = jnp.dot(x1, gate_w, preferred_element_type=jnp.float32).reshape(slots, TASKS, EXPERTS)
    picked = jax.nn.sigmoid(jnp.sum(logits * task_hot[:, :, None], axis=1))
    gates = picked / jnp.sum(picked, axis=1, keepdims=True)
    terms = expert_terms(lax.all_gather(x1, ("tp", "rep"), axis=0, tiled=True), expert_w, head_w)
    mine = lax.psum_scatter(terms, ("tp", "rep"), scatter_dimension=0, tiled=True)
    expert_out = jnp.sum(mine.reshape(slots, EXPERTS, TASKS) * task_hot[:, None, :], axis=2)
    score = jnp.sum(gates * expert_out, axis=1)
    return jnp.where(owner < REQ_GRP, score, jnp.float32(0.0))


def solution(mesh):
    in_specs = (
        P("grp", ("tp", "rep")),
        P(None, ("tp", "rep")),
        P(None, ("tp", "rep")),
        P(("tp", "rep"), None),
        P(("tp", "rep")),
        P(("tp", "rep"), None),
        P(("grp", "tp", "rep"), None),
        P(("grp", "tp", "rep")),
        P(("grp", "tp", "rep")),
        P(),
        P(),
        P(),
        P(),
        P(None, None, ("tp", "rep")),
        P(None, None, ("tp", "rep")),
    )
    out_specs = P(("grp", "tp", "rep"))
    return jax.shard_map(body, mesh=mesh, in_specs=in_specs, out_specs=out_specs, check_vma=False)
```

profile of v0, /device:TPU:56, one launch (start us, length us, event | category | flops | bytes accessed | tf_op | source)
XLA Modules:
  0.0 1013.7 jit_solution(17781265301011389638)
XLA Ops:
  6.5 0.0 copy-start
  6.5 0.0 all-gather.3.cloned.1.call-start
  6.5 0.7 all-gather.3.cloned.1.call-update
  7.3 0.0 reduce-scatter.7.cloned.1.call-start
  7.3 1.3 dynamic-slice
  9.2 0.9 dynamic-update-slice
  10.1 136.8 %all-reduce = bf16[4096]{0:T(1024)(128)(2,1)S(1)} all-reduce(bf16[4096]{0:T(1024)(128)(2,1)S(1)} %dynamic-update-slice), channel_id=1, replica_groups=mesh['grp'=8,'tp'=16,'rep'=4] {'tp','rep'}, use_global_device_ids=true, to_apply=%add | all-reduce | flops 4096 | bytes 16384
  147.0 0.0 all-gather.3.cloned.1.call-done
  147.0 1.8 fusion.12
  148.8 4.7 convolution_bitcast_fusion
  153.5 2.9 copy.20
  156.4 0.0 reduce-scatter.7.cloned.1.call-update
  156.4 0.0 copy-start.4
  156.4 0.0 copy-start.8
  156.4 0.0 copy-start.1
  156.5 0.0 copy-start.2
  156.5 0.0 all-reduce.4.cloned.1.call-start
  156.5 0.5 copy-done.11
  157.0 257.9 %reduce-scatter.7.cloned.1.call-done = f32[64,128]{1,0:T(8,128)} async-done(((f32[4096,128]{1,0:T(8,128)}), f32[64,128]{1,0:T(8,128)}) %reduce-scatter.7.cloned.1.call-update) | async-done | bytes 32784 | tf_op jit(solution)/shard_map/reduce_scatter | solution.py:52
  415.0 0.0 copy-done.6
  415.0 0.9 fusion.33
  415.8 0.0 copy-done.3
  415.8 1.4 fusion.52
  417.2 0.0 all-reduce.4.cloned.1.call-update
  417.2 0.0 all-gather.5.cloned.1.call-start
  417.3 0.0 copy-done.7
  417.3 124.3 %all-reduce.1 = (f32[128]{0:T(128)S(1)}, f32[128]{0:T(128)S(1)}) all-reduce(f32[128]{0:T(128)S(1)} %get-tuple-element.6, f32[128]{0:T(128)S(1)} %get-tuple-element.5), channel_id=1, replica_groups=mesh['grp'=8,'tp'=16,'rep'=4] {'tp','rep'}, use_global_device_ids=true, to_apply=%region_3.0 | all-reduce | flops 256 | bytes 2048 | tf_op jit(solution)/shard_map/psum | solution.py:67
  541.6 69.8 %all-reduce.4.cloned.1.call-done = f32[128,2048]{1,0:T(8,128)} async-done(((f32[128,2048]{1,0:T(8,128)}), f32[128,2048]{1,0:T(8,128)}) %all-reduce.4.cloned.1.call-update) | async-done | bytes 1048592 | tf_op jit(solution)/shard_map/psum | solution.py:67
  611.4 1.4 bitcast_reduce_fusion
  612.8 0.0 copy-done.4
  612.8 0.0 copy-done.8
  612.8 0.3 fusion.9
  613.1 0.0 copy-done.1
  613.1 0.0 copy-done.2
  613.2 1.1 fusion.10
  614.2 0.0 all-gather.5.cloned.1.call-update
  614.2 0.0 reduce-scatter.9.cloned.1.call-start
  614.3 0.0 copy-done.9
  614.3 0.0 copy-done.5
  614.3 1.0 fusion.53
  615.4 119.2 %all-gather.5.cloned.1.call-done = bf16[2048,2048]{1,0:T(8,128)(2,1)} async-done(((bf16[32,2048]{1,0:T(8,128)(2,1)}), bf16[2048,2048]{1,0:T(8,128)(2,1)}) %all-gather.5.cloned.1.call-update) | async-done | bytes 8388624 | tf_op jit(solution)/shard_map/all_gather | solution.py:90
  734.6 8.3 convolution_bitcast_fusion.1
  742.9 0.1 reshape.62
  742.9 1.4 copy.22
  744.3 0.0 reduce-scatter.9.cloned.1.call-update
  744.4 261.5 %reduce-scatter.9.cloned.1.call-done = f32[32,12]{1,0:T(8,128)} async-done(((f32[2048,12]{1,0:T(8,128)}), f32[32,12]{1,0:T(8,128)}) %reduce-scatter.9.cloned.1.call-update) | async-done | bytes 1552
  1005.8 0.8 copy.23
  1006.7 0.5 compare_select_fusion
  (22 shorter events, 0.2 us)
Async XLA Ops:
  6.5 728.1 %copy-start = (bf16[3,2048,128]{2,1,0:T(8,128)(2,1)S(1)}, bf16[3,2048,128]{2,1,0:T(8,128)(2,1)}, u32[]{:S(2)}) copy-start(bf16[3,2048,128]{2,1,0:T(8,128)(2,1)} %param.28) | copy-start | bytes 4718596
  6.5 140.4 %all-gather.3.cloned.1.call-start = ((), (), s32[]{:S(2)}) async-start(), calls=%async_computation.2 | async-start | bytes 1064960 | tf_op jit(solution)/shard_map/all_gather | solution.py:43
  7.3 407.7 %reduce-scatter.7.cloned.1.call-start = ((), (), s32[]{:S(2)}) async-start(), calls=%async_computation.5 | async-start | bytes 2129920 | tf_op jit(solution)/shard_map/reduce_scatter | solution.py:52
  156.4 0.7 copy-start.11
  156.4 258.6 %copy-start.6 = (bf16[128,64]{0,1:T(8,128)(2,1)S(1)}, bf16[128,64]{0,1:T(8,128)(2,1)}, u32[]{:S(2)}) copy-start(bf16[128,64]{0,1:T(8,128)(2,1)} %param.15) | copy-start | bytes 49156
  156.4 259.5 %copy-start.3 = (bf16[64,2048]{1,0:T(8,128)(2,1)S(1)}, bf16[64,2048]{1,0:T(8,128)(2,1)}, u32[]{:S(2)}) copy-start(bf16[64,2048]{1,0:T(8,128)(2,1)} %param.20) | copy-start | bytes 786436
  156.4 260.9 %copy-start.7 = (bf16[2048]{0:T(1024)(128)(2,1)S(1)}, bf16[2048]{0:T(1024)(128)(2,1)}, u32[]{:S(2)}) copy-start(bf16[2048]{0:T(1024)(128)(2,1)} %param.26) | copy-start | bytes 12292
  156.4 456.4 %copy-start.4 = (bf16[32,2048]{1,0:T(8,128)(2,1)S(1)}, bf16[32,2048]{1,0:T(8,128)(2,1)}, u32[]{:S(2)}) copy-start(bf16[32,2048]{1,0:T(8,128)(2,1)} %param.21) | copy-start | bytes 393220
  156.4 456.4 %copy-start.8 = (s32[32]{0:T(128)S(1)}, s32[32]{0:T(128)}, u32[]{:S(2)}) copy-start(s32[32]{0:T(128)} %param.22) | copy-start | bytes 388
  156.4 456.7 %copy-start.1 = (bf16[128,2048]{1,0:T(8,128)(2,1)S(1)}, bf16[128,2048]{1,0:T(8,128)(2,1)}, u32[]{:S(2)}) copy-start(bf16[128,2048]{1,0:T(8,128)(2,1)} %param.25) | copy-start | bytes 1572868
  156.5 456.7 %copy-start.2 = (bf16[2048,128]{1,0:T(8,128)(2,1)S(1)}, bf16[2048,128]{1,0:T(8,128)(2,1)}, u32[]{:S(2)}) copy-start(bf16[2048,128]{1,0:T(8,128)(2,1)} %param.24) | copy-start | bytes 1572868
  156.5 454.9 %all-reduce.4.cloned.1.call-start = ((), (), s32[]{:S(2)}) async-start(), calls=%async_computation.3 | async-start | bytes 2097152 | tf_op jit(solution)/shard_map/psum | solution.py:67
  417.2 197.1 %copy-start.9 = (s32[32]{0:T(128)S(1)}, s32[32]{0:T(128)}, u32[]{:S(2)}) copy-start(s32[32]{0:T(128)} %param.23) | copy-start | bytes 388
  417.2 197.1 %copy-start.5 = (bf16[2048,12]{0,1:T(8,128)(2,1)S(1)}, bf16[2048,12]{0,1:T(8,128)(2,1)}, u32[]{:S(2)}) copy-start(bf16[2048,12]{0,1:T(8,128)(2,1)} %param.27) | copy-start | bytes 147460
  417.2 317.4 %copy-start.10 = (bf16[4,3,128]{2,0,1:T(4,128)(2,1)S(1)}, bf16[4,3,128]{2,0,1:T(4,128)(2,1)}, u32[]{:S(2)}) copy-start(bf16[4,3,128]{2,0,1:T(4,128)(2,1)} %param.29) | copy-start | bytes 9220
  417.2 317.4 %all-gather.5.cloned.1.call-start = ((), (), s32[]{:S(2)}) async-start(), calls=%async_computation.4 | async-start | bytes 8519680 | tf_op jit(solution)/shard_map/all_gather | solution.py:90
  614.2 391.6 %reduce-scatter.9.cloned.1.call-start = ((), (), s32[]{:S(2)}) async-start(), calls=%async_computation.6 | async-start | bytes 1064960
Sparse Core Ops, SparseCore 0:
  9.5 119.6 all-gather.2
  156.5 258.3 reduce-scatter.6
  418.8 192.5 all-reduce.3
  614.4 120.1 all-gather.4
  744.4 261.3 reduce-scatter.8
where the time goes:
time: 1010 us
  waiting for transfers between devices  709 us (70%)
  blocking collectives  261 us (26%)
  matrix products  16.7 us (2%)
  between operations  14 us (1%)
    unnamed x6, waiting for transfers between devices  262 us
    reduce_scatter x1, waiting for transfers between devices, body(): lax.psum_scatter(lax.dot_general(down_w, hidden, (((0,), (1,)), ((), ()))...  258 us
    unnamed x1, blocking collectives  137 us
    psum x1, blocking collectives, body(): lax.psum((values, part_squares, part_dotted), ('tp', 'rep'))  124 us
    all_gather x1, waiting for transfers between devices, body(): lax.all_gather(x1, ('tp', 'rep'), axis=0, tiled=True)  119 us
    psum x1, waiting for transfers between devices, body(): lax.psum((values, part_squares, part_dotted), ('tp', 'rep'))  69.8 us
  transfers between devices with their start and end apart: 5, of which 4 were waited for; matrix products, arithmetic and copies ran while one was open for 0% of the time, Pallas kernels for 0%

commit v1 on v0

v1 whole, which is shorter than its diff:
```python
import math

import jax
import jax.numpy as jnp
from jax import lax
from jax.experimental import pallas as pl
from jax.experimental.pallas import tpu as pltpu
from jax.sharding import Mesh, PartitionSpec as P

D = 4096
EXPERTS = 3
TASKS = 4
REQ_GRP = 4
HIST = 32
epsilon = 1e-05

CHIPS = ("z", "xh", "xl")
ALL = ("z", "xh", "xl", "c")
N_CHIPS = 32
F32 = jnp.float32
BF16 = jnp.bfloat16
HIGH = lax.Precision.HIGHEST

VMEM = pl.BlockSpec(memory_space=pltpu.VMEM)


def params(mib):
    return pltpu.CompilerParams(vmem_limit_bytes=mib << 20)


def block_of(chip):
    return (chip & ~3) | ((chip & 1) << 1) | ((chip >> 1) & 1)


def split2(x):
    high = x.astype(BF16).astype(F32)
    return high, x - high


def lanes(shape):
    return lax.broadcasted_iota(jnp.int32, shape, len(shape) - 1)


def rows(shape):
    return lax.broadcasted_iota(jnp.int32, shape, len(shape) - 2)


def token_sums(x):
    padded = jnp.concatenate([x, jnp.zeros_like(x)], axis=0)
    return lax.dot_general(
        jnp.ones((16, 128), F32), padded, (((1,), (1,)), ((), ())), precision=HIGH, preferred_element_type=F32
    )


def spread_kernel(pair_ref, slots_ref, out_ref, hist_ref, query_ref):
    core = lax.axis_index("c")
    tokens = pl.ds(pl.multiple_of(core * 64, 64), 64)
    first = pair_ref[0, tokens, :].astype(F32)
    second = pair_ref[1, tokens, :].astype(F32)
    low = lanes((64, 128)) < 64
    hist = jnp.where(low, first, pltpu.roll(second, 64, 1))
    head0 = pair_ref[0, 128:144, :].astype(F32)[0:1]
    head1 = pair_ref[1, 128:144, :].astype(F32)[0:1]
    low1 = lanes((1, 128)) < 64
    gain = jnp.where(low1, head0, pltpu.roll(jnp.broadcast_to(head1, (8, 128)), 64, 1)[0:1])
    query = jnp.where(low1, pltpu.roll(jnp.broadcast_to(head0, (8, 128)), 64, 1)[0:1], head1)
    scaled = (hist * gain).astype(BF16)
    high, rest = split2(token_sums(hist * hist))
    owner = slots_ref[0:1, :].astype(F32)
    task = slots_ref[1:2, :].astype(F32)
    row = rows((16, 128))
    extra = jnp.where(row == 0, high, jnp.where(row == 1, rest, jnp.where(row == 2, owner, jnp.where(row == 3, task, 0.0))))
    extra = extra.astype(BF16)
    for chip in range(N_CHIPS):
        out_ref[chip, 0:64, :] = scaled
        out_ref[chip, 64:80, :] = extra
    hist_ref[...] = hist.astype(BF16)
    query_ref[...] = jnp.broadcast_to(query, (8, 128))


def tower_kernel(got_ref, up0_ref, up1_ref, down0_ref, down1_ref, out_ref, owner_ref, task_ref):
    stats = jnp.zeros((16, 128), F32)
    extras = []
    for chip in range(N_CHIPS):
        extra = got_ref[chip, 64:80, :].astype(F32)
        stats = stats + extra
        extras.append(extra)
    quarter = lanes((1, 128)) // 32
    owners, tasks = [], []
    for b in range(8):
        owner = jnp.zeros((1, 128), F32)
        task = jnp.zeros((1, 128), F32)
        for q in range(4):
            owner = jnp.where(quarter == q, extras[4 * b + q][2:3], owner)
            task = jnp.where(quarter == q, extras[4 * b + q][3:4], task)
        owners.append(owner)
        tasks.append(task)
    owner_ref[...] = jnp.concatenate(owners, axis=0)
    task_ref[...] = jnp.concatenate(tasks, axis=0)
    inverse = lax.rsqrt((stats[0:1] + stats[1:2]) / D + epsilon)
    column = jnp.broadcast_to(inverse, (128, 128)).T[0:64]
    total = jnp.zeros((64, 256), F32)
    for b in range(0, N_CHIPS, 2):
        left = jnp.concatenate([got_ref[block_of(b), 0:64, :], got_ref[block_of(b + 1), 0:64, :]], axis=1)
        right = jnp.concatenate([up0_ref[b * 128 : b * 128 + 256, :], up1_ref[b * 128 : b * 128 + 256, :]], axis=1)
        total = total + jnp.dot(left, right, preferred_element_type=F32)
    hidden = jax.nn.gelu(total * jnp.concatenate([column, column], axis=1)).astype(BF16)
    for b in range(0, N_CHIPS, 2):
        right = jnp.concatenate([down0_ref[:, b * 128 : b * 128 + 256], down1_ref[:, b * 128 : b * 128 + 256]], axis=0)
        part = jnp.dot(hidden, right, preferred_element_type=F32).astype(BF16)
        out_ref[block_of(b), :, :] = part[:, 0:128]
        out_ref[block_of(b + 1), :, :] = part[:, 128:256]


def values_kernel(got_ref, hist_ref, query_ref, proj0_ref, proj1_ref, out_ref):
    core = lax.axis_index("c")
    summed = got_ref[0].astype(F32)
    for chip in range(1, N_CHIPS):
        summed = summed + got_ref[chip].astype(F32)
    tower = (hist_ref[...].astype(F32) + summed).astype(BF16).astype(F32)
    square_high, square_rest = split2(token_sums(tower * tower))
    dot_high, dot_rest = split2(token_sums(tower * query_ref[0:1, :]))
    row = rows((16, 128))
    extra = jnp.where(
        row == 0, square_high, jnp.where(row == 1, square_rest, jnp.where(row == 2, dot_high, jnp.where(row == 3, dot_rest, 0.0)))
    ).astype(BF16)
    mine = jnp.where(core == 0, tower, pltpu.roll(tower, 64, 1)).astype(BF16)
    low = lanes((32, 128)) < 64
    for j in range(16):
        cols = slice(128 * j, 128 * j + 128)
        right = jnp.concatenate([proj0_ref[:, cols], proj1_ref[:, cols]], axis=0)
        part = jnp.dot(mine, right, preferred_element_type=F32)
        turned = pltpu.roll(part, 64, 1)
        out_ref[2 * j, 0:32, :] = jnp.where(low, part[0:32], turned[32:64]).astype(BF16)
        out_ref[2 * j + 1, 0:32, :] = jnp.where(low, turned[0:32], part[32:64]).astype(BF16)
        out_ref[2 * j, 32:48, :] = extra
        out_ref[2 * j + 1, 32:48, :] = extra


def user_kernel(got_ref, out_ref):
    values = got_ref[0].astype(F32)
    for chip in range(1, N_CHIPS):
        values = values + got_ref[chip].astype(F32)
    stats = values[32:48]
    squares = stats[0:1] + stats[1:2]
    dotted = stats[2:3] + stats[3:4]
    weight = jax.nn.sigmoid(dotted * lax.rsqrt(squares / D + epsilon))
    column = jnp.broadcast_to(weight, (128, 128)).T
    weights = jnp.where(lanes((32, 128)) < 64, column[0:32], column[32:64])
    user = jnp.sum(weights * values[0:32], axis=0, keepdims=True) / math.sqrt(HIST)
    out_ref[...] = jnp.broadcast_to(user, (64, 128))


ROWS = 256


def score_kernel(
    user_ref, cand_ref, owner_ref, task_ref, pair_ref, cross_u_ref, cross_v_ref, bias_ref, gate_ref, w0_ref, w1_ref,
    out_ref, users, x0s, x1s,
):
    core = lax.axis_index("c")
    step = pl.program_id(0)

    @pl.when(step == 0)
    def _():
        got = user_ref[...]
        turned = pltpu.roll(got, 64, 1)
        row = rows((16, 128))
        low = lanes((1, 128)) < 64
        for j in range(16):
            a = 4 * j
            picks = []
            for c in range(2):
                picks.append(jnp.where(low, got[a + c : a + c + 1], turned[a + 2 + c : a + 3 + c]))
                picks.append(jnp.where(low, turned[a + c : a + c + 1], got[a + 2 + c : a + 3 + c]))
            r4 = row % 4
            full = jnp.where(r4 == 0, picks[0], jnp.where(r4 == 1, picks[1], jnp.where(r4 == 2, picks[2], picks[3])))
            high, rest = split2(full)
            mid, last = split2(rest)
            users[:, 128 * j : 128 * j + 128] = jnp.where(
                row < 4, high, jnp.where(row < 8, mid, jnp.where(row < 12, last, 0.0))
            ).astype(BF16)

    owner = jnp.concatenate([owner_ref[pl.ds(2 * step, 1), :], owner_ref[pl.ds(2 * step + 1, 1), :]], axis=1)
    task = jnp.concatenate([task_ref[pl.ds(2 * step, 1), :], task_ref[pl.ds(2 * step + 1, 1), :]], axis=1)
    row = rows((16, ROWS))
    hot = jnp.where((row % 4).astype(F32) == owner, 1.0, 0.0)
    hot = hot.T.astype(BF16)
    low = jnp.zeros((ROWS, 128), F32)
    for j in range(8):
        cols = slice(256 * j, 256 * j + 256)
        added = jnp.dot(hot, users[:, cols], preferred_element_type=F32)
        x0 = (cand_ref[:, cols].astype(F32) + added).astype(BF16)
        x0s[:, cols] = x0
        low = low + jnp.dot(x0, cross_u_ref[cols, :], preferred_element_type=F32)
    low = low.astype(BF16)
    for j in range(8):
        cols = slice(256 * j, 256 * j + 256)
        cross = jnp.dot(low, cross_v_ref[:, cols], preferred_element_type=F32) + bias_ref[:, cols].astype(F32)
        x0 = x0s[:, cols].astype(F32)
        x1s[:, cols] = (x0 * cross + x0).astype(BF16)
    contract = (((1,), (1,)), ((), ()))
    logits = lax.dot_general(gate_ref[...], x1s[...], contract, preferred_element_type=F32)
    heads = jnp.concatenate([pair_ref[core, 144:160, :], pair_ref[1 - core, 144:160, :]], axis=1)
    terms = []
    for k in range(EXPERTS):
        total = jnp.zeros((ROWS, 256), F32)
        for j in range(8):
            cols = slice(256 * j, 256 * j + 256)
            right = jnp.concatenate([w0_ref[k, cols, :], w1_ref[k, cols, :]], axis=1)
            total = total + jnp.dot(x1s[:, cols], right, preferred_element_type=F32)
        active = jax.nn.relu(total).astype(BF16)
        terms.append(lax.dot_general(heads, active, contract, preferred_element_type=F32))
    mine = (row // 3).astype(F32) == task
    picked = jnp.where(mine, jax.nn.sigmoid(logits), 0.0)
    term = jnp.where(row % 3 == 0, terms[0], jnp.where(row % 3 == 1, terms[1], terms[2]))
    gates = picked / jnp.sum(picked, axis=0, keepdims=True)
    part = jnp.sum(jnp.where(mine, gates * term, 0.0), axis=0, keepdims=True)
    for half in range(2):
        out_ref[4 * half : 4 * half + 4, :] = jnp.broadcast_to(part[:, 128 * half : 128 * half + 128], (4, 128))


def home_kernel(got_ref, slots_ref, out_ref):
    place = lax.axis_index("xh") * 2 + lax.axis_index("xl")
    total = jnp.sum(got_ref[...], axis=0, keepdims=True)
    lane = lanes((1, 128))
    quarters = [total] + [pltpu.roll(jnp.broadcast_to(total, (8, 128)), 128 - 32 * q, 1)[0:1] for q in range(1, 4)]
    mine = jnp.where(place == 0, quarters[0], jnp.where(place == 1, quarters[1], jnp.where(place == 2, quarters[2], quarters[3])))
    out_ref[...] = jnp.where(slots_ref[0:1, :] < REQ_GRP, mine, 0.0)


def body(
    hist, tower_gain, up_w, down_w, query, proj_w, cand, owner, task, cross_u, cross_v, cross_bias, gate_w, expert_w, head_w,
):
    everyone = lax.all_gather(cand, CHIPS, axis=0, tiled=True)
    swap = lambda x: lax.ppermute(x, "c", [(0, 1), (1, 0)])
    ends = jnp.concatenate([tower_gain, query[None, :]], axis=1)
    message = jnp.concatenate(
        [jnp.pad(hist, ((0, 0), (0, 64))), jnp.pad(ends, ((0, 15), (0, 0))), jnp.pad(head_w.reshape(12, 128), ((0, 4), (0, 0)))],
        axis=0,
    )
    pair = lax.all_gather(message, "c", axis=0)
    up_other = swap(up_w)
    down_other = swap(down_w)
    slots = jnp.concatenate([jnp.tile(owner[None, :], (1, 4)), jnp.tile(task[None, :], (1, 4))], axis=0)
    spread, hist_c, query_c = pl.pallas_call(
        spread_kernel,
        out_shape=(
            jax.ShapeDtypeStruct((N_CHIPS, 80, 128), BF16),
            jax.ShapeDtypeStruct((64, 128), BF16),
            jax.ShapeDtypeStruct((8, 128), F32),
        ),
        in_specs=[VMEM] * 2,
        out_specs=(VMEM,) * 3,
        compiler_params=params(8),
    )(pair, slots)
    tokens = lax.all_to_all(spread, CHIPS, 0, 0, tiled=True)
    proj_other = swap(proj_w)
    expert_other = swap(expert_w)
    parts, owners, tasks = pl.pallas_call(
        tower_kernel,
        out_shape=(
            jax.ShapeDtypeStruct((N_CHIPS, 64, 128), BF16),
            jax.ShapeDtypeStruct((8, 128), F32),
            jax.ShapeDtypeStruct((8, 128), F32),
        ),
        in_specs=[VMEM] * 5,
        out_specs=(VMEM,) * 3,
        compiler_params=params(16),
    )(tokens, up_w, up_other, down_w, down_other)
    summed = lax.all_to_all(parts, CHIPS, 0, 0, tiled=True)
    values = pl.pallas_call(
        values_kernel,
        out_shape=jax.ShapeDtypeStruct((N_CHIPS, 48, 128), BF16),
        in_specs=[VMEM] * 5,
        out_specs=VMEM,
        compiler_params=params(8),
    )(summed, hist_c, query_c, proj_w, proj_other)
    values = lax.all_to_all(values, CHIPS, 0, 0, tiled=True)
    user = pl.pallas_call(
        user_kernel,
        out_shape=jax.ShapeDtypeStruct((64, 128), F32),
        in_specs=[VMEM],
        out_specs=VMEM,
        compiler_params=params(8),
    )(values)
    users = lax.all_to_all(user, ALL, 0, 0, tiled=True)
    gates = jnp.pad(gate_w.T, ((0, 4), (0, 0)))
    whole = lambda *shape: pl.BlockSpec(shape, lambda i: (0,) * len(shape))
    part = pl.pallas_call(
        score_kernel,
        grid=(4,),
        out_shape=jax.ShapeDtypeStruct((N_CHIPS, 128), F32),
        in_specs=[
            whole(64, 128),
            pl.BlockSpec((ROWS, 2048), lambda i: (i, 0)),
            whole(8, 128),
            whole(8, 128),
            whole(2, 160, 128),
            whole(2048, 128),
            whole(128, 2048),
            whole(1, 2048),
            whole(16, 2048),
            whole(3, 2048, 128),
            whole(3, 2048, 128),
        ],
        out_specs=pl.BlockSpec((8, 128), lambda i: (i, 0)),
        scratch_shapes=[
            pltpu.VMEM((16, 2048), BF16),
            pltpu.VMEM((ROWS, 2048), BF16),
            pltpu.VMEM((ROWS, 2048), BF16),
        ],
        compiler_params=params(32),
    )(users, everyone, owners, tasks, pair, cross_u, cross_v, cross_bias[None, :], gates, expert_w, expert_other)
    back = lax.all_to_all(part, CHIPS, 0, 0, tiled=True)
    score = pl.pallas_call(
        home_kernel,
        out_shape=jax.ShapeDtypeStruct((1, 128), F32),
        in_specs=[VMEM] * 2,
        out_specs=VMEM,
        compiler_params=params(4),
    )(back, slots)
    return score[0, 0:32]


def solution(mesh):
    fine = Mesh(mesh.devices.reshape(mesh.devices.shape[0], 8, 2, 2, 2), ("grp", "z", "xl", "xh", "c"))
    t = ("z", "xl", "xh", "c")
    in_specs = (
        P("grp", t),
        P(None, t),
        P(None, t),
        P(t, None),
        P(t),
        P(t, None),
        P(("grp",) + t, None),
        P(("grp",) + t),
        P(("grp",) + t),
        P(),
        P(),
        P(),
        P(),
        P(None, None, t),
        P(None, None, t),
    )
    return jax.shard_map(body, mesh=fine, in_specs=in_specs, out_specs=P(("grp",) + t), check_vma=False)
```

time: 1010 us -> 158 us (0.16)
  waiting for transfers between devices: 709 us -> 39.2 us
  blocking collectives: 261 us -> 38.1 us
  starting transfers between devices: 0.17 us -> 31.8 us
  Pallas kernels: 0 us -> 18.8 us
  matrix products: 16.7 us -> 0 us
    unnamed x6 -> x1, waiting for transfers between devices: 262 us -> 0.71 us
    reduce_scatter x1 -> x0, waiting for transfers between devices: 258 us -> none  [body(): lax.psum_scatter(lax.dot_general(down_w, hidden, (((0,), (1,)), ((), ()))...]
    unnamed x1 -> x0, blocking collectives: 137 us -> none
    psum x1 -> x0, blocking collectives: 124 us -> none  [body(): lax.psum((values, part_squares, part_dotted), ('tp', 'rep'))]
    all_gather x2 -> x1, waiting for transfers between devices: 119 us -> 0.01 us  [body(): everyone = lax.all_gather(cand, CHIPS, axis=0, tiled=True)]
    psum x1 -> x0, waiting for transfers between devices: 69.8 us -> none  [body(): lax.psum((values, part_squares, part_dotted), ('tp', 'rep'))]
    all_to_all x0 -> x2, blocking collectives: none -> 36.2 us  [the longest x1 23.5 us: body(): values = lax.all_to_all(values, CHIPS, 0, 0, tiled=True)]
    all_to_all x0 -> x3, waiting for transfers between devices: none -> 35.4 us  [the longest x1 15.1 us: body(): tokens = lax.all_to_all(spread, CHIPS, 0, 0, tiled=True)]
  transfers between devices with their start and end apart: 5 -> 8, of which waited for: 4 -> 6; matrix products, arithmetic and copies ran while one was open for 0% -> 2% of each run, Pallas kernels for 0% -> 2%
where the time goes in v1:
time: 158 us; the launch traced here: 156 us
  waiting for transfers between devices  39.2 us (25%)
  blocking collectives  38.1 us (24%)
  starting transfers between devices  31.8 us (20%)
  Pallas kernels  18.8 us (12%)
  local copies, waits for them, and re-layouts  14.2 us (9%)
  between operations  13.6 us (9%)
    all_to_all x1, blocking collectives, body(): values = lax.all_to_all(values, CHIPS, 0, 0, tiled=True)  23.5 us
    all_to_all x1, waiting for transfers between devices, body(): tokens = lax.all_to_all(spread, CHIPS, 0, 0, tiled=True)  15.1 us
    pallas_call x1, Pallas kernels, body(): pl.pallas_call(score_kernel, grid=(4,), out_shape=jax.ShapeDtypeStruct((N...  14.9 us
    all_to_all x1, starting transfers between devices, body(): tokens = lax.all_to_all(spread, CHIPS, 0, 0, tiled=True)  13.2 us
    all_to_all x1, blocking collectives, body(): back = lax.all_to_all(part, CHIPS, 0, 0, tiled=True)  12.7 us
    unnamed x30, local copies, waits for them, and re-layouts  12.2 us
    all_to_all x1, waiting for transfers between devices, body(): summed = lax.all_to_all(parts, CHIPS, 0, 0, tiled=True)  10.8 us
    all_to_all x1, waiting for transfers between devices, body(): users = lax.all_to_all(user, ALL, 0, 0, tiled=True)  9.52 us
  transfers between devices with their start and end apart: 8, of which 6 were waited for; matrix products, arithmetic and copies ran while one was open for 2% of the time, Pallas kernels for 2%

profile of v1, /device:TPU:56, one launch (start us, length us, event | category | flops | bytes accessed | tf_op | source)
XLA Modules:
  0.0 156.5 jit_solution(10041265053700098408)
XLA Ops:
  6.5 0.0 all-gather.3.cloned.1.call-start
  6.5 0.7 all-gather.3.cloned.1.call-update
  7.3 0.8 copy.22
  8.1 0.7 copy.23
  8.8 0.7 tile.16
  9.5 0.1 tile.17
  9.5 0.7 tile.18
  10.2 0.1 tile.19
  10.3 0.7 fusion.6
  11.1 1.9 %all-gather = bf16[320,128]{1,0:T(8,128)(2,1)S(1)} all-gather(bf16[160,128]{1,0:T(8,128)(2,1)S(1)} %fusion.2), channel_id=2, replica_groups=mesh['grp'=8,'z'=8,'xl'=2,'xh'=2,'c'=2] {'c'}, dimensions={0}, use_global_device_ids=true | all-gather | bytes 122880 | tf_op jit(solution)/shard_map/all_gather | solution.py:242
  12.9 1.1 shard_map.145
  14.0 13.2 %all-to-all-start = ((bf16[32,80,128]{2,1,0:T(8,128)(2,1)}), bf16[32,80,128]{2,1,0:T(8,128)(2,1)S(1)}, u32[]{:S(2)}, u32[]{:S(2)}) async-start(bf16[32,80,128]{2,1,0:T(8,128)(2,1)} %get-tuple-element.11), calls=%async_computation | async-start | bytes 1310720 | tf_op jit(solution)/shard_map/all_to_all | solution.py:257
  27.2 0.0 copy-done.2
  27.2 0.0 copy-start.1
  27.2 2.1 %collective-permute-start = (bf16[4096,128]{1,0:T(8,128)(2,1)S(1)}, bf16[4096,128]{1,0:T(8,128)(2,1)S(1)}, u32[]{:S(2)}, u32[]{:S(2)}) collective-permute-start(bf16[4096,128]{1,0:T(8,128)(2,1)S(1)} %copy-done.2), channel_id=1, source_target_pairs={{0,1},{1,0},{2,3},{3,2},{4,5},{5,4},{6,7},{7,6},{8,9},{9,8},{10,11... | collective-permute-start | bytes 3145736 | tf_op jit(solution)/shard_map/ppermute | solution.py:236
  29.3 2.4 %collective-permute-start.1 = (bf16[128,4096]{1,0:T(8,128)(2,1)}, bf16[128,4096]{1,0:T(8,128)(2,1)S(1)}, u32[]{:S(2)}, u32[]{:S(2)}) collective-permute-start(bf16[128,4096]{1,0:T(8,128)(2,1)} %down0_ref.1), channel_id=1, source_target_pairs={{0,1},{1,0},{2,3},{3,2},{4,5},{5,4},{6,7},{7,6},{8,9},{9,8},{10,11... | collective-permute-start | bytes 3145736 | tf_op jit(solution)/shard_map/ppermute | solution.py:236
  31.7 0.2 collective-permute-done.up1_ref
  31.9 1.0 copy-done.4
  32.9 1.3 collective-permute-done.1.down1_ref
  34.2 1.0 copy-done.6
  35.2 15.1 %all-to-all-done.got_ref = bf16[32,80,128]{2,1,0:T(8,128)(2,1)S(1)} async-done(((bf16[32,80,128]{2,1,0:T(8,128)(2,1)}), bf16[32,80,128]{2,1,0:T(8,128)(2,1)S(1)}, u32[]{:S(2)}, u32[]{:S(2)}) %all-to-all-start) | async-done | bytes 655392 | tf_op jit(solution)/shard_map/all_to_all | solution.py:257
  50.2 1.2 copy-done.3
  51.5 1.2 copy-done.5
  52.7 1.2 copy-done.7
  53.9 1.4 shard_map.146
  55.3 0.0 copy-start.10
  55.4 0.8 copy-done.10
  56.2 5.1 %all-to-all-start.1 = ((bf16[32,64,128]{2,1,0:T(8,128)(2,1)}), bf16[32,64,128]{2,1,0:T(8,128)(2,1)S(1)}, u32[]{:S(2)}, u32[]{:S(2)}) async-start(bf16[32,64,128]{2,1,0:T(8,128)(2,1)} %copy-done.10), calls=%async_computation.1 | async-start | bytes 1048576 | tf_op jit(solution)/shard_map/all_to_all | solution.py:271
  61.3 0.0 copy-done.1
  61.3 0.0 copy-start.8
  61.3 2.1 %collective-permute-start.3 = (bf16[3,2048,128]{2,1,0:T(8,128)(2,1)S(1)}, bf16[3,2048,128]{2,1,0:T(8,128)(2,1)}, u32[]{:S(2)}, u32[]{:S(2)}) collective-permute-start(bf16[3,2048,128]{2,1,0:T(8,128)(2,1)S(1)} %copy-done.1), channel_id=1, source_target_pairs={{0,1},{1,0},{2,3},{3,2},{4,5},{5,4},{6,7},{7,6},{8,9},{9,8},{10,11... | collective-permute-start | bytes 4718600 | tf_op jit(solution)/shard_map/ppermute | solution.py:236
  63.4 2.4 %collective-permute-start.2 = (bf16[64,2048]{1,0:T(8,128)(2,1)}, bf16[64,2048]{1,0:T(8,128)(2,1)S(1)}, u32[]{:S(2)}, u32[]{:S(2)}) collective-permute-start(bf16[64,2048]{1,0:T(8,128)(2,1)} %proj0_ref.1), channel_id=1, source_target_pairs={{0,1},{1,0},{2,3},{3,2},{4,5},{5,4},{6,7},{7,6},{8,9},{9,8},{10,11... | collective-permute-start | bytes 786440 | tf_op jit(solution)/shard_map/ppermute | solution.py:236
  65.8 1.5 collective-permute-done.2.proj1_ref
  67.3 10.8 %all-to-all-done.1.got_ref = bf16[32,64,128]{2,1,0:T(8,128)(2,1)S(1)} async-done(((bf16[32,64,128]{2,1,0:T(8,128)(2,1)}), bf16[32,64,128]{2,1,0:T(8,128)(2,1)S(1)}, u32[]{:S(2)}, u32[]{:S(2)}) %all-to-all-start.1) | async-done | bytes 524320 | tf_op jit(solution)/shard_map/all_to_all | solution.py:271
  78.2 1.0 copy-done.11
  79.1 0.5 shard_map.147
  79.6 23.5 %all_to_all.37.got_ref = bf16[32,48,128]{2,1,0:T(8,128)(2,1)S(1)} all-to-all(bf16[32,48,128]{2,1,0:T(8,128)(2,1)S(1)} %shard_map.147), channel_id=1, replica_groups=mesh['grp'=8,'z'=8,'xl'=2,'xh'=2,'c'=2] {'z','xh','xl'}, dimensions={0} | all-to-all | bytes 786432 | tf_op jit(solution)/shard_map/all_to_all | solution.py:279
  103.2 0.8 shard_map.148
  103.9 4.6 %all-to-all-start.3 = ((f32[64,1,128]{2,1,0:T(1,128)}), f32[64,1,128]{2,1,0:T(1,128)S(1)}, u32[]{:S(2)}, u32[]{:S(2)}) async-start(f32[64,1,128]{2,1,0:T(1,128)} %bitcast.3), calls=%async_computation.3 | async-start | bytes 65536 | tf_op jit(solution)/shard_map/all_to_all | solution.py:287
  108.6 0.0 collective-permute-done.3.w1_ref
  108.6 9.5 %all-to-all-done.3 = f32[64,1,128]{2,1,0:T(1,128)S(1)} async-done(((f32[64,1,128]{2,1,0:T(1,128)}), f32[64,1,128]{2,1,0:T(1,128)S(1)}, u32[]{:S(2)}, u32[]{:S(2)}) %all-to-all-start.3) | async-done | bytes 32800 | tf_op jit(solution)/shard_map/all_to_all | solution.py:287
  118.1 0.0 copy-done.8
  118.1 2.2 %copy-done = bf16[1024,2048]{1,0:T(8,128)(2,1)S(1)} copy-done((bf16[1024,2048]{1,0:T(8,128)(2,1)S(1)}, bf16[1024,2048]{1,0:T(8,128)(2,1)}, u32[]{:S(2)}) %copy-start) | copy-done | bytes 4194328
  120.3 1.0 copy-done.9
  121.4 14.9 %shard_map.149 = f32[32,128]{1,0:T(8,128)S(1)} custom-call(f32[64,128]{1,0:T(8,128)S(1)} %bitcast.15, bf16[1024,2048]{1,0:T(8,128)(2,1)S(1)} %copy-done, f32[8,128]{1,0:T(8,128)S(1)} %get-tuple-element.15.owner_ref, f32[8,128]{1,0:T(8,128)S(1)} %get-tuple-element.16.task_ref, bf16[2,160,128]{2,1,0:T(8,128)(2,1)S(1)} %bitcast.14, ...), custom_call_target="tpu_custom_call" | custom-call | tf_op jit(solution)/shard_map/pallas_call | solution.py:290
  136.3 12.7 %all_to_all.38 = f32[32,1,128]{2,1,0:T(1,128)S(1)} all-to-all(f32[32,1,128]{2,1,0:T(1,128)S(1)} %bitcast.16), channel_id=1, replica_groups=mesh['grp'=8,'z'=8,'xl'=2,'xh'=2,'c'=2] {'z','xh','xl'}, dimensions={0} | all-to-all | bytes 32768 | tf_op jit(solution)/shard_map/all_to_all | solution.py:315
  149.0 0.1 shard_map.150
  149.1 0.5 slice_bitcast_fusion
  (19 shorter events, 0.1 us)
Async XLA Ops:
  6.5 20.7 %copy-start.2 = (bf16[4096,128]{1,0:T(8,128)(2,1)S(1)}, bf16[4096,128]{1,0:T(8,128)(2,1)}, u32[]{:S(2)}) copy-start(bf16[4096,128]{1,0:T(8,128)(2,1)} %up0_ref.1) | copy-start | bytes 3145732
  6.5 111.6 %all-gather.3.cloned.1.call-start = ((), (), s32[]{:S(2)}) async-start(), calls=%async_computation.5 | async-start | bytes 4325376 | tf_op jit(solution)/shard_map/all_gather | solution.py:235
  14.0 36.2 %all-to-all-start = ((bf16[32,80,128]{2,1,0:T(8,128)(2,1)}), bf16[32,80,128]{2,1,0:T(8,128)(2,1)S(1)}, u32[]{:S(2)}, u32[]{:S(2)}) async-start(bf16[32,80,128]{2,1,0:T(8,128)(2,1)} %get-tuple-element.11), calls=%async_computation | async-start | bytes 1310720 | tf_op jit(solution)/shard_map/all_to_all | solution.py:257
  27.2 34.1 %copy-start.1 = (bf16[3,2048,128]{2,1,0:T(8,128)(2,1)S(1)}, bf16[3,2048,128]{2,1,0:T(8,128)(2,1)}, u32[]{:S(2)}) copy-start(bf16[3,2048,128]{2,1,0:T(8,128)(2,1)} %w0_ref.1) | copy-start | bytes 4718596
  27.2 4.7 %collective-permute-start = (bf16[4096,128]{1,0:T(8,128)(2,1)S(1)}, bf16[4096,128]{1,0:T(8,128)(2,1)S(1)}, u32[]{:S(2)}, u32[]{:S(2)}) collective-permute-start(bf16[4096,128]{1,0:T(8,128)(2,1)S(1)} %copy-done.2), channel_id=1, source_target_pairs={{0,1},{1,0},{2,3},{3,2},{4,5},{5,4},{6,7},{7,6},{8,9},{9,8},{10,11... | collective-permute-start | bytes 3145736 | tf_op jit(solution)/shard_map/ppermute | solution.py:236
  29.3 4.9 %collective-permute-start.1 = (bf16[128,4096]{1,0:T(8,128)(2,1)}, bf16[128,4096]{1,0:T(8,128)(2,1)S(1)}, u32[]{:S(2)}, u32[]{:S(2)}) collective-permute-start(bf16[128,4096]{1,0:T(8,128)(2,1)} %down0_ref.1), channel_id=1, source_target_pairs={{0,1},{1,0},{2,3},{3,2},{4,5},{5,4},{6,7},{7,6},{8,9},{9,8},{10,11... | collective-permute-start | bytes 3145736 | tf_op jit(solution)/shard_map/ppermute | solution.py:236
  31.9 1.0 copy-start.4
  34.2 1.0 copy-start.6
  50.2 1.2 copy-start.3
  51.5 1.2 copy-start.5
  52.7 1.2 copy-start.7
  55.3 0.8 copy-start.10
  56.2 52.4 %copy-start.13 = (bf16[2048]{0:T(1024)(128)(2,1)S(1)}, bf16[2048]{0:T(1024)(128)(2,1)}, u32[]{:S(2)}) copy-start(bf16[2048]{0:T(1024)(128)(2,1)} %param.26) | copy-start | bytes 12292
  56.2 52.4 %copy-start.12 = (bf16[2048,12]{0,1:T(8,128)(2,1)S(1)}, bf16[2048,12]{0,1:T(8,128)(2,1)}, u32[]{:S(2)}) copy-start(bf16[2048,12]{0,1:T(8,128)(2,1)} %param.27) | copy-start | bytes 147460
  56.2 22.0 %all-to-all-start.1 = ((bf16[32,64,128]{2,1,0:T(8,128)(2,1)}), bf16[32,64,128]{2,1,0:T(8,128)(2,1)S(1)}, u32[]{:S(2)}, u32[]{:S(2)}) async-start(bf16[32,64,128]{2,1,0:T(8,128)(2,1)} %copy-done.10), calls=%async_computation.1 | async-start | bytes 1048576 | tf_op jit(solution)/shard_map/all_to_all | solution.py:271
  61.3 56.8 %copy-start.8 = (bf16[2048,128]{1,0:T(8,128)(2,1)S(1)}, bf16[2048,128]{1,0:T(8,128)(2,1)}, u32[]{:S(2)}) copy-start(bf16[2048,128]{1,0:T(8,128)(2,1)} %cross_u_ref.1) | copy-start | bytes 1572868
  61.3 47.3 %collective-permute-start.3 = (bf16[3,2048,128]{2,1,0:T(8,128)(2,1)S(1)}, bf16[3,2048,128]{2,1,0:T(8,128)(2,1)}, u32[]{:S(2)}, u32[]{:S(2)}) collective-permute-start(bf16[3,2048,128]{2,1,0:T(8,128)(2,1)S(1)} %copy-done.1), channel_id=1, source_target_pairs={{0,1},{1,0},{2,3},{3,2},{4,5},{5,4},{6,7},{7,6},{8,9},{9,8},{10,11... | collective-permute-start | bytes 4718600 | tf_op jit(solution)/shard_map/ppermute | solution.py:236
  63.4 4.0 %collective-permute-start.2 = (bf16[64,2048]{1,0:T(8,128)(2,1)}, bf16[64,2048]{1,0:T(8,128)(2,1)S(1)}, u32[]{:S(2)}, u32[]{:S(2)}) collective-permute-start(bf16[64,2048]{1,0:T(8,128)(2,1)} %proj0_ref.1), channel_id=1, source_target_pairs={{0,1},{1,0},{2,3},{3,2},{4,5},{5,4},{6,7},{7,6},{8,9},{9,8},{10,11... | collective-permute-start | bytes 786440 | tf_op jit(solution)/shard_map/ppermute | solution.py:236
  78.2 1.0 copy-start.11
  103.9 14.2 %all-to-all-start.3 = ((f32[64,1,128]{2,1,0:T(1,128)}), f32[64,1,128]{2,1,0:T(1,128)S(1)}, u32[]{:S(2)}, u32[]{:S(2)}) async-start(f32[64,1,128]{2,1,0:T(1,128)} %bitcast.3), calls=%async_computation.3 | async-start | bytes 65536 | tf_op jit(solution)/shard_map/all_to_all | solution.py:287
  118.1 2.2 %copy-start = (bf16[1024,2048]{1,0:T(8,128)(2,1)S(1)}, bf16[1024,2048]{1,0:T(8,128)(2,1)}, u32[]{:S(2)}) copy-start(bf16[1024,2048]{1,0:T(8,128)(2,1)} %all-gather.3.cloned.1.call-done.cand_ref) | copy-start | bytes 12582916
  120.3 1.0 copy-start.9
Sparse Core Ops, SparseCore 0:
  10.5 101.5 all-gather.2

commit v2 on v1

v2 whole, which is shorter than its diff:
```python
import math

import jax
import jax.numpy as jnp
from jax import lax
from jax.experimental import pallas as pl
from jax.experimental.pallas import tpu as pltpu
from jax.sharding import Mesh, PartitionSpec as P

D = 4096
EXPERTS = 3
TASKS = 4
REQ_GRP = 4
HIST = 32
epsilon = 1e-05

CHIPS = ("z", "xh", "xl")
ALL = ("z", "xh", "xl", "c")
N_CHIPS = 32
F32 = jnp.float32
BF16 = jnp.bfloat16
HIGH = lax.Precision.HIGHEST

VMEM = pl.BlockSpec(memory_space=pltpu.VMEM)
ANY = pl.BlockSpec(memory_space=pl.ANY)
HBM = pl.BlockSpec(memory_space=pltpu.HBM)
ROW_BY_ROW = (((1,), (1,)), ((), ()))


def params(room_kib):
    return pltpu.CompilerParams(vmem_limit_bytes=(64 << 20) - (room_kib << 10))


def block_of(chip):
    return (chip & ~3) | ((chip & 1) << 1) | ((chip >> 1) & 1)


def split2(x):
    high = x.astype(BF16).astype(F32)
    return high, x - high


def lanes(shape):
    return lax.broadcasted_iota(jnp.int32, shape, len(shape) - 1)


def rows(shape):
    return lax.broadcasted_iota(jnp.int32, shape, len(shape) - 2)


def token_sums(x):
    padded = jnp.concatenate([x, jnp.zeros((128 - x.shape[0], 128), F32)], axis=0)
    return lax.dot_general(jnp.ones((8, 128), F32), padded, ROW_BY_ROW, precision=HIGH, preferred_element_type=F32)


def turn(x, by):
    return pltpu.roll(jnp.broadcast_to(x, (8, 128)), by, 1)[0:1]


def widen(x):
    return jnp.concatenate([x, jnp.zeros((1, 128 - x.shape[1]), x.dtype)], axis=1)


def pack_kernel(hist_ref, gain_ref, query_ref, head_ref, out_ref):
    hist = hist_ref[...].astype(F32)
    out_ref[0:128, :] = jnp.concatenate([hist, jnp.zeros((64, 128), F32)], axis=0).T.astype(BF16)
    row = rows((16, 128))
    ends = jnp.concatenate([gain_ref[...].astype(F32), query_ref[...].astype(F32)], axis=1)
    out_ref[128:144, :] = jnp.where(row == 0, ends, 0.0).astype(BF16)
    heads = jnp.zeros((16, 128), F32)
    for k in range(EXPERTS):
        head = head_ref[k].astype(F32)
        for t in range(TASKS):
            heads = jnp.where(row == t * EXPERTS + k, head[t : t + 1], heads)
    out_ref[144:160, :] = heads.astype(BF16)


def spread_kernel(pair_ref, owner_ref, task_ref, out_ref, hist_ref, query_ref):
    core = lax.axis_index("c")
    tokens = pl.ds(pl.multiple_of(core * 64, 64), 64)
    first = pair_ref[0, tokens, :].astype(F32)
    second = pair_ref[1, tokens, :].astype(F32)
    hist = jnp.where(lanes((64, 128)) < 64, first, pltpu.roll(second, 64, 1))
    head0 = pair_ref[0, 128:144, :].astype(F32)[0:1]
    head1 = pair_ref[1, 128:144, :].astype(F32)[0:1]
    low = lanes((1, 128)) < 64
    gain = jnp.where(low, head0, turn(head1, 64))
    query = jnp.where(low, turn(head0, 64), head1)
    scaled = (hist * gain).astype(BF16)
    high, rest = split2(token_sums(hist * hist))
    owner = widen(owner_ref[...].astype(F32))
    task = widen(task_ref[...].astype(F32))
    owner = owner + turn(owner, 32)
    owner = owner + turn(owner, 64)
    task = task + turn(task, 32)
    task = task + turn(task, 64)
    row = rows((8, 128))
    extra = jnp.where(row == 0, high, jnp.where(row == 1, rest, jnp.where(row == 2, owner, jnp.where(row == 3, task, 0.0))))
    extra = extra.astype(BF16)
    for chip in range(N_CHIPS):
        out_ref[chip, 0:64, :] = scaled
        out_ref[chip, 64:72, :] = extra
    hist_ref[...] = hist.astype(BF16)
    query_ref[...] = jnp.broadcast_to(query, (8, 128))


def piece_chip(piece, z):
    x = lax.axis_index("xh") * 2 + lax.axis_index("xl")
    return z * 4 + ((x + (0, 3, 1, 2)[piece]) & 3)


def tower_kernel(got_ref, up0_ref, up1_ref, down0_ref, down1_ref, out_ref, owner_ref, task_ref, up, down, sems):
    copies = []
    for i, source in enumerate((up0_ref, up1_ref)):
        copies.append(pltpu.make_async_copy(source, up.at[i], sems.at[i]))
    for i, source in enumerate((down0_ref, down1_ref)):
        copies.append(pltpu.make_async_copy(source, down.at[i], sems.at[2 + i]))
    for copy in copies:
        copy.start()
    stats = jnp.zeros((8, 128), F32)
    for chip in range(N_CHIPS):
        stats = stats + got_ref[chip, 64:72, :].astype(F32)
    quarter = lanes((1, 128)) // 32
    owners, tasks = [], []
    for b in range(8):
        owner = jnp.zeros((1, 128), F32)
        task = jnp.zeros((1, 128), F32)
        for q in range(4):
            extra = got_ref[piece_chip(b // 2, 4 * (b % 2) + q), 64:72, :].astype(F32)
            owner = jnp.where(quarter == q, extra[2:3], owner)
            task = jnp.where(quarter == q, extra[3:4], task)
        owners.append(owner)
        tasks.append(task)
    owner_ref[...] = jnp.concatenate(owners, axis=0)
    task_ref[...] = jnp.concatenate(tasks, axis=0)
    inverse = lax.rsqrt((stats[0:1] + stats[1:2]) / D + epsilon)
    column = jnp.broadcast_to(inverse, (128, 128)).T[0:64]
    copies[0].wait()
    copies[1].wait()
    total = jnp.zeros((64, 256), F32)
    for b in range(0, N_CHIPS, 2):
        left = jnp.concatenate([got_ref[block_of(b), 0:64, :], got_ref[block_of(b + 1), 0:64, :]], axis=1)
        right = jnp.concatenate([up[0, b * 128 : b * 128 + 256, :], up[1, b * 128 : b * 128 + 256, :]], axis=1)
        total = total + jnp.dot(left, right, preferred_element_type=F32)
    hidden = jax.nn.gelu(total * jnp.concatenate([column, column], axis=1)).astype(BF16)
    copies[2].wait()
    copies[3].wait()
    for b in range(0, N_CHIPS, 2):
        right = jnp.concatenate([down[0, :, b * 128 : b * 128 + 256], down[1, :, b * 128 : b * 128 + 256]], axis=0)
        part = jnp.dot(hidden, right, preferred_element_type=F32).astype(BF16)
        out_ref[block_of(b), :, :] = part[:, 0:128]
        out_ref[block_of(b + 1), :, :] = part[:, 128:256]


def values_kernel(got_ref, hist_ref, query_ref, proj0_ref, proj1_ref, out_ref, proj, sems):
    copies = []
    for i, source in enumerate((proj0_ref, proj1_ref)):
        copies.append(pltpu.make_async_copy(source, proj.at[64 * i : 64 * i + 64, :], sems.at[i]))
    for copy in copies:
        copy.start()
    core = lax.axis_index("c")
    summed = got_ref[0].astype(F32)
    for chip in range(1, N_CHIPS):
        summed = summed + got_ref[chip].astype(F32)
    tower = (hist_ref[...].astype(F32) + summed).astype(BF16).astype(F32)
    square_high, square_rest = split2(token_sums(tower * tower))
    dot_high, dot_rest = split2(token_sums(tower * query_ref[0:1, :]))
    row = rows((8, 128))
    extra = jnp.where(row == 2, dot_high, jnp.where(row == 3, dot_rest, 0.0))
    extra = jnp.where(row == 0, square_high, jnp.where(row == 1, square_rest, extra)).astype(BF16)
    mine = jnp.where(core == 0, tower, pltpu.roll(tower, 64, 1)).astype(BF16)
    low = lanes((32, 128)) < 64
    for copy in copies:
        copy.wait()
    for j in range(16):
        part = jnp.dot(mine, proj[:, 128 * j : 128 * j + 128], preferred_element_type=F32)
        turned = pltpu.roll(part, 64, 1)
        out_ref[2 * j, 0:32, :] = jnp.where(low, part[0:32], turned[32:64]).astype(BF16)
        out_ref[2 * j + 1, 0:32, :] = jnp.where(low, turned[0:32], part[32:64]).astype(BF16)
        out_ref[2 * j, 32:40, :] = extra
        out_ref[2 * j + 1, 32:40, :] = extra


def user_kernel(got_ref, out_ref):
    values = got_ref[0, 0:32, :].astype(F32)
    stats = got_ref[0, 32:40, :].astype(F32)
    for chip in range(1, N_CHIPS):
        values = values + got_ref[chip, 0:32, :].astype(F32)
        stats = stats + got_ref[chip, 32:40, :].astype(F32)
    squares = stats[0:1] + stats[1:2]
    dotted = stats[2:3] + stats[3:4]
    weight = jax.nn.sigmoid(dotted * lax.rsqrt(squares / D + epsilon))
    column = jnp.broadcast_to(weight, (128, 128)).T
    weights = jnp.where(lanes((32, 128)) < 64, column[0:32], column[32:64])
    user = jnp.sum(weights * values, axis=0, keepdims=True) / math.sqrt(HIST)
    out_ref[...] = jnp.broadcast_to(user, (64, 128))


PIECE = 256


def score_kernel(
    user_ref, c0_ref, c1_ref, c2_ref, c3_ref, c4_ref, owner_ref, task_ref, own_task_ref, pair_ref, cross_u_ref,
    cross_v_ref, bias_ref, gate_ref, w0_ref, w1_ref,
    out_ref, gates_ref, users, x, cross_u, cross_v, w, sems,
):
    core = lax.axis_index("c")
    arrivals = []
    for i, (source, start, size) in enumerate(
        ((c0_ref, 0, 256), (c1_ref, 256, 256), (c2_ref, 512, 256), (c3_ref, 768, 128), (c4_ref, 896, 128))
    ):
        arrivals.append(pltpu.make_async_copy(source, x.at[start : start + size, :], sems.at[i]))
    get_u = pltpu.make_async_copy(cross_u_ref, cross_u, sems.at[5])
    get_v = pltpu.make_async_copy(cross_v_ref, cross_v.at[0:128, :], sems.at[6])
    get_w = [
        pltpu.make_async_copy(w0_ref, w.at[0], sems.at[7]),
        pltpu.make_async_copy(w1_ref, w.at[1], sems.at[8]),
    ]
    for copy in (arrivals[0], get_u, get_v, arrivals[1], *get_w, *arrivals[2:]):
        copy.start()
    got = user_ref[...]
    turned = pltpu.roll(got, 64, 1)
    row = rows((16, 128))
    low_half = lanes((1, 128)) < 64
    for j in range(16):
        full = jnp.zeros((16, 128), F32)
        for r in range(REQ_GRP):
            a = 4 * j + r // 2
            if r % 2 == 0:
                pick = jnp.where(low_half, got[a : a + 1], turned[a + 2 : a + 3])
            else:
                pick = jnp.where(low_half, turned[a : a + 1], got[a + 2 : a + 3])
            full = jnp.where(row % 4 == r, pick, full)
        high, rest = split2(full)
        mid, last = split2(rest)
        users[:, 128 * j : 128 * j + 128] = jnp.where(
            row < 4, high, jnp.where(row < 8, mid, jnp.where(row < 12, last, 0.0))
        ).astype(BF16)
    heads = jnp.concatenate([pair_ref[core, 144:160, :], pair_ref[1 - core, 144:160, :]], axis=1)
    row = rows((16, 2048))
    bias = bias_ref[...].astype(F32)
    cross_v[128:144, :] = jnp.where(row == 0, bias, jnp.where(row == 1, 1.0, 0.0)).astype(BF16)
    cross_v[144:256, :] = jnp.zeros((112, 2048), BF16)
    ones = jnp.where(lanes((PIECE, 128)) < 2, 1.0, 0.0).astype(BF16)
    row = rows((16, PIECE))
    task_row = lambda p, ref: jnp.concatenate([ref[2 * p : 2 * p + 1, :], ref[2 * p + 1 : 2 * p + 2, :]], axis=1)

    def cross_rows(p):
        part = slice(PIECE * p, PIECE * p + PIECE)
        hot = jnp.where((row % 4).astype(F32) == task_row(p, owner_ref), 1.0, 0.0).T.astype(BF16)
        low = jnp.zeros((PIECE, 128), F32)
        for j in range(8):
            cols = slice(256 * j, 256 * j + 256)
            added = jnp.dot(hot, users[:, cols], preferred_element_type=F32)
            x0 = (x[part, cols].astype(F32) + added).astype(BF16)
            x[part, cols] = x0
            low = low + jnp.dot(x0, cross_u[cols, :], preferred_element_type=F32)
        left = jnp.concatenate([low.astype(BF16), ones], axis=1)
        if p == 0:
            get_v.wait()
        for j in range(8):
            cols = slice(256 * j, 256 * j + 256)
            cross = jnp.dot(left, cross_v[:, cols], preferred_element_type=F32)
            x[part, cols] = (x[part, cols].astype(F32) * cross).astype(BF16)

    quarter = lanes((1, 128)) // 32

    def expert_rows(p):
        part = slice(PIECE * p, PIECE * p + PIECE)
        task = task_row(p, task_ref)
        outs = []
        for k in range(EXPERTS):
            right = jnp.concatenate([w[0, k], w[1, k]], axis=1)
            active = jax.nn.relu(jnp.dot(x[part, :], right, preferred_element_type=F32)).astype(BF16)
            terms = lax.dot_general(heads, active, ROW_BY_ROW, preferred_element_type=F32)
            outs.append(jnp.sum(jnp.where(row.astype(F32) == task * EXPERTS + k, terms, 0.0), axis=0, keepdims=True))
        for half in range(2):
            stack = jnp.concatenate([o[:, 128 * half : 128 * half + 128] for o in outs] + [jnp.zeros((5, 128), F32)], axis=0)
            turns = [stack] + [pltpu.roll(stack, 32 * q, 1) for q in range(1, 4)]
            for q in range(4):
                message = jnp.zeros((1, 128), F32)
                for k in range(EXPERTS):
                    message = jnp.where(quarter == k, turns[(k - q) % 4][k : k + 1], message)
                out_ref[pl.ds(piece_chip(p, 4 * half + q), 1), :] = message

    arrivals[0].wait()
    get_u.wait()
    cross_rows(0)
    arrivals[1].wait()
    for copy in get_w:
        copy.wait()
    own = x[pl.ds(pl.multiple_of(lax.axis_index("z") * 32, 32), 32), :]
    logits = lax.dot_general(gate_ref[...], own, ROW_BY_ROW, preferred_element_type=F32)
    own_row = rows((16, 32))
    picked = jnp.where(own_row // EXPERTS == own_task_ref[...], jax.nn.sigmoid(logits), 0.0)
    gates = picked / jnp.sum(picked, axis=0, keepdims=True)
    row_of = jnp.zeros((1, 128), F32)
    for k in range(EXPERTS):
        gate = jnp.sum(jnp.where(own_row % EXPERTS == k, gates, 0.0), axis=0, keepdims=True)
        gate = widen(gate)
        row_of = row_of + (gate if k == 0 else turn(gate, 32 * k))
    gates_ref[...] = row_of
    cross_rows(1)
    expert_rows(0)
    for copy in arrivals[2:]:
        copy.wait()
    cross_rows(2)
    expert_rows(1)
    cross_rows(3)
    expert_rows(2)
    expert_rows(3)


def home_kernel(got_ref, gates_ref, owner_ref, out_ref):
    total = jnp.sum(got_ref[...], axis=0, keepdims=True) * gates_ref[...]
    total = total + turn(total, 64)
    total = total + turn(total, 32)
    out_ref[...] = jnp.where(owner_ref[...] < REQ_GRP, total[:, 0:32], 0.0)


def hold_kernel(x_ref, after_ref, out_ref):
    del x_ref, after_ref, out_ref


def hold(x, after):
    return pl.pallas_call(
        hold_kernel,
        out_shape=jax.ShapeDtypeStruct(x.shape, x.dtype),
        in_specs=[HBM, ANY],
        out_specs=HBM,
        input_output_aliases={0: 0},
        compiler_params=params(256),
    )(x, after)


def body(
    hist, tower_gain, up_w, down_w, query, proj_w, cand, owner, task, cross_u, cross_v, cross_bias, gate_w, expert_w, head_w,
):
    owner, task = owner[None, :], task[None, :]
    column = lax.all_gather(cand, "z", axis=0, tiled=True)
    message = pl.pallas_call(
        pack_kernel,
        out_shape=jax.ShapeDtypeStruct((160, 128), BF16),
        in_specs=[VMEM] * 4,
        out_specs=VMEM,
        compiler_params=params(64),
    )(hist.T, tower_gain, query[None, :], head_w.transpose(1, 0, 2))
    pair = lax.all_gather(message, "c", axis=0)
    spread, hist_c, query_c = pl.pallas_call(
        spread_kernel,
        out_shape=(
            jax.ShapeDtypeStruct((N_CHIPS, 72, 128), BF16),
            jax.ShapeDtypeStruct((64, 128), BF16),
            jax.ShapeDtypeStruct((8, 128), F32),
        ),
        in_specs=[VMEM] * 3,
        out_specs=(VMEM,) * 3,
        compiler_params=params(1024),
    )(pair, owner, task)
    tokens = lax.all_to_all(spread, CHIPS, 0, 0, tiled=True)
    swap = lambda x: lax.ppermute(x, "c", [(0, 1), (1, 0)])
    parts, owners, tasks = pl.pallas_call(
        tower_kernel,
        out_shape=(
            jax.ShapeDtypeStruct((N_CHIPS, 64, 128), BF16),
            jax.ShapeDtypeStruct((8, 128), F32),
            jax.ShapeDtypeStruct((8, 128), F32),
        ),
        in_specs=[VMEM] + [HBM] * 4,
        out_specs=(VMEM,) * 3,
        scratch_shapes=[
            pltpu.VMEM((2, 4096, 128), BF16),
            pltpu.VMEM((2, 128, 4096), BF16),
            pltpu.SemaphoreType.DMA((4,)),
        ],
        compiler_params=params(11264),
    )(tokens, up_w, swap(up_w), down_w, swap(down_w))
    summed = lax.all_to_all(parts, CHIPS, 0, 0, tiled=True)
    at = lambda x: (x % 2) * 2 + (x % 4) // 2
    shift = lambda x, by: lax.ppermute(x, ("xl", "xh"), [(at(i), at(i + by)) for i in range(4)])
    held = hold(column, owners)
    left, right = shift(held, 1), shift(held, 3)
    far0, far1 = shift(left[0:128], 1), shift(right[128:256], 3)
    values = pl.pallas_call(
        values_kernel,
        out_shape=jax.ShapeDtypeStruct((N_CHIPS, 40, 128), BF16),
        in_specs=[VMEM] * 3 + [HBM] * 2,
        out_specs=VMEM,
        scratch_shapes=[pltpu.VMEM((128, 2048), BF16), pltpu.SemaphoreType.DMA((2,))],
        compiler_params=params(1024),
    )(summed, hist_c, query_c, proj_w, swap(proj_w))
    values = lax.all_to_all(values, CHIPS, 0, 0, tiled=True)
    user = pl.pallas_call(
        user_kernel,
        out_shape=jax.ShapeDtypeStruct((64, 128), F32),
        in_specs=[VMEM],
        out_specs=VMEM,
        compiler_params=params(12288),
    )(values)
    users = lax.all_to_all(user, ALL, 0, 0, tiled=True)
    gate_rows = jnp.pad(gate_w.T, ((0, 4), (0, 0)))
    part, gates = pl.pallas_call(
        score_kernel,
        out_shape=(jax.ShapeDtypeStruct((N_CHIPS, 128), F32), jax.ShapeDtypeStruct((1, 128), F32)),
        in_specs=[VMEM] + [HBM] * 5 + [VMEM] * 4 + [HBM] * 2 + [VMEM] * 2 + [HBM] * 2,
        out_specs=(VMEM,) * 2,
        scratch_shapes=[
            pltpu.VMEM((16, 2048), BF16),
            pltpu.VMEM((4 * PIECE, 2048), BF16),
            pltpu.VMEM((2048, 128), BF16),
            pltpu.VMEM((256, 2048), BF16),
            pltpu.VMEM((2, EXPERTS, 2048, 128), BF16),
            pltpu.SemaphoreType.DMA((9,)),
        ],
        compiler_params=params(384),
    )(
        users, held, left, right, far0, far1, owners, tasks, task, pair, cross_u, cross_v, cross_bias[None, :],
        gate_rows, expert_w, swap(expert_w),
    )
    back = lax.all_to_all(part, CHIPS, 0, 0, tiled=True)
    score = pl.pallas_call(
        home_kernel,
        out_shape=jax.ShapeDtypeStruct((1, 32), F32),
        in_specs=[VMEM] * 3,
        out_specs=VMEM,
        compiler_params=params(256),
    )(back, gates, owner)
    return score[0]


def solution(mesh):
    fine = Mesh(mesh.devices.reshape(mesh.devices.shape[0], 8, 2, 2, 2), ("grp", "z", "xl", "xh", "c"))
    t = ("z", "xl", "xh", "c")
    in_specs = (
        P("grp", t),
        P(None, t),
        P(None, t),
        P(t, None),
        P(t),
        P(t, None),
        P(("grp",) + t, None),
        P(("grp",) + t),
        P(("grp",) + t),
        P(),
        P(),
        P(),
        P(),
        P(None, None, t),
        P(None, None, t),
    )
    return jax.shard_map(body, mesh=fine, in_specs=in_specs, out_specs=P(("grp",) + t), check_vma=False)
```

time: 158 us -> 168 us (1.063)
  starting transfers between devices: 31.8 us -> 55.8 us
  blocking collectives: 38.1 us -> 17.2 us
  Pallas kernels: 18.8 us -> 30.7 us
  local copies, waits for them, and re-layouts: 14.2 us -> 6 us
  waiting for transfers between devices: 39.2 us -> 43.6 us
    all_to_all x1 -> x0, blocking collectives: 23.5 us -> none  [body(): values = lax.all_to_all(values, CHIPS, 0, 0, tiled=True)]
    ppermute x0 -> x4, starting transfers between devices: none -> 14.4 us  [body(): lax.ppermute(x, ('xl', 'xh'), [(at(i), at(i + by)) for i in range(4)])]
    unnamed x30 -> x18, local copies, waits for them, and re-layouts: 12.2 us -> 2.62 us
    pallas_call x4 -> x6, Pallas kernels: 16.6 us -> 25 us  [the longest x1 17 us: body(): pl.pallas_call(score_kernel, out_shape=(jax.ShapeDtypeStruct((N_CHIPS, 12...]
    ppermute x0 -> x4, waiting for transfers between devices: none -> 7.35 us  [body(): lax.ppermute(x, ('xl', 'xh'), [(at(i), at(i + by)) for i in range(4)])]
    all_to_all x1, waiting for transfers between devices: 10.8 us -> 5.49 us  [body(): summed = lax.all_to_all(parts, CHIPS, 0, 0, tiled=True)]
    all_to_all x1, starting transfers between devices: 4.61 us -> 9.87 us  [body(): users = lax.all_to_all(user, ALL, 0, 0, tiled=True)]
    all_to_all x0 -> x1, starting transfers between devices: none -> 5.01 us  [body(): values = lax.all_to_all(values, CHIPS, 0, 0, tiled=True)]
  transfers between devices with their start and end apart: 8 -> 13, of which waited for: 6 -> 7; matrix products, arithmetic and copies ran while one was open for 2% -> 2% of each run, Pallas kernels for 2% -> 7%
where the time goes in v2:
time: 168 us; the launch traced here: 167 us
  starting transfers between devices  55.8 us (33%)
  waiting for transfers between devices  43.6 us (26%)
  Pallas kernels  30.7 us (18%)
  blocking collectives  17.2 us (10%)
  between operations  13.6 us (8%)
  local copies, waits for them, and re-layouts  6 us (4%)
    all_to_all x1, waiting for transfers between devices, body(): tokens = lax.all_to_all(spread, CHIPS, 0, 0, tiled=True)  18 us
    pallas_call x1, Pallas kernels, body(): pl.pallas_call(score_kernel, out_shape=(jax.ShapeDtypeStruct((N_CHIPS, 12...  17 us
    ppermute x4, starting transfers between devices, body(): lax.ppermute(x, ('xl', 'xh'), [(at(i), at(i + by)) for i in range(4)])  14.4 us
    all_to_all x1, blocking collectives, body(): back = lax.all_to_all(part, CHIPS, 0, 0, tiled=True)  14 us
    all_to_all x1, starting transfers between devices, body(): tokens = lax.all_to_all(spread, CHIPS, 0, 0, tiled=True)  13.2 us
    all_to_all x1, starting transfers between devices, body(): users = lax.all_to_all(user, ALL, 0, 0, tiled=True)  9.87 us
    ppermute x4, starting transfers between devices, body(): swap = lambda x: lax.ppermute(x, 'c', [(0, 1), (1, 0)])  8.66 us
    all_to_all x1, waiting for transfers between devices, body(): users = lax.all_to_all(user, ALL, 0, 0, tiled=True)  8.17 us
  transfers between devices with their start and end apart: 13, of which 7 were waited for; matrix products, arithmetic and copies ran while one was open for 2% of the time, Pallas kernels for 7%

profile of v2, /device:TPU:56, one launch (start us, length us, event | category | flops | bytes accessed | tf_op | source)
XLA Modules:
  0.0 166.9 jit_solution(4932346012007476001)
XLA Ops:
  6.5 0.0 all-gather.3.cloned.1.call-start
  6.5 0.7 all-gather.3.cloned.1.call-update
  7.3 1.5 shard_map.145
  8.7 3.2 %all-gather = bf16[320,128]{1,0:T(8,128)(2,1)} all-gather(bf16[160,128]{1,0:T(8,128)(2,1)} %shard_map.145), channel_id=2, replica_groups=mesh['grp'=8,'z'=8,'xl'=2,'xh'=2,'c'=2] {'c'}, dimensions={0}, use_global_device_ids=true | all-gather | bytes 122880 | tf_op jit(solution)/shard_map/all_gather | solution.py:348
  12.0 2.0 %shard_map.146 = (bf16[32,72,128]{2,1,0:T(8,128)(2,1)}, bf16[64,128]{1,0:T(8,128)(2,1)}, f32[8,128]{1,0:T(8,128)}) custom-call(bf16[2,160,128]{2,1,0:T(8,128)(2,1)} %bitcast.16, s32[1,32]{1,0:T(1,128)} %bitcast.26, s32[1,32]{1,0:T(1,128)} %bitcast.24), custom_call_target="tpu_custom_call" | custom-call | tf_op jit(solution)/shard_map/pallas_call | solution.py:349
  13.9 13.2 %all-to-all-start = ((bf16[32,72,128]{2,1,0:T(8,128)(2,1)}), bf16[32,72,128]{2,1,0:T(8,128)(2,1)S(1)}, u32[]{:S(2)}, u32[]{:S(2)}) async-start(bf16[32,72,128]{2,1,0:T(8,128)(2,1)} %get-tuple-element.13), calls=%async_computation | async-start | bytes 1179648 | tf_op jit(solution)/shard_map/all_to_all | solution.py:360
  27.1 2.0 %collective-permute-start = (bf16[4096,128]{1,0:T(8,128)(2,1)}, bf16[4096,128]{1,0:T(8,128)(2,1)S(1)}, u32[]{:S(2)}, u32[]{:S(2)}) collective-permute-start(bf16[4096,128]{1,0:T(8,128)(2,1)} %up0_ref.1), channel_id=1, source_target_pairs={{0,1},{1,0},{2,3},{3,2},{4,5},{5,4},{6,7},{7,6},{8,9},{9,8},{10,11... | collective-permute-start | bytes 3145736 | tf_op jit(solution)/shard_map/ppermute | solution.py:361
  29.1 2.4 %collective-permute-start.1 = (bf16[128,4096]{1,0:T(8,128)(2,1)}, bf16[128,4096]{1,0:T(8,128)(2,1)S(1)}, u32[]{:S(2)}, u32[]{:S(2)}) collective-permute-start(bf16[128,4096]{1,0:T(8,128)(2,1)} %down0_ref.1), channel_id=1, source_target_pairs={{0,1},{1,0},{2,3},{3,2},{4,5},{5,4},{6,7},{7,6},{8,9},{9,8},{10,11... | collective-permute-start | bytes 3145736 | tf_op jit(solution)/shard_map/ppermute | solution.py:361
  31.5 0.4 collective-permute-done.up1_ref
  31.9 2.1 %collective-permute-done.1.down1_ref = bf16[128,4096]{1,0:T(8,128)(2,1)S(1)} collective-permute-done((bf16[128,4096]{1,0:T(8,128)(2,1)}, bf16[128,4096]{1,0:T(8,128)(2,1)S(1)}, u32[]{:S(2)}, u32[]{:S(2)}) %collective-permute-start.1) | collective-permute-done | bytes 1048608 | tf_op jit(solution)/shard_map/ppermute | solution.py:361
  33.9 18.0 %all-to-all-done.got_ref = bf16[32,72,128]{2,1,0:T(8,128)(2,1)S(1)} async-done(((bf16[32,72,128]{2,1,0:T(8,128)(2,1)}), bf16[32,72,128]{2,1,0:T(8,128)(2,1)S(1)}, u32[]{:S(2)}, u32[]{:S(2)}) %all-to-all-start) | async-done | bytes 589856 | tf_op jit(solution)/shard_map/all_to_all | solution.py:360
  52.0 0.0 copy-done.3
  52.0 0.8 copy-done.2
  52.8 5.0 %shard_map.147 = (bf16[32,64,128]{2,1,0:T(8,128)(2,1)}, f32[8,128]{1,0:T(8,128)S(1)}, f32[8,128]{1,0:T(8,128)S(1)}) custom-call(bf16[32,72,128]{2,1,0:T(8,128)(2,1)} %copy-done.2, bf16[4096,128]{1,0:T(8,128)(2,1)} %up0_ref.1, bf16[4096,128]{1,0:T(8,128)(2,1)} %copy-done.3, bf16[128,4096]{1,0:T(8,128)(2,1)} %down0_ref.1, bf16[128,4096]{1,0:T(8,128)(2,1)} %copy-done.4), custom_call_target="tpu_custom_call" | custom-call | tf_op jit(solution)/shard_map/pallas_call | solution.py:362
  57.8 0.6 copy-done
  58.4 0.6 copy-done.1
  59.0 4.6 %all-to-all-start.1 = ((bf16[32,64,128]{2,1,0:T(8,128)(2,1)}), bf16[32,64,128]{2,1,0:T(8,128)(2,1)}, u32[]{:S(2)}, u32[]{:S(2)}) async-start(bf16[32,64,128]{2,1,0:T(8,128)(2,1)} %get-tuple-element.14), calls=%async_computation.1 | async-start | bytes 1048576 | tf_op jit(solution)/shard_map/all_to_all | solution.py:378
  63.6 0.0 all-gather.3.cloned.1.call-done.x_ref
  63.6 4.8 %collective-permute-start.4 = (bf16[256,2048]{1,0:T(8,128)(2,1)}, bf16[256,2048]{1,0:T(8,128)(2,1)}, u32[]{:S(2)}, u32[]{:S(2)}) collective-permute-start(bf16[256,2048]{1,0:T(8,128)(2,1)} %shard_map.150.c0_ref), channel_id=1, source_target_pairs={{0,6},{4,0},{2,4},{6,2},{1,7},{5,1},{3,5},{7,3},{8,14},{12,8},{10,... | collective-permute-start | bytes 3145736 | tf_op jit(solution)/shard_map/ppermute | solution.py:380
  68.4 1.9 %collective-permute-start.7 = (bf16[3,2048,128]{2,1,0:T(8,128)(2,1)}, bf16[3,2048,128]{2,1,0:T(8,128)(2,1)}, u32[]{:S(2)}, u32[]{:S(2)}) collective-permute-start(bf16[3,2048,128]{2,1,0:T(8,128)(2,1)} %w0_ref.1), channel_id=1, source_target_pairs={{0,1},{1,0},{2,3},{3,2},{4,5},{5,4},{6,7},{7,6},{8,9},{9,8},{10,11... | collective-permute-start | bytes 4718600 | tf_op jit(solution)/shard_map/ppermute | solution.py:361
  70.3 1.9 %collective-permute-start.3 = (bf16[256,2048]{1,0:T(8,128)(2,1)}, bf16[256,2048]{1,0:T(8,128)(2,1)}, u32[]{:S(2)}, u32[]{:S(2)}) collective-permute-start(bf16[256,2048]{1,0:T(8,128)(2,1)} %shard_map.150.c0_ref), channel_id=1, source_target_pairs={{0,4},{4,2},{2,6},{6,0},{1,5},{5,3},{3,7},{7,1},{8,12},{12,10},{10... | collective-permute-start | bytes 3145736 | tf_op jit(solution)/shard_map/ppermute | solution.py:380
  72.3 2.4 %collective-permute-start.2 = (bf16[64,2048]{1,0:T(8,128)(2,1)}, bf16[64,2048]{1,0:T(8,128)(2,1)S(1)}, u32[]{:S(2)}, u32[]{:S(2)}) collective-permute-start(bf16[64,2048]{1,0:T(8,128)(2,1)} %proj0_ref.1), channel_id=1, source_target_pairs={{0,1},{1,0},{2,3},{3,2},{4,5},{5,4},{6,7},{7,6},{8,9},{9,8},{10,11... | collective-permute-start | bytes 786440 | tf_op jit(solution)/shard_map/ppermute | solution.py:361
  74.7 1.4 collective-permute-done.2.proj1_ref
  76.0 5.5 %all-to-all-done.1.got_ref = bf16[32,64,128]{2,1,0:T(8,128)(2,1)} async-done(((bf16[32,64,128]{2,1,0:T(8,128)(2,1)}), bf16[32,64,128]{2,1,0:T(8,128)(2,1)}, u32[]{:S(2)}, u32[]{:S(2)}) %all-to-all-start.1) | async-done | bytes 524320 | tf_op jit(solution)/shard_map/all_to_all | solution.py:378
  81.5 3.2 %shard_map.148 = bf16[32,40,128]{2,1,0:T(8,128)(2,1)} custom-call(bf16[32,64,128]{2,1,0:T(8,128)(2,1)} %all-to-all-done.1.got_ref, bf16[64,128]{1,0:T(8,128)(2,1)} %get-tuple-element.15.hist_ref, f32[8,128]{1,0:T(8,128)} %get-tuple-element.16.query_ref, bf16[64,2048]{1,0:T(8,128)(2,1)} %proj0_ref.1, bf16[64,2048]{1,0:T(8,128)(2,1)} %copy-done.5), custom_call_target="tpu_custom_call" | custom-call | tf_op jit(solution)/shard_map/pallas_call | solution.py:384
  84.7 0.0 copy-start.8
  84.7 0.0 copy-start.7
  84.8 5.0 %all-to-all-start.2 = ((bf16[32,40,128]{2,1,0:T(8,128)(2,1)}), bf16[32,40,128]{2,1,0:T(8,128)(2,1)S(1)}, u32[]{:S(2)}, u32[]{:S(2)}) async-start(bf16[32,40,128]{2,1,0:T(8,128)(2,1)} %shard_map.148), calls=%async_computation.2 | async-start | bytes 655360 | tf_op jit(solution)/shard_map/all_to_all | solution.py:392
  89.8 7.3 %collective-permute-done.4.c2_ref = bf16[256,2048]{1,0:T(8,128)(2,1)} collective-permute-done((bf16[256,2048]{1,0:T(8,128)(2,1)}, bf16[256,2048]{1,0:T(8,128)(2,1)}, u32[]{:S(2)}, u32[]{:S(2)}) %collective-permute-start.4) | collective-permute-done | bytes 1048608 | tf_op jit(solution)/shard_map/ppermute | solution.py:380
  97.1 1.1 slice.9
  98.2 5.8 %collective-permute-start.6 = (bf16[128,2048]{1,0:T(8,128)(2,1)S(1)}, bf16[128,2048]{1,0:T(8,128)(2,1)}, u32[]{:S(2)}, u32[]{:S(2)}) collective-permute-start(bf16[128,2048]{1,0:T(8,128)(2,1)S(1)} %slice.9), channel_id=1, source_target_pairs={{0,6},{4,0},{2,4},{6,2},{1,7},{5,1},{3,5},{7,3},{8,14},{12,8},{10,... | collective-permute-start | bytes 1572872 | tf_op jit(solution)/shard_map/ppermute | solution.py:380
  104.0 0.0 collective-permute-done.3.c1_ref
  104.0 1.1 slice.8
  105.1 1.9 %collective-permute-start.5 = (bf16[128,2048]{1,0:T(8,128)(2,1)S(1)}, bf16[128,2048]{1,0:T(8,128)(2,1)}, u32[]{:S(2)}, u32[]{:S(2)}) collective-permute-start(bf16[128,2048]{1,0:T(8,128)(2,1)S(1)} %slice.8), channel_id=1, source_target_pairs={{0,4},{4,2},{2,6},{6,0},{1,5},{5,3},{3,7},{7,1},{8,12},{12,10},{10... | collective-permute-start | bytes 1572872 | tf_op jit(solution)/shard_map/ppermute | solution.py:380
  107.0 0.0 all-to-all-done.2.got_ref
  107.0 0.8 shard_map.149
  107.8 9.9 %all-to-all-start.3 = ((f32[64,1,128]{2,1,0:T(1,128)}), f32[64,1,128]{2,1,0:T(1,128)S(1)}, u32[]{:S(2)}, u32[]{:S(2)}) async-start(f32[64,1,128]{2,1,0:T(1,128)} %bitcast.7), calls=%async_computation.3 | async-start | bytes 65536 | tf_op jit(solution)/shard_map/all_to_all | solution.py:400
  117.7 0.6 broadcast_in_dim.15.bias_ref
  118.3 0.0 copy-done.7
  118.3 0.6 pad.4.gate_ref
  118.9 0.0 collective-permute-done.7.w1_ref
  118.9 8.2 %all-to-all-done.3 = f32[64,1,128]{2,1,0:T(1,128)S(1)} async-done(((f32[64,1,128]{2,1,0:T(1,128)}), f32[64,1,128]{2,1,0:T(1,128)S(1)}, u32[]{:S(2)}, u32[]{:S(2)}) %all-to-all-start.3) | async-done | bytes 32800 | tf_op jit(solution)/shard_map/all_to_all | solution.py:400
  127.1 0.0 collective-permute-done.6.c4_ref
  127.1 0.0 collective-permute-done.5.c3_ref
  127.1 0.6 copy-done.6
  127.7 17.0 %shard_map.151 = (f32[32,128]{1,0:T(8,128)}, f32[1,128]{1,0:T(1,128)}) custom-call(f32[64,128]{1,0:T(8,128)} %bitcast.18, bf16[256,2048]{1,0:T(8,128)(2,1)} %shard_map.150.c0_ref, bf16[256,2048]{1,0:T(8,128)(2,1)} %collective-permute-done.3.c1_ref, bf16[256,2048]{1,0:T(8,128)(2,1)} %collective-permute-done.4.c2_ref, ...), custom_call_target="tpu_custom_call" | custom-call | tf_op jit(solution)/shard_map/pallas_call | solution.py:402
  144.7 14.0 %all_to_all.37 = f32[32,1,128]{2,1,0:T(1,128)} all-to-all(f32[32,1,128]{2,1,0:T(1,128)} %bitcast.21), channel_id=1, replica_groups=mesh['grp'=8,'z'=8,'xl'=2,'xh'=2,'c'=2] {'z','xh','xl'}, dimensions={0} | all-to-all | bytes 32768 | tf_op jit(solution)/shard_map/all_to_all | solution.py:420
  158.7 1.4 shard_map.152
  (11 shorter events, 0.0 us)
Async XLA Ops:
  6.5 57.1 %all-gather.3.cloned.1.call-start = ((), (), s32[]{:S(2)}) async-start(), calls=%async_computation.5 | async-start | bytes 1179648 | tf_op jit(solution)/shard_map/all_gather | solution.py:340
  13.9 38.0 %all-to-all-start = ((bf16[32,72,128]{2,1,0:T(8,128)(2,1)}), bf16[32,72,128]{2,1,0:T(8,128)(2,1)S(1)}, u32[]{:S(2)}, u32[]{:S(2)}) async-start(bf16[32,72,128]{2,1,0:T(8,128)(2,1)} %get-tuple-element.13), calls=%async_computation | async-start | bytes 1179648 | tf_op jit(solution)/shard_map/all_to_all | solution.py:360
  27.1 4.8 %collective-permute-start = (bf16[4096,128]{1,0:T(8,128)(2,1)}, bf16[4096,128]{1,0:T(8,128)(2,1)S(1)}, u32[]{:S(2)}, u32[]{:S(2)}) collective-permute-start(bf16[4096,128]{1,0:T(8,128)(2,1)} %up0_ref.1), channel_id=1, source_target_pairs={{0,1},{1,0},{2,3},{3,2},{4,5},{5,4},{6,7},{7,6},{8,9},{9,8},{10,11... | collective-permute-start | bytes 3145736 | tf_op jit(solution)/shard_map/ppermute | solution.py:361
  29.1 4.8 %collective-permute-start.1 = (bf16[128,4096]{1,0:T(8,128)(2,1)}, bf16[128,4096]{1,0:T(8,128)(2,1)S(1)}, u32[]{:S(2)}, u32[]{:S(2)}) collective-permute-start(bf16[128,4096]{1,0:T(8,128)(2,1)} %down0_ref.1), channel_id=1, source_target_pairs={{0,1},{1,0},{2,3},{3,2},{4,5},{5,4},{6,7},{7,6},{8,9},{9,8},{10,11... | collective-permute-start | bytes 3145736 | tf_op jit(solution)/shard_map/ppermute | solution.py:361
  31.9 20.1 %copy-start.3 = (bf16[4096,128]{1,0:T(8,128)(2,1)}, bf16[4096,128]{1,0:T(8,128)(2,1)S(1)}, u32[]{:S(2)}) copy-start(bf16[4096,128]{1,0:T(8,128)(2,1)S(1)} %collective-permute-done.up1_ref) | copy-start | bytes 3145732
  33.9 18.1 %copy-start.4 = (bf16[128,4096]{1,0:T(8,128)(2,1)}, bf16[128,4096]{1,0:T(8,128)(2,1)S(1)}, u32[]{:S(2)}) copy-start(bf16[128,4096]{1,0:T(8,128)(2,1)S(1)} %collective-permute-done.1.down1_ref) | copy-start | bytes 3145732
  52.0 0.8 copy-start.2
  57.8 0.6 copy-start
  58.4 0.6 copy-start.1
  59.0 22.6 %all-to-all-start.1 = ((bf16[32,64,128]{2,1,0:T(8,128)(2,1)}), bf16[32,64,128]{2,1,0:T(8,128)(2,1)}, u32[]{:S(2)}, u32[]{:S(2)}) async-start(bf16[32,64,128]{2,1,0:T(8,128)(2,1)} %get-tuple-element.14), calls=%async_computation.1 | async-start | bytes 1048576 | tf_op jit(solution)/shard_map/all_to_all | solution.py:378
  63.6 33.4 %collective-permute-start.4 = (bf16[256,2048]{1,0:T(8,128)(2,1)}, bf16[256,2048]{1,0:T(8,128)(2,1)}, u32[]{:S(2)}, u32[]{:S(2)}) collective-permute-start(bf16[256,2048]{1,0:T(8,128)(2,1)} %shard_map.150.c0_ref), channel_id=1, source_target_pairs={{0,6},{4,0},{2,4},{6,2},{1,7},{5,1},{3,5},{7,3},{8,14},{12,8},{10,... | collective-permute-start | bytes 3145736 | tf_op jit(solution)/shard_map/ppermute | solution.py:380
  68.4 50.5 %collective-permute-start.7 = (bf16[3,2048,128]{2,1,0:T(8,128)(2,1)}, bf16[3,2048,128]{2,1,0:T(8,128)(2,1)}, u32[]{:S(2)}, u32[]{:S(2)}) collective-permute-start(bf16[3,2048,128]{2,1,0:T(8,128)(2,1)} %w0_ref.1), channel_id=1, source_target_pairs={{0,1},{1,0},{2,3},{3,2},{4,5},{5,4},{6,7},{7,6},{8,9},{9,8},{10,11... | collective-permute-start | bytes 4718600 | tf_op jit(solution)/shard_map/ppermute | solution.py:361
  70.3 33.7 %collective-permute-start.3 = (bf16[256,2048]{1,0:T(8,128)(2,1)}, bf16[256,2048]{1,0:T(8,128)(2,1)}, u32[]{:S(2)}, u32[]{:S(2)}) collective-permute-start(bf16[256,2048]{1,0:T(8,128)(2,1)} %shard_map.150.c0_ref), channel_id=1, source_target_pairs={{0,4},{4,2},{2,6},{6,0},{1,5},{5,3},{3,7},{7,1},{8,12},{12,10},{10... | collective-permute-start | bytes 3145736 | tf_op jit(solution)/shard_map/ppermute | solution.py:380
  72.3 3.8 %collective-permute-start.2 = (bf16[64,2048]{1,0:T(8,128)(2,1)}, bf16[64,2048]{1,0:T(8,128)(2,1)S(1)}, u32[]{:S(2)}, u32[]{:S(2)}) collective-permute-start(bf16[64,2048]{1,0:T(8,128)(2,1)} %proj0_ref.1), channel_id=1, source_target_pairs={{0,1},{1,0},{2,3},{3,2},{4,5},{5,4},{6,7},{7,6},{8,9},{9,8},{10,11... | collective-permute-start | bytes 786440 | tf_op jit(solution)/shard_map/ppermute | solution.py:361
  76.0 5.5 %copy-start.5 = (bf16[64,2048]{1,0:T(8,128)(2,1)}, bf16[64,2048]{1,0:T(8,128)(2,1)S(1)}, u32[]{:S(2)}) copy-start(bf16[64,2048]{1,0:T(8,128)(2,1)S(1)} %collective-permute-done.2.proj1_ref) | copy-start | bytes 786436
  84.7 32.9 %copy-start.8 = (bf16[2048]{0:T(1024)(128)(2,1)S(1)}, bf16[2048]{0:T(1024)(128)(2,1)}, u32[]{:S(2)}) copy-start(bf16[2048]{0:T(1024)(128)(2,1)} %param.26) | copy-start | bytes 12292
  84.7 33.5 %copy-start.7 = (bf16[2048,12]{0,1:T(8,128)(2,1)S(1)}, bf16[2048,12]{0,1:T(8,128)(2,1)}, u32[]{:S(2)}) copy-start(bf16[2048,12]{0,1:T(8,128)(2,1)} %param.27) | copy-start | bytes 147460
  84.8 22.3 %all-to-all-start.2 = ((bf16[32,40,128]{2,1,0:T(8,128)(2,1)}), bf16[32,40,128]{2,1,0:T(8,128)(2,1)S(1)}, u32[]{:S(2)}, u32[]{:S(2)}) async-start(bf16[32,40,128]{2,1,0:T(8,128)(2,1)} %shard_map.148), calls=%async_computation.2 | async-start | bytes 655360 | tf_op jit(solution)/shard_map/all_to_all | solution.py:392
  98.2 28.9 %collective-permute-start.6 = (bf16[128,2048]{1,0:T(8,128)(2,1)S(1)}, bf16[128,2048]{1,0:T(8,128)(2,1)}, u32[]{:S(2)}, u32[]{:S(2)}) collective-permute-start(bf16[128,2048]{1,0:T(8,128)(2,1)S(1)} %slice.9), channel_id=1, source_target_pairs={{0,6},{4,0},{2,4},{6,2},{1,7},{5,1},{3,5},{7,3},{8,14},{12,8},{10,... | collective-permute-start | bytes 1572872 | tf_op jit(solution)/shard_map/ppermute | solution.py:380
  105.1 22.0 %collective-permute-start.5 = (bf16[128,2048]{1,0:T(8,128)(2,1)S(1)}, bf16[128,2048]{1,0:T(8,128)(2,1)}, u32[]{:S(2)}, u32[]{:S(2)}) collective-permute-start(bf16[128,2048]{1,0:T(8,128)(2,1)S(1)} %slice.8), channel_id=1, source_target_pairs={{0,4},{4,2},{2,6},{6,0},{1,5},{5,3},{3,7},{7,1},{8,12},{12,10},{10... | collective-permute-start | bytes 1572872 | tf_op jit(solution)/shard_map/ppermute | solution.py:380
  107.8 19.3 %all-to-all-start.3 = ((f32[64,1,128]{2,1,0:T(1,128)}), f32[64,1,128]{2,1,0:T(1,128)S(1)}, u32[]{:S(2)}, u32[]{:S(2)}) async-start(f32[64,1,128]{2,1,0:T(1,128)} %bitcast.7), calls=%async_computation.3 | async-start | bytes 65536 | tf_op jit(solution)/shard_map/all_to_all | solution.py:400
  127.1 0.6 copy-start.6
Sparse Core Ops, SparseCore 0:
  9.4 51.1 all-gather.2

commit v3 on v2

v3 whole, which is shorter than its diff:
```python
import math

import jax
import jax.numpy as jnp
from jax import lax
from jax.experimental import pallas as pl
from jax.experimental.pallas import tpu as pltpu
from jax.sharding import Mesh, PartitionSpec as P

D = 4096
EXPERTS = 3
TASKS = 4
REQ_GRP = 4
HIST = 32
epsilon = 1e-05

CHIPS = ("z", "xh", "xl")
ALL = ("z", "xh", "xl", "c")
N_CHIPS = 32
F32 = jnp.float32
BF16 = jnp.bfloat16
HIGH = lax.Precision.HIGHEST

VMEM = pl.BlockSpec(memory_space=pltpu.VMEM)
ANY = pl.BlockSpec(memory_space=pl.ANY)
HBM = pl.BlockSpec(memory_space=pltpu.HBM)
ROW_BY_ROW = (((1,), (1,)), ((), ()))


def params(room_kib):
    return pltpu.CompilerParams(vmem_limit_bytes=(64 << 20) - (room_kib << 10))


def block_of(chip):
    return (chip & ~3) | ((chip & 1) << 1) | ((chip >> 1) & 1)


def split2(x):
    high = x.astype(BF16).astype(F32)
    return high, x - high


def lanes(shape):
    return lax.broadcasted_iota(jnp.int32, shape, len(shape) - 1)


def rows(shape):
    return lax.broadcasted_iota(jnp.int32, shape, len(shape) - 2)


def token_sums(x):
    padded = jnp.concatenate([x, jnp.zeros((128 - x.shape[0], 128), F32)], axis=0)
    return lax.dot_general(jnp.ones((8, 128), F32), padded, ROW_BY_ROW, precision=HIGH, preferred_element_type=F32)


def turn(x, by):
    return pltpu.roll(jnp.broadcast_to(x, (8, 128)), by, 1)[0:1]


def widen(x):
    return jnp.concatenate([x, jnp.zeros((1, 128 - x.shape[1]), x.dtype)], axis=1)


def pack_kernel(hist_ref, gain_ref, query_ref, head_ref, out_ref):
    hist = hist_ref[...].astype(F32)
    out_ref[0:128, :] = jnp.concatenate([hist, jnp.zeros((64, 128), F32)], axis=0).T.astype(BF16)
    row = rows((16, 128))
    ends = jnp.concatenate([gain_ref[...].astype(F32), query_ref[...].astype(F32)], axis=1)
    out_ref[128:144, :] = jnp.where(row == 0, ends, 0.0).astype(BF16)
    heads = jnp.zeros((16, 128), F32)
    for k in range(EXPERTS):
        head = head_ref[k].astype(F32)
        for t in range(TASKS):
            heads = jnp.where(row == t * EXPERTS + k, head[t : t + 1], heads)
    out_ref[144:160, :] = heads.astype(BF16)


def spread_kernel(pair_ref, out_ref, hist_ref, query_ref):
    core = lax.axis_index("c")
    tokens = pl.ds(pl.multiple_of(core * 64, 64), 64)
    first = pair_ref[0, tokens, :].astype(F32)
    second = pair_ref[1, tokens, :].astype(F32)
    hist = jnp.where(lanes((64, 128)) < 64, first, pltpu.roll(second, 64, 1))
    head0 = pair_ref[0, 128:144, :].astype(F32)[0:1]
    head1 = pair_ref[1, 128:144, :].astype(F32)[0:1]
    low = lanes((1, 128)) < 64
    gain = jnp.where(low, head0, turn(head1, 64))
    query = jnp.where(low, turn(head0, 64), head1)
    scaled = (hist * gain).astype(BF16)
    high, rest = split2(token_sums(hist * hist))
    row = rows((8, 128))
    extra = jnp.where(row == 0, high, jnp.where(row == 1, rest, 0.0)).astype(BF16)
    for chip in range(N_CHIPS):
        out_ref[chip, 0:64, :] = scaled
        out_ref[chip, 64:72, :] = extra
    hist_ref[...] = hist.astype(BF16)
    query_ref[...] = jnp.broadcast_to(query, (8, 128))


def tower_kernel(got_ref, up0_ref, up1_ref, down0_ref, down1_ref, out_ref, down, sems):
    copies = []
    for i, source in enumerate((down0_ref, down1_ref)):
        copies.append(pltpu.make_async_copy(source, down.at[128 * i : 128 * i + 128, :], sems.at[i]))
    for copy in copies:
        copy.start()
    stats = jnp.zeros((8, 128), F32)
    for chip in range(N_CHIPS):
        stats = stats + got_ref[chip, 64:72, :].astype(F32)
    inverse = lax.rsqrt((stats[0:1] + stats[1:2]) / D + epsilon)
    column = jnp.broadcast_to(inverse, (128, 128)).T[0:64]
    total = jnp.zeros((64, 256), F32)
    for b in range(0, N_CHIPS, 2):
        left = jnp.concatenate([got_ref[block_of(b), 0:64, :], got_ref[block_of(b + 1), 0:64, :]], axis=1)
        part = slice(b * 128, b * 128 + 256)
        right = jnp.concatenate([up0_ref[part, :], up1_ref[part, :]], axis=1)
        total = total + jnp.dot(left, right, preferred_element_type=F32)
    hidden = jax.nn.gelu(total * jnp.concatenate([column, column], axis=1)).astype(BF16)
    for copy in copies:
        copy.wait()
    for b in range(0, N_CHIPS, 2):
        part = jnp.dot(hidden, down[:, b * 128 : b * 128 + 256], preferred_element_type=F32).astype(BF16)
        out_ref[block_of(b), :, :] = part[:, 0:128]
        out_ref[block_of(b + 1), :, :] = part[:, 128:256]


def values_kernel(got_ref, hist_ref, query_ref, proj0_ref, proj1_ref, out_ref, proj, sems):
    copies = []
    for i, source in enumerate((proj0_ref, proj1_ref)):
        copies.append(pltpu.make_async_copy(source, proj.at[64 * i : 64 * i + 64, :], sems.at[i]))
    for copy in copies:
        copy.start()
    core = lax.axis_index("c")
    summed = got_ref[0].astype(F32)
    for chip in range(1, N_CHIPS):
        summed = summed + got_ref[chip].astype(F32)
    tower = (hist_ref[...].astype(F32) + summed).astype(BF16).astype(F32)
    square_high, square_rest = split2(token_sums(tower * tower))
    dot_high, dot_rest = split2(token_sums(tower * query_ref[0:1, :]))
    row = rows((8, 128))
    extra = jnp.where(row == 2, dot_high, jnp.where(row == 3, dot_rest, 0.0))
    extra = jnp.where(row == 0, square_high, jnp.where(row == 1, square_rest, extra)).astype(BF16)
    mine = jnp.where(core == 0, tower, pltpu.roll(tower, 64, 1)).astype(BF16)
    low = lanes((32, 128)) < 64
    for copy in copies:
        copy.wait()
    for j in range(16):
        part = jnp.dot(mine, proj[:, 128 * j : 128 * j + 128], preferred_element_type=F32)
        turned = pltpu.roll(part, 64, 1)
        out_ref[2 * j, 0:32, :] = jnp.where(low, part[0:32], turned[32:64]).astype(BF16)
        out_ref[2 * j + 1, 0:32, :] = jnp.where(low, turned[0:32], part[32:64]).astype(BF16)
        out_ref[2 * j, 32:40, :] = extra
        out_ref[2 * j + 1, 32:40, :] = extra


def user_kernel(got_ref, owner_ref, task_ref, out_ref):
    values = got_ref[0, 0:32, :].astype(F32)
    stats = got_ref[0, 32:40, :].astype(F32)
    for chip in range(1, N_CHIPS):
        values = values + got_ref[chip, 0:32, :].astype(F32)
        stats = stats + got_ref[chip, 32:40, :].astype(F32)
    squares = stats[0:1] + stats[1:2]
    dotted = stats[2:3] + stats[3:4]
    weight = jax.nn.sigmoid(dotted * lax.rsqrt(squares / D + epsilon))
    column = jnp.broadcast_to(weight, (128, 128)).T
    weights = jnp.where(lanes((32, 128)) < 64, column[0:32], column[32:64])
    user = jnp.sum(weights * values, axis=0, keepdims=True) / math.sqrt(HIST)
    slots = widen(owner_ref[...].astype(F32)) + turn(widen(task_ref[...].astype(F32)), 32)
    slots = slots + turn(slots, 64)
    out_ref[...] = jnp.where(rows((128, 128)) % 2 == 0, user, slots)


SLOTS = 1024
HALF = 512


def score_kernel(
    got_ref, cand_ref, own_task_ref, pair_ref, cross_u_ref, cross_v_ref, bias_ref, gate_ref, w0_ref, w1_ref,
    out_ref, gates_ref, users, x, cross_u, cross_v, w, sems,
):
    core = lax.axis_index("c")
    chip_here = lax.axis_index("z") * 4 + lax.axis_index("xh") * 2 + lax.axis_index("xl")

    def piece(i):
        part = slice(HALF * i, HALF * i + HALF)
        return pltpu.make_async_copy(cand_ref.at[part, :], x.at[part, :], sems.at[i])

    arrivals = [piece(0), piece(1)]
    get_u = pltpu.make_async_copy(cross_u_ref, cross_u, sems.at[2])
    get_v = pltpu.make_async_copy(cross_v_ref, cross_v.at[0:128, :], sems.at[3])
    get_w = []
    for k in range(EXPERTS):
        for i, source in enumerate((w0_ref, w1_ref)):
            start = 256 * k + 128 * i
            get_w.append(pltpu.make_async_copy(source.at[k], w.at[:, start : start + 128], sems.at[4 + 2 * k + i]))
    for copy in (arrivals[0], get_u, get_v, arrivals[1], *get_w):
        copy.start()
    row = rows((16, 128))
    low_half = lanes((1, 128)) < 64
    for j in range(16):
        full = jnp.zeros((16, 128), F32)
        for c in range(2):
            first = got_ref[8 * j + 2 * c : 8 * j + 2 * c + 1, :]
            second = got_ref[8 * j + 4 + 2 * c : 8 * j + 5 + 2 * c, :]
            full = jnp.where(row % 4 == 2 * c, jnp.where(low_half, first, turn(second, 64)), full)
            full = jnp.where(row % 4 == 2 * c + 1, jnp.where(low_half, turn(first, 64), second), full)
        high, rest = split2(full)
        mid, last = split2(rest)
        users[:, 128 * j : 128 * j + 128] = jnp.where(
            row < 4, high, jnp.where(row < 8, mid, jnp.where(row < 12, last, 0.0))
        ).astype(BF16)
    quarter = lanes((1, 128)) // 32
    owners, tasks = [], []
    for b in range(8):
        owner = jnp.zeros((1, 128), F32)
        task = jnp.zeros((1, 128), F32)
        for q in range(4):
            slots = got_ref[pl.ds(4 * (4 * b + q) + 2 * core + 1, 1), :]
            turned = turn(slots, 32)
            owner = jnp.where(quarter == q, (slots, turned)[q % 2], owner)
            task = jnp.where(quarter == q, (turned, slots)[q % 2], task)
        owners.append(owner)
        tasks.append(task)
    owners = jnp.concatenate(owners, axis=1)
    tasks = jnp.concatenate(tasks, axis=1)
    heads = jnp.concatenate([pair_ref[core, 144:160, :], pair_ref[1 - core, 144:160, :]], axis=1)
    row = rows((16, 2048))
    bias = bias_ref[...].astype(F32)
    cross_v[128:144, :] = jnp.where(row == 0, bias, jnp.where(row == 1, 1.0, 0.0)).astype(BF16)
    cross_v[144:256, :] = jnp.zeros((112, 2048), BF16)
    ones = jnp.where(lanes((HALF, 128)) < 2, 1.0, 0.0).astype(BF16)
    row = rows((16, HALF))
    for i in range(2):
        part = slice(HALF * i, HALF * i + HALF)
        hot = jnp.where((row % 4).astype(F32) == owners[:, part], 1.0, 0.0).T.astype(BF16)
        arrivals[i].wait()
        for j in range(4):
            cols = slice(512 * j, 512 * j + 512)
            added = jnp.dot(hot, users[:, cols], preferred_element_type=F32)
            x[part, cols] = (x[part, cols].astype(F32) + added).astype(BF16)
        if i == 0:
            get_u.wait()
        low = jnp.dot(x[part, :], cross_u[...], preferred_element_type=F32).astype(BF16)
        left = jnp.concatenate([low, ones], axis=1)
        if i == 0:
            get_v.wait()
        for j in range(4):
            cols = slice(512 * j, 512 * j + 512)
            cross = jnp.dot(left, cross_v[:, cols], preferred_element_type=F32)
            x[part, cols] = (x[part, cols].astype(F32) * cross).astype(BF16)
    own = x[pl.ds(pl.multiple_of(chip_here * 32, 32), 32), :]
    logits = lax.dot_general(gate_ref[...], own, ROW_BY_ROW, preferred_element_type=F32)
    row = rows((16, 32))
    picked = jnp.where(row // EXPERTS == own_task_ref[...], jax.nn.sigmoid(logits), 0.0)
    gates = picked / jnp.sum(picked, axis=0, keepdims=True)
    row_of = jnp.zeros((1, 128), F32)
    for k in range(EXPERTS):
        gate = widen(jnp.sum(jnp.where(row % EXPERTS == k, gates, 0.0), axis=0, keepdims=True))
        row_of = row_of + (gate if k == 0 else turn(gate, 32 * k))
    gates_ref[...] = row_of
    for copy in get_w:
        copy.wait()
    active = jax.nn.relu(jnp.dot(x[...], w[...], preferred_element_type=F32)).astype(BF16)
    row = rows((16, SLOTS)).astype(F32)
    outs = []
    for k in range(EXPERTS):
        terms = lax.dot_general(heads, active[:, 256 * k : 256 * k + 256], ROW_BY_ROW, preferred_element_type=F32)
        outs.append(jnp.sum(jnp.where(row == tasks * EXPERTS + k, terms, 0.0), axis=0, keepdims=True))
    for b in range(8):
        stack = jnp.concatenate([o[:, 128 * b : 128 * b + 128] for o in outs] + [jnp.zeros((5, 128), F32)], axis=0)
        turns = [stack] + [pltpu.roll(stack, 32 * q, 1) for q in range(1, 4)]
        for q in range(4):
            message = jnp.zeros((1, 128), F32)
            for k in range(EXPERTS):
                message = jnp.where(quarter == k, turns[(k - q) % 4][k : k + 1], message)
            out_ref[4 * b + q : 4 * b + q + 1, :] = message


def home_kernel(got_ref, gates_ref, owner_ref, out_ref):
    total = jnp.sum(got_ref[...], axis=0, keepdims=True) * gates_ref[...]
    total = total + turn(total, 64)
    total = total + turn(total, 32)
    out_ref[...] = jnp.where(owner_ref[...] < REQ_GRP, total[:, 0:32], 0.0)


def body(
    hist, tower_gain, up_w, down_w, query, proj_w, cand, owner, task, cross_u, cross_v, cross_bias, gate_w, expert_w, head_w,
):
    owner, task = owner[None, :], task[None, :]
    everyone = lax.all_gather(cand, CHIPS, axis=0, tiled=True)
    message = pl.pallas_call(
        pack_kernel,
        out_shape=jax.ShapeDtypeStruct((160, 128), BF16),
        in_specs=[VMEM] * 4,
        out_specs=VMEM,
        compiler_params=params(64),
    )(hist.T, tower_gain, query[None, :], head_w.transpose(1, 0, 2))
    pair = lax.all_gather(message, "c", axis=0)
    spread, hist_c, query_c = pl.pallas_call(
        spread_kernel,
        out_shape=(
            jax.ShapeDtypeStruct((N_CHIPS, 72, 128), BF16),
            jax.ShapeDtypeStruct((64, 128), BF16),
            jax.ShapeDtypeStruct((8, 128), F32),
        ),
        in_specs=[VMEM],
        out_specs=(VMEM,) * 3,
        compiler_params=params(63 << 10),
    )(pair)
    tokens = lax.all_to_all(spread, CHIPS, 0, 0, tiled=True)
    swap = lambda x: lax.ppermute(x, "c", [(0, 1), (1, 0)])
    parts = pl.pallas_call(
        tower_kernel,
        out_shape=jax.ShapeDtypeStruct((N_CHIPS, 64, 128), BF16),
        in_specs=[VMEM] * 3 + [HBM] * 2,
        out_specs=VMEM,
        scratch_shapes=[pltpu.VMEM((256, 4096), BF16), pltpu.SemaphoreType.DMA((2,))],
        compiler_params=params(13900),
    )(tokens, up_w, swap(up_w), down_w, swap(down_w))
    summed = lax.all_to_all(parts, CHIPS, 0, 0, tiled=True)
    values = pl.pallas_call(
        values_kernel,
        out_shape=jax.ShapeDtypeStruct((N_CHIPS, 40, 128), BF16),
        in_specs=[VMEM] * 3 + [HBM] * 2,
        out_specs=VMEM,
        scratch_shapes=[pltpu.VMEM((128, 2048), BF16), pltpu.SemaphoreType.DMA((2,))],
        compiler_params=params(12160),
    )(summed, hist_c, query_c, proj_w, swap(proj_w))
    values = lax.all_to_all(values, CHIPS, 0, 0, tiled=True)
    user = pl.pallas_call(
        user_kernel,
        out_shape=jax.ShapeDtypeStruct((128, 128), F32),
        in_specs=[VMEM] * 3,
        out_specs=VMEM,
        compiler_params=params(12288),
    )(values, owner, task)
    users = lax.all_to_all(user, ALL, 0, 0, tiled=True)
    gate_rows = jnp.pad(gate_w.T, ((0, 4), (0, 0)))
    part, gates = pl.pallas_call(
        score_kernel,
        out_shape=(jax.ShapeDtypeStruct((N_CHIPS, 128), F32), jax.ShapeDtypeStruct((1, 128), F32)),
        in_specs=[VMEM, HBM, VMEM, VMEM, HBM, HBM, VMEM, VMEM, HBM, HBM],
        out_specs=(VMEM,) * 2,
        scratch_shapes=[
            pltpu.VMEM((16, 2048), BF16),
            pltpu.VMEM((SLOTS, 2048), BF16),
            pltpu.VMEM((2048, 128), BF16),
            pltpu.VMEM((256, 2048), BF16),
            pltpu.VMEM((2048, 768), BF16),
            pltpu.SemaphoreType.DMA((10,)),
        ],
        compiler_params=params(11700),
    )(users, everyone, task, pair, cross_u, cross_v, cross_bias[None, :], gate_rows, expert_w, swap(expert_w))
    back = lax.all_to_all(part, CHIPS, 0, 0, tiled=True)
    score = pl.pallas_call(
        home_kernel,
        out_shape=jax.ShapeDtypeStruct((1, 32), F32),
        in_specs=[VMEM] * 3,
        out_specs=VMEM,
        compiler_params=params(12288),
    )(back, gates, owner)
    return score[0]


def solution(mesh):
    fine = Mesh(mesh.devices.reshape(mesh.devices.shape[0], 8, 2, 2, 2), ("grp", "z", "xl", "xh", "c"))
    t = ("z", "xl", "xh", "c")
    in_specs = (
        P("grp", t),
        P(None, t),
        P(None, t),
        P(t, None),
        P(t),
        P(t, None),
        P(("grp",) + t, None),
        P(("grp",) + t),
        P(("grp",) + t),
        P(),
        P(),
        P(),
        P(),
        P(None, None, t),
        P(None, None, t),
    )
    return jax.shard_map(body, mesh=fine, in_specs=in_specs, out_specs=P(("grp",) + t), check_vma=False)
```

time: 168 us -> 145 us (0.86)
  starting transfers between devices: 55.8 us -> 32 us
  blocking collectives: 17.2 us -> 37.9 us
  Pallas kernels: 30.7 us -> 20.3 us
  local copies, waits for them, and re-layouts: 6 us -> 0.07 us
  waiting for transfers between devices: 43.6 us -> 39.7 us
    all_to_all x0 -> x1, blocking collectives: none -> 21 us  [body(): values = lax.all_to_all(values, CHIPS, 0, 0, tiled=True)]
    ppermute x4 -> x0, starting transfers between devices: 14.4 us -> none  [body(): lax.ppermute(x, ('xl', 'xh'), [(at(i), at(i + by)) for i in range(4)])]
    ppermute x4 -> x0, waiting for transfers between devices: 7.35 us -> none  [body(): lax.ppermute(x, ('xl', 'xh'), [(at(i), at(i + by)) for i in range(4)])]
    all_to_all x1, waiting for transfers between devices: 5.49 us -> 10.9 us  [body(): summed = lax.all_to_all(parts, CHIPS, 0, 0, tiled=True)]
    all_to_all x1 -> x0, starting transfers between devices: 5.01 us -> none  [body(): values = lax.all_to_all(values, CHIPS, 0, 0, tiled=True)]
    pallas_call x1, Pallas kernels: 17 us -> 12.2 us  [body(): pl.pallas_call(score_kernel, out_shape=(jax.ShapeDtypeStruct((N_CHIPS, 12...]
    all_to_all x1, starting transfers between devices: 9.87 us -> 5.26 us  [body(): users = lax.all_to_all(user, ALL, 0, 0, tiled=True)]
    all_to_all x1, waiting for transfers between devices: 18 us -> 14.2 us  [body(): tokens = lax.all_to_all(spread, CHIPS, 0, 0, tiled=True)]
  transfers between devices with their start and end apart: 13 -> 8, of which waited for: 7 -> 6; matrix products, arithmetic and copies ran while one was open for 2% -> 0% of each run, Pallas kernels for 7% -> 5%
where the time goes in v3:
time: 145 us; the launch traced here: 144 us
  waiting for transfers between devices  39.7 us (27%)
  blocking collectives  37.9 us (26%)
  starting transfers between devices  32 us (22%)
  Pallas kernels  20.3 us (14%)
  between operations  13.6 us (9%)
    all_to_all x1, blocking collectives, body(): values = lax.all_to_all(values, CHIPS, 0, 0, tiled=True)  21 us
    all_to_all x1, blocking collectives, body(): back = lax.all_to_all(part, CHIPS, 0, 0, tiled=True)  14.7 us
    all_to_all x1, waiting for transfers between devices, body(): tokens = lax.all_to_all(spread, CHIPS, 0, 0, tiled=True)  14.2 us
    all_to_all x1, starting transfers between devices, body(): tokens = lax.all_to_all(spread, CHIPS, 0, 0, tiled=True)  13.2 us
    pallas_call x1, Pallas kernels, body(): pl.pallas_call(score_kernel, out_shape=(jax.ShapeDtypeStruct((N_CHIPS, 12...  12.2 us
    all_to_all x1, waiting for transfers between devices, body(): summed = lax.all_to_all(parts, CHIPS, 0, 0, tiled=True)  10.9 us
    all_to_all x1, waiting for transfers between devices, body(): users = lax.all_to_all(user, ALL, 0, 0, tiled=True)  9.96 us
    ppermute x4, starting transfers between devices, body(): swap = lambda x: lax.ppermute(x, 'c', [(0, 1), (1, 0)])  8.93 us
  transfers between devices with their start and end apart: 8, of which 6 were waited for; matrix products, arithmetic and copies ran while one was open for 0% of the time, Pallas kernels for 5%

profile of v3, /device:TPU:56, one launch (start us, length us, event | category | flops | bytes accessed | tf_op | source)
XLA Modules:
  0.0 143.7 jit_solution(7800854778787239602)
XLA Ops:
  6.5 0.0 all-gather.3.cloned.1.call-start
  6.5 0.7 all-gather.3.cloned.1.call-update
  7.3 1.5 %shard_map.145 = bf16[160,128]{1,0:T(8,128)(2,1)} custom-call(bf16[64,128]{1,0:T(8,128)(2,1)} %bitcast.24, bf16[1,64]{1,0:T(2,128)(2,1)} %gain_ref.1, bf16[1,64]{1,0:T(2,128)(2,1)} %bitcast.26, bf16[3,4,128]{2,1,0:T(4,128)(2,1)} %bitcast.25), custom_call_target="tpu_custom_call" | custom-call | tf_op jit(solution)/shard_map/pallas_call | solution.py:290
  8.7 0.0 copy-start
  8.7 2.2 %all-gather = bf16[320,128]{1,0:T(8,128)(2,1)S(1)} all-gather(bf16[160,128]{1,0:T(8,128)(2,1)} %shard_map.145), channel_id=2, replica_groups=mesh['grp'=8,'z'=8,'xl'=2,'xh'=2,'c'=2] {'c'}, dimensions={0}, use_global_device_ids=true | all-gather | bytes 122880 | tf_op jit(solution)/shard_map/all_gather | solution.py:297
  10.9 1.1 shard_map.146
  12.0 13.2 %all-to-all-start = ((bf16[32,72,128]{2,1,0:T(8,128)(2,1)}), bf16[32,72,128]{2,1,0:T(8,128)(2,1)S(1)}, u32[]{:S(2)}, u32[]{:S(2)}) async-start(bf16[32,72,128]{2,1,0:T(8,128)(2,1)} %get-tuple-element.10), calls=%async_computation | async-start | bytes 1179648 | tf_op jit(solution)/shard_map/all_to_all | solution.py:309
  25.2 0.0 copy-start.3
  25.2 2.1 %collective-permute-start = (bf16[4096,128]{1,0:T(8,128)(2,1)}, bf16[4096,128]{1,0:T(8,128)(2,1)S(1)}, u32[]{:S(2)}, u32[]{:S(2)}) collective-permute-start(bf16[4096,128]{1,0:T(8,128)(2,1)} %up0_ref.1), channel_id=1, source_target_pairs={{0,1},{1,0},{2,3},{3,2},{4,5},{5,4},{6,7},{7,6},{8,9},{9,8},{10,11... | collective-permute-start | bytes 3145736 | tf_op jit(solution)/shard_map/ppermute | solution.py:310
  27.3 2.4 %collective-permute-start.1 = (bf16[128,4096]{1,0:T(8,128)(2,1)}, bf16[128,4096]{1,0:T(8,128)(2,1)}, u32[]{:S(2)}, u32[]{:S(2)}) collective-permute-start(bf16[128,4096]{1,0:T(8,128)(2,1)} %down0_ref.1), channel_id=1, source_target_pairs={{0,1},{1,0},{2,3},{3,2},{4,5},{5,4},{6,7},{7,6},{8,9},{9,8},{10,11... | collective-permute-start | bytes 3145736 | tf_op jit(solution)/shard_map/ppermute | solution.py:310
  29.7 0.4 collective-permute-done.up1_ref
  30.1 2.2 %collective-permute-done.1.down1_ref = bf16[128,4096]{1,0:T(8,128)(2,1)} collective-permute-done((bf16[128,4096]{1,0:T(8,128)(2,1)}, bf16[128,4096]{1,0:T(8,128)(2,1)}, u32[]{:S(2)}, u32[]{:S(2)}) %collective-permute-start.1) | collective-permute-done | bytes 1048608 | tf_op jit(solution)/shard_map/ppermute | solution.py:310
  32.3 14.2 %all-to-all-done.got_ref = bf16[32,72,128]{2,1,0:T(8,128)(2,1)S(1)} async-done(((bf16[32,72,128]{2,1,0:T(8,128)(2,1)}), bf16[32,72,128]{2,1,0:T(8,128)(2,1)S(1)}, u32[]{:S(2)}, u32[]{:S(2)}) %all-to-all-start) | async-done | bytes 589856 | tf_op jit(solution)/shard_map/all_to_all | solution.py:309
  46.5 0.0 copy-done
  46.5 3.4 %shard_map.147 = bf16[32,64,128]{2,1,0:T(8,128)(2,1)} custom-call(bf16[32,72,128]{2,1,0:T(8,128)(2,1)S(1)} %all-to-all-done.got_ref, bf16[4096,128]{1,0:T(8,128)(2,1)S(1)} %copy-done, bf16[4096,128]{1,0:T(8,128)(2,1)S(1)} %collective-permute-done.up1_ref, bf16[128,4096]{1,0:T(8,128)(2,1)} %down0_ref.1, bf16[128,4096]{1,0:T(8,128)(2,1)} %collective-permute-done.1.down1_ref), custom_call_target="tpu_custom_call" | custom-call | tf_op jit(solution)/shard_map/pallas_call | solution.py:311
  49.9 0.0 copy-start.4
  49.9 0.0 copy-start.5
  50.0 0.0 copy-start.7
  50.0 0.0 copy-start.6
  50.0 4.7 %all-to-all-start.1 = ((bf16[32,64,128]{2,1,0:T(8,128)(2,1)}), bf16[32,64,128]{2,1,0:T(8,128)(2,1)S(1)}, u32[]{:S(2)}, u32[]{:S(2)}) async-start(bf16[32,64,128]{2,1,0:T(8,128)(2,1)} %shard_map.147), calls=%async_computation.1 | async-start | bytes 1048576 | tf_op jit(solution)/shard_map/all_to_all | solution.py:319
  54.7 0.0 copy-start.1
  54.7 0.0 copy-start.2
  54.7 2.1 %collective-permute-start.3 = (bf16[3,2048,128]{2,1,0:T(8,128)(2,1)}, bf16[3,2048,128]{2,1,0:T(8,128)(2,1)}, u32[]{:S(2)}, u32[]{:S(2)}) collective-permute-start(bf16[3,2048,128]{2,1,0:T(8,128)(2,1)} %w0_ref.1), channel_id=1, source_target_pairs={{0,1},{1,0},{2,3},{3,2},{4,5},{5,4},{6,7},{7,6},{8,9},{9,8},{10,11... | collective-permute-start | bytes 4718600 | tf_op jit(solution)/shard_map/ppermute | solution.py:310
  56.7 0.0 copy-done.3
  56.8 2.4 %collective-permute-start.2 = (bf16[64,2048]{1,0:T(8,128)(2,1)S(1)}, bf16[64,2048]{1,0:T(8,128)(2,1)S(1)}, u32[]{:S(2)}, u32[]{:S(2)}) collective-permute-start(bf16[64,2048]{1,0:T(8,128)(2,1)S(1)} %copy-done.3), channel_id=1, source_target_pairs={{0,1},{1,0},{2,3},{3,2},{4,5},{5,4},{6,7},{7,6},{8,9},{9,8},{10,11... | collective-permute-start | bytes 786440 | tf_op jit(solution)/shard_map/ppermute | solution.py:310
  59.2 1.3 collective-permute-done.2.proj1_ref
  60.5 10.9 %all-to-all-done.1.got_ref = bf16[32,64,128]{2,1,0:T(8,128)(2,1)S(1)} async-done(((bf16[32,64,128]{2,1,0:T(8,128)(2,1)}), bf16[32,64,128]{2,1,0:T(8,128)(2,1)S(1)}, u32[]{:S(2)}, u32[]{:S(2)}) %all-to-all-start.1) | async-done | bytes 524320 | tf_op jit(solution)/shard_map/all_to_all | solution.py:319
  71.4 0.7 shard_map.148
  72.1 21.0 %all_to_all.37.got_ref = bf16[32,40,128]{2,1,0:T(8,128)(2,1)S(1)} all-to-all(bf16[32,40,128]{2,1,0:T(8,128)(2,1)S(1)} %shard_map.148), channel_id=1, replica_groups=mesh['grp'=8,'z'=8,'xl'=2,'xh'=2,'c'=2] {'z','xh','xl'}, dimensions={0} | all-to-all | bytes 655360 | tf_op jit(solution)/shard_map/all_to_all | solution.py:328
  93.1 0.0 copy-done.4
  93.1 0.0 copy-done.5
  93.1 0.8 shard_map.149
  93.9 5.3 %all-to-all-start.3 = ((f32[64,2,128]{2,1,0:T(2,128)}), f32[64,2,128]{2,1,0:T(2,128)S(1)}, u32[]{:S(2)}, u32[]{:S(2)}) async-start(f32[64,2,128]{2,1,0:T(2,128)} %bitcast.6), calls=%async_computation.3 | async-start | bytes 131072 | tf_op jit(solution)/shard_map/all_to_all | solution.py:336
  99.1 0.0 copy-done.7
  99.2 0.0 copy-done.6
  99.2 0.0 collective-permute-done.3.w1_ref
  99.2 10.0 %all-to-all-done.3 = f32[64,2,128]{2,1,0:T(2,128)S(1)} async-done(((f32[64,2,128]{2,1,0:T(2,128)}), f32[64,2,128]{2,1,0:T(2,128)S(1)}, u32[]{:S(2)}, u32[]{:S(2)}) %all-to-all-start.3) | async-done | bytes 65568 | tf_op jit(solution)/shard_map/all_to_all | solution.py:336
  109.2 0.0 all-gather.3.cloned.1.call-done.cand_ref
  109.2 0.0 copy-done.1
  109.2 0.0 copy-done.2
  109.2 12.2 %shard_map.150 = (f32[32,128]{1,0:T(8,128)S(1)}, f32[1,128]{1,0:T(1,128)S(1)}) custom-call(f32[128,128]{1,0:T(8,128)S(1)} %bitcast.16, bf16[1024,2048]{1,0:T(8,128)(2,1)} %all-gather.3.cloned.1.call-done.cand_ref, s32[1,32]{1,0:T(1,128)S(1)} %bitcast.20, bf16[2,160,128]{2,1,0:T(8,128)(2,1)S(1)} %bitcast.15, bf16[2048,128]{1,0:T(8,128)(2,1)S(1)} %copy-done.1, ...), custom_call_target="tpu_custom_call" | custom-call | tf_op jit(solution)/shard_map/pallas_call | solution.py:338
  121.4 14.7 %all_to_all.38 = f32[32,1,128]{2,1,0:T(1,128)S(1)} all-to-all(f32[32,1,128]{2,1,0:T(1,128)S(1)} %bitcast.18), channel_id=1, replica_groups=mesh['grp'=8,'z'=8,'xl'=2,'xh'=2,'c'=2] {'z','xh','xl'}, dimensions={0} | all-to-all | bytes 32768 | tf_op jit(solution)/shard_map/all_to_all | solution.py:353
  136.2 0.7 shard_map.151
  (2 shorter events, 0.0 us)
Async XLA Ops:
  6.5 102.6 %all-gather.3.cloned.1.call-start = ((), (), s32[]{:S(2)}) async-start(), calls=%async_computation.5 | async-start | bytes 4325376 | tf_op jit(solution)/shard_map/all_gather | solution.py:289
  8.7 37.8 %copy-start = (bf16[4096,128]{1,0:T(8,128)(2,1)S(1)}, bf16[4096,128]{1,0:T(8,128)(2,1)}, u32[]{:S(2)}) copy-start(bf16[4096,128]{1,0:T(8,128)(2,1)} %up0_ref.1) | copy-start | bytes 3145732
  12.0 34.5 %all-to-all-start = ((bf16[32,72,128]{2,1,0:T(8,128)(2,1)}), bf16[32,72,128]{2,1,0:T(8,128)(2,1)S(1)}, u32[]{:S(2)}, u32[]{:S(2)}) async-start(bf16[32,72,128]{2,1,0:T(8,128)(2,1)} %get-tuple-element.10), calls=%async_computation | async-start | bytes 1179648 | tf_op jit(solution)/shard_map/all_to_all | solution.py:309
  25.2 31.6 %copy-start.3 = (bf16[64,2048]{1,0:T(8,128)(2,1)S(1)}, bf16[64,2048]{1,0:T(8,128)(2,1)}, u32[]{:S(2)}) copy-start(bf16[64,2048]{1,0:T(8,128)(2,1)} %proj0_ref.1) | copy-start | bytes 786436
  25.2 4.9 %collective-permute-start = (bf16[4096,128]{1,0:T(8,128)(2,1)}, bf16[4096,128]{1,0:T(8,128)(2,1)S(1)}, u32[]{:S(2)}, u32[]{:S(2)}) collective-permute-start(bf16[4096,128]{1,0:T(8,128)(2,1)} %up0_ref.1), channel_id=1, source_target_pairs={{0,1},{1,0},{2,3},{3,2},{4,5},{5,4},{6,7},{7,6},{8,9},{9,8},{10,11... | collective-permute-start | bytes 3145736 | tf_op jit(solution)/shard_map/ppermute | solution.py:310
  27.3 5.0 %collective-permute-start.1 = (bf16[128,4096]{1,0:T(8,128)(2,1)}, bf16[128,4096]{1,0:T(8,128)(2,1)}, u32[]{:S(2)}, u32[]{:S(2)}) collective-permute-start(bf16[128,4096]{1,0:T(8,128)(2,1)} %down0_ref.1), channel_id=1, source_target_pairs={{0,1},{1,0},{2,3},{3,2},{4,5},{5,4},{6,7},{7,6},{8,9},{9,8},{10,11... | collective-permute-start | bytes 3145736 | tf_op jit(solution)/shard_map/ppermute | solution.py:310
  49.9 43.2 %copy-start.4 = (s32[32]{0:T(128)S(1)}, s32[32]{0:T(128)}, u32[]{:S(2)}) copy-start(s32[32]{0:T(128)} %param.23) | copy-start | bytes 388
  49.9 43.2 %copy-start.5 = (s32[32]{0:T(128)S(1)}, s32[32]{0:T(128)}, u32[]{:S(2)}) copy-start(s32[32]{0:T(128)} %param.22) | copy-start | bytes 388
  50.0 49.2 %copy-start.7 = (bf16[2048]{0:T(1024)(128)(2,1)S(1)}, bf16[2048]{0:T(1024)(128)(2,1)}, u32[]{:S(2)}) copy-start(bf16[2048]{0:T(1024)(128)(2,1)} %param.26) | copy-start | bytes 12292
  50.0 49.2 %copy-start.6 = (bf16[2048,12]{0,1:T(8,128)(2,1)S(1)}, bf16[2048,12]{0,1:T(8,128)(2,1)}, u32[]{:S(2)}) copy-start(bf16[2048,12]{0,1:T(8,128)(2,1)} %param.27) | copy-start | bytes 147460
  50.0 21.4 %all-to-all-start.1 = ((bf16[32,64,128]{2,1,0:T(8,128)(2,1)}), bf16[32,64,128]{2,1,0:T(8,128)(2,1)S(1)}, u32[]{:S(2)}, u32[]{:S(2)}) async-start(bf16[32,64,128]{2,1,0:T(8,128)(2,1)} %shard_map.147), calls=%async_computation.1 | async-start | bytes 1048576 | tf_op jit(solution)/shard_map/all_to_all | solution.py:319
  54.7 54.5 %copy-start.1 = (bf16[2048,128]{1,0:T(8,128)(2,1)S(1)}, bf16[2048,128]{1,0:T(8,128)(2,1)}, u32[]{:S(2)}) copy-start(bf16[2048,128]{1,0:T(8,128)(2,1)} %cross_u_ref.1) | copy-start | bytes 1572868
  54.7 54.5 %copy-start.2 = (bf16[128,2048]{1,0:T(8,128)(2,1)S(1)}, bf16[128,2048]{1,0:T(8,128)(2,1)}, u32[]{:S(2)}) copy-start(bf16[128,2048]{1,0:T(8,128)(2,1)} %cross_v_ref.1) | copy-start | bytes 1572868
  54.7 44.5 %collective-permute-start.3 = (bf16[3,2048,128]{2,1,0:T(8,128)(2,1)}, bf16[3,2048,128]{2,1,0:T(8,128)(2,1)}, u32[]{:S(2)}, u32[]{:S(2)}) collective-permute-start(bf16[3,2048,128]{2,1,0:T(8,128)(2,1)} %w0_ref.1), channel_id=1, source_target_pairs={{0,1},{1,0},{2,3},{3,2},{4,5},{5,4},{6,7},{7,6},{8,9},{9,8},{10,11... | collective-permute-start | bytes 4718600 | tf_op jit(solution)/shard_map/ppermute | solution.py:310
  56.8 3.7 %collective-permute-start.2 = (bf16[64,2048]{1,0:T(8,128)(2,1)S(1)}, bf16[64,2048]{1,0:T(8,128)(2,1)S(1)}, u32[]{:S(2)}, u32[]{:S(2)}) collective-permute-start(bf16[64,2048]{1,0:T(8,128)(2,1)S(1)} %copy-done.3), channel_id=1, source_target_pairs={{0,1},{1,0},{2,3},{3,2},{4,5},{5,4},{6,7},{7,6},{8,9},{9,8},{10,11... | collective-permute-start | bytes 786440 | tf_op jit(solution)/shard_map/ppermute | solution.py:310
  93.9 15.3 %all-to-all-start.3 = ((f32[64,2,128]{2,1,0:T(2,128)}), f32[64,2,128]{2,1,0:T(2,128)S(1)}, u32[]{:S(2)}, u32[]{:S(2)}) async-start(f32[64,2,128]{2,1,0:T(2,128)} %bitcast.6), calls=%async_computation.3 | async-start | bytes 131072 | tf_op jit(solution)/shard_map/all_to_all | solution.py:336
Sparse Core Ops, SparseCore 0:
  10.5 96.9 all-gather.2

commit v4 on v3

--- a/solution.py
+++ b/solution.py
@@ -108,19 +108,16 @@
         stats = stats + got_ref[chip, 64:72, :].astype(F32)
     inverse = lax.rsqrt((stats[0:1] + stats[1:2]) / D + epsilon)
     column = jnp.broadcast_to(inverse, (128, 128)).T[0:64]
-    total = jnp.zeros((64, 256), F32)
-    for b in range(0, N_CHIPS, 2):
-        left = jnp.concatenate([got_ref[block_of(b), 0:64, :], got_ref[block_of(b + 1), 0:64, :]], axis=1)
-        part = slice(b * 128, b * 128 + 256)
-        right = jnp.concatenate([up0_ref[part, :], up1_ref[part, :]], axis=1)
-        total = total + jnp.dot(left, right, preferred_element_type=F32)
+    left = jnp.concatenate([got_ref[block_of(b), 0:64, :] for b in range(N_CHIPS)], axis=1)
+    total = jnp.concatenate(
+        [jnp.dot(left, up[...], preferred_element_type=F32) for up in (up0_ref, up1_ref)], axis=1
+    )
     hidden = jax.nn.gelu(total * jnp.concatenate([column, column], axis=1)).astype(BF16)
     for copy in copies:
         copy.wait()
-    for b in range(0, N_CHIPS, 2):
-        part = jnp.dot(hidden, down[:, b * 128 : b * 128 + 256], preferred_element_type=F32).astype(BF16)
-        out_ref[block_of(b), :, :] = part[:, 0:128]
-        out_ref[block_of(b + 1), :, :] = part[:, 128:256]
+    part = jnp.dot(hidden, down[...], preferred_element_type=F32).astype(BF16)
+    for b in range(N_CHIPS):
+        out_ref[block_of(b), :, :] = part[:, 128 * b : 128 * b + 128]
 
 
 def values_kernel(got_ref, hist_ref, query_ref, proj0_ref, proj1_ref, out_ref, proj, sems):
@@ -170,7 +167,7 @@
 
 
 SLOTS = 1024
-HALF = 512
+STEP = 256
 
 
 def score_kernel(
@@ -181,18 +178,18 @@
     chip_here = lax.axis_index("z") * 4 + lax.axis_index("xh") * 2 + lax.axis_index("xl")
 
     def piece(i):
-        part = slice(HALF * i, HALF * i + HALF)
+        part = slice(STEP * i, STEP * i + STEP)
         return pltpu.make_async_copy(cand_ref.at[part, :], x.at[part, :], sems.at[i])
 
-    arrivals = [piece(0), piece(1)]
-    get_u = pltpu.make_async_copy(cross_u_ref, cross_u, sems.at[2])
-    get_v = pltpu.make_async_copy(cross_v_ref, cross_v.at[0:128, :], sems.at[3])
+    arrivals = [piece(i) for i in range(4)]
+    get_u = pltpu.make_async_copy(cross_u_ref, cross_u, sems.at[4])
+    get_v = pltpu.make_async_copy(cross_v_ref, cross_v.at[0:128, :], sems.at[5])
     get_w = []
     for k in range(EXPERTS):
         for i, source in enumerate((w0_ref, w1_ref)):
             start = 256 * k + 128 * i
-            get_w.append(pltpu.make_async_copy(source.at[k], w.at[:, start : start + 128], sems.at[4 + 2 * k + i]))
-    for copy in (arrivals[0], get_u, get_v, arrivals[1], *get_w):
+            get_w.append(pltpu.make_async_copy(source.at[k], w.at[:, start : start + 128], sems.at[6 + 2 * k + i]))
+    for copy in (arrivals[0], get_u, get_v, *arrivals[1:], *get_w):
         copy.start()
     row = rows((16, 128))
     low_half = lanes((1, 128)) < 64
@@ -227,24 +224,26 @@
     bias = bias_ref[...].astype(F32)
     cross_v[128:144, :] = jnp.where(row == 0, bias, jnp.where(row == 1, 1.0, 0.0)).astype(BF16)
     cross_v[144:256, :] = jnp.zeros((112, 2048), BF16)
-    ones = jnp.where(lanes((HALF, 128)) < 2, 1.0, 0.0).astype(BF16)
-    row = rows((16, HALF))
-    for i in range(2):
-        part = slice(HALF * i, HALF * i + HALF)
+    ones = jnp.where(lanes((STEP, 128)) < 2, 1.0, 0.0).astype(BF16)
+    row = rows((16, STEP))
+    for i in range(4):
+        part = slice(STEP * i, STEP * i + STEP)
         hot = jnp.where((row % 4).astype(F32) == owners[:, part], 1.0, 0.0).T.astype(BF16)
         arrivals[i].wait()
-        for j in range(4):
-            cols = slice(512 * j, 512 * j + 512)
-            added = jnp.dot(hot, users[:, cols], preferred_element_type=F32)
-            x[part, cols] = (x[part, cols].astype(F32) + added).astype(BF16)
         if i == 0:
             get_u.wait()
-        low = jnp.dot(x[part, :], cross_u[...], preferred_element_type=F32).astype(BF16)
-        left = jnp.concatenate([low, ones], axis=1)
+        low = jnp.zeros((STEP, 128), F32)
+        for j in range(8):
+            cols = slice(256 * j, 256 * j + 256)
+            added = jnp.dot(hot, users[:, cols], preferred_element_type=F32)
+            x0 = (x[part, cols].astype(F32) + added).astype(BF16)
+            x[part, cols] = x0
+            low = low + jnp.dot(x0, cross_u[cols, :], preferred_element_type=F32)
+        left = jnp.concatenate([low.astype(BF16), ones], axis=1)
         if i == 0:
             get_v.wait()
-        for j in range(4):
-            cols = slice(512 * j, 512 * j + 512)
+        for j in range(8):
+            cols = slice(256 * j, 256 * j + 256)
             cross = jnp.dot(left, cross_v[:, cols], preferred_element_type=F32)
             x[part, cols] = (x[part, cols].astype(F32) * cross).astype(BF16)
     own = x[pl.ds(pl.multiple_of(chip_here * 32, 32), 32), :]
@@ -346,7 +345,7 @@
             pltpu.VMEM((2048, 128), BF16),
             pltpu.VMEM((256, 2048), BF16),
             pltpu.VMEM((2048, 768), BF16),
-            pltpu.SemaphoreType.DMA((10,)),
+            pltpu.SemaphoreType.DMA((12,)),
         ],
         compiler_params=params(11700),
     )(users, everyone, task, pair, cross_u, cross_v, cross_bias[None, :], gate_rows, expert_w, swap(expert_w))

time: 145 us -> 144 us (level)
  Pallas kernels: 20.3 us -> 18.6 us
    pallas_call x1, Pallas kernels: 12.2 us -> 10.7 us  [body(): pl.pallas_call(score_kernel, out_shape=(jax.ShapeDtypeStruct((N_CHIPS, 12...]
where the time goes in v4:
time: 144 us; the launch traced here: 143 us
  waiting for transfers between devices  39.8 us (28%)
  blocking collectives  38.7 us (27%)
  starting transfers between devices  31.9 us (22%)
  Pallas kernels  18.6 us (13%)
  between operations  13.6 us (9%)
    all_to_all x1, blocking collectives, body(): values = lax.all_to_all(values, CHIPS, 0, 0, tiled=True)  21.1 us
    all_to_all x1, blocking collectives, body(): back = lax.all_to_all(part, CHIPS, 0, 0, tiled=True)  15.4 us
    all_to_all x1, waiting for transfers between devices, body(): tokens = lax.all_to_all(spread, CHIPS, 0, 0, tiled=True)  14.2 us
    all_to_all x1, starting transfers between devices, body(): tokens = lax.all_to_all(spread, CHIPS, 0, 0, tiled=True)  13.2 us
    all_to_all x1, waiting for transfers between devices, body(): summed = lax.all_to_all(parts, CHIPS, 0, 0, tiled=True)  11.1 us
    pallas_call x1, Pallas kernels, body(): pl.pallas_call(score_kernel, out_shape=(jax.ShapeDtypeStruct((N_CHIPS, 12...  10.7 us
    all_to_all x1, waiting for transfers between devices, body(): users = lax.all_to_all(user, ALL, 0, 0, tiled=True)  9.89 us
    ppermute x4, starting transfers between devices, body(): swap = lambda x: lax.ppermute(x, 'c', [(0, 1), (1, 0)])  8.93 us
  transfers between devices with their start and end apart: 8, of which 6 were waited for; matrix products, arithmetic and copies ran while one was open for 0% of the time, Pallas kernels for 5%

profile of v4, /device:TPU:56, one launch (start us, length us, event | category | flops | bytes accessed | tf_op | source)
XLA Modules:
  0.0 142.6 jit_solution(11974464004633437786)
XLA Ops:
  6.5 0.0 all-gather.3.cloned.1.call-start
  6.5 0.7 all-gather.3.cloned.1.call-update
  7.3 1.5 %shard_map.145 = bf16[160,128]{1,0:T(8,128)(2,1)} custom-call(bf16[64,128]{1,0:T(8,128)(2,1)} %bitcast.24, bf16[1,64]{1,0:T(2,128)(2,1)} %gain_ref.1, bf16[1,64]{1,0:T(2,128)(2,1)} %bitcast.26, bf16[3,4,128]{2,1,0:T(4,128)(2,1)} %bitcast.25), custom_call_target="tpu_custom_call" | custom-call | tf_op jit(solution)/shard_map/pallas_call | solution.py:289
  8.7 0.0 copy-start
  8.7 2.2 %all-gather = bf16[320,128]{1,0:T(8,128)(2,1)S(1)} all-gather(bf16[160,128]{1,0:T(8,128)(2,1)} %shard_map.145), channel_id=2, replica_groups=mesh['grp'=8,'z'=8,'xl'=2,'xh'=2,'c'=2] {'c'}, dimensions={0}, use_global_device_ids=true | all-gather | bytes 122880 | tf_op jit(solution)/shard_map/all_gather | solution.py:296
  10.9 1.1 shard_map.146
  12.0 13.2 %all-to-all-start = ((bf16[32,72,128]{2,1,0:T(8,128)(2,1)}), bf16[32,72,128]{2,1,0:T(8,128)(2,1)S(1)}, u32[]{:S(2)}, u32[]{:S(2)}) async-start(bf16[32,72,128]{2,1,0:T(8,128)(2,1)} %get-tuple-element.10), calls=%async_computation | async-start | bytes 1179648 | tf_op jit(solution)/shard_map/all_to_all | solution.py:308
  25.2 0.0 copy-start.3
  25.2 2.1 %collective-permute-start = (bf16[4096,128]{1,0:T(8,128)(2,1)}, bf16[4096,128]{1,0:T(8,128)(2,1)S(1)}, u32[]{:S(2)}, u32[]{:S(2)}) collective-permute-start(bf16[4096,128]{1,0:T(8,128)(2,1)} %up0_ref.1), channel_id=1, source_target_pairs={{0,1},{1,0},{2,3},{3,2},{4,5},{5,4},{6,7},{7,6},{8,9},{9,8},{10,11... | collective-permute-start | bytes 3145736 | tf_op jit(solution)/shard_map/ppermute | solution.py:309
  27.3 2.4 %collective-permute-start.1 = (bf16[128,4096]{1,0:T(8,128)(2,1)}, bf16[128,4096]{1,0:T(8,128)(2,1)}, u32[]{:S(2)}, u32[]{:S(2)}) collective-permute-start(bf16[128,4096]{1,0:T(8,128)(2,1)} %down0_ref.1), channel_id=1, source_target_pairs={{0,1},{1,0},{2,3},{3,2},{4,5},{5,4},{6,7},{7,6},{8,9},{9,8},{10,11... | collective-permute-start | bytes 3145736 | tf_op jit(solution)/shard_map/ppermute | solution.py:309
  29.7 0.4 collective-permute-done.up1_ref
  30.1 2.2 %collective-permute-done.1.down1_ref = bf16[128,4096]{1,0:T(8,128)(2,1)} collective-permute-done((bf16[128,4096]{1,0:T(8,128)(2,1)}, bf16[128,4096]{1,0:T(8,128)(2,1)}, u32[]{:S(2)}, u32[]{:S(2)}) %collective-permute-start.1) | collective-permute-done | bytes 1048608 | tf_op jit(solution)/shard_map/ppermute | solution.py:309
  32.3 14.2 %all-to-all-done.got_ref = bf16[32,72,128]{2,1,0:T(8,128)(2,1)S(1)} async-done(((bf16[32,72,128]{2,1,0:T(8,128)(2,1)}), bf16[32,72,128]{2,1,0:T(8,128)(2,1)S(1)}, u32[]{:S(2)}, u32[]{:S(2)}) %all-to-all-start) | async-done | bytes 589856 | tf_op jit(solution)/shard_map/all_to_all | solution.py:308
  46.5 0.0 copy-done
  46.5 3.2 %shard_map.147 = bf16[32,64,128]{2,1,0:T(8,128)(2,1)} custom-call(bf16[32,72,128]{2,1,0:T(8,128)(2,1)S(1)} %all-to-all-done.got_ref, bf16[4096,128]{1,0:T(8,128)(2,1)S(1)} %copy-done, bf16[4096,128]{1,0:T(8,128)(2,1)S(1)} %collective-permute-done.up1_ref, bf16[128,4096]{1,0:T(8,128)(2,1)} %down0_ref.1, bf16[128,4096]{1,0:T(8,128)(2,1)} %collective-permute-done.1.down1_ref), custom_call_target="tpu_custom_call" | custom-call | tf_op jit(solution)/shard_map/pallas_call | solution.py:310
  49.7 0.0 copy-start.4
  49.7 0.0 copy-start.5
  49.8 0.0 copy-start.7
  49.8 0.0 copy-start.6
  49.8 4.7 %all-to-all-start.1 = ((bf16[32,64,128]{2,1,0:T(8,128)(2,1)}), bf16[32,64,128]{2,1,0:T(8,128)(2,1)S(1)}, u32[]{:S(2)}, u32[]{:S(2)}) async-start(bf16[32,64,128]{2,1,0:T(8,128)(2,1)} %shard_map.147), calls=%async_computation.1 | async-start | bytes 1048576 | tf_op jit(solution)/shard_map/all_to_all | solution.py:318
  54.5 0.0 copy-start.1
  54.5 0.0 copy-start.2
  54.5 2.1 %collective-permute-start.3 = (bf16[3,2048,128]{2,1,0:T(8,128)(2,1)}, bf16[3,2048,128]{2,1,0:T(8,128)(2,1)}, u32[]{:S(2)}, u32[]{:S(2)}) collective-permute-start(bf16[3,2048,128]{2,1,0:T(8,128)(2,1)} %w0_ref.1), channel_id=1, source_target_pairs={{0,1},{1,0},{2,3},{3,2},{4,5},{5,4},{6,7},{7,6},{8,9},{9,8},{10,11... | collective-permute-start | bytes 4718600 | tf_op jit(solution)/shard_map/ppermute | solution.py:309
  56.5 0.0 copy-done.3
  56.6 2.4 %collective-permute-start.2 = (bf16[64,2048]{1,0:T(8,128)(2,1)S(1)}, bf16[64,2048]{1,0:T(8,128)(2,1)S(1)}, u32[]{:S(2)}, u32[]{:S(2)}) collective-permute-start(bf16[64,2048]{1,0:T(8,128)(2,1)S(1)} %copy-done.3), channel_id=1, source_target_pairs={{0,1},{1,0},{2,3},{3,2},{4,5},{5,4},{6,7},{7,6},{8,9},{9,8},{10,11... | collective-permute-start | bytes 786440 | tf_op jit(solution)/shard_map/ppermute | solution.py:309
  59.0 1.3 collective-permute-done.2.proj1_ref
  60.3 11.1 %all-to-all-done.1.got_ref = bf16[32,64,128]{2,1,0:T(8,128)(2,1)S(1)} async-done(((bf16[32,64,128]{2,1,0:T(8,128)(2,1)}), bf16[32,64,128]{2,1,0:T(8,128)(2,1)S(1)}, u32[]{:S(2)}, u32[]{:S(2)}) %all-to-all-start.1) | async-done | bytes 524320 | tf_op jit(solution)/shard_map/all_to_all | solution.py:318
  71.4 0.7 shard_map.148
  72.1 21.1 %all_to_all.37.got_ref = bf16[32,40,128]{2,1,0:T(8,128)(2,1)S(1)} all-to-all(bf16[32,40,128]{2,1,0:T(8,128)(2,1)S(1)} %shard_map.148), channel_id=1, replica_groups=mesh['grp'=8,'z'=8,'xl'=2,'xh'=2,'c'=2] {'z','xh','xl'}, dimensions={0} | all-to-all | bytes 655360 | tf_op jit(solution)/shard_map/all_to_all | solution.py:327
  93.2 0.0 copy-done.4
  93.2 0.0 copy-done.5
  93.2 0.8 shard_map.149
  94.0 5.2 %all-to-all-start.3 = ((f32[64,2,128]{2,1,0:T(2,128)}), f32[64,2,128]{2,1,0:T(2,128)S(1)}, u32[]{:S(2)}, u32[]{:S(2)}) async-start(f32[64,2,128]{2,1,0:T(2,128)} %bitcast.6), calls=%async_computation.3 | async-start | bytes 131072 | tf_op jit(solution)/shard_map/all_to_all | solution.py:335
  99.1 0.0 copy-done.7
  99.2 0.0 copy-done.6
  99.2 0.0 collective-permute-done.3.w1_ref
  99.2 9.9 %all-to-all-done.3 = f32[64,2,128]{2,1,0:T(2,128)S(1)} async-done(((f32[64,2,128]{2,1,0:T(2,128)}), f32[64,2,128]{2,1,0:T(2,128)S(1)}, u32[]{:S(2)}, u32[]{:S(2)}) %all-to-all-start.3) | async-done | bytes 65568 | tf_op jit(solution)/shard_map/all_to_all | solution.py:335
  109.1 0.0 all-gather.3.cloned.1.call-done.cand_ref
  109.1 0.0 copy-done.1
  109.1 0.0 copy-done.2
  109.1 10.7 %shard_map.150 = (f32[32,128]{1,0:T(8,128)S(1)}, f32[1,128]{1,0:T(1,128)S(1)}) custom-call(f32[128,128]{1,0:T(8,128)S(1)} %bitcast.16, bf16[1024,2048]{1,0:T(8,128)(2,1)} %all-gather.3.cloned.1.call-done.cand_ref, s32[1,32]{1,0:T(1,128)S(1)} %bitcast.20, bf16[2,160,128]{2,1,0:T(8,128)(2,1)S(1)} %bitcast.15, bf16[2048,128]{1,0:T(8,128)(2,1)S(1)} %copy-done.1, ...), custom_call_target="tpu_custom_call" | custom-call | tf_op jit(solution)/shard_map/pallas_call | solution.py:337
  119.8 15.4 %all_to_all.38 = f32[32,1,128]{2,1,0:T(1,128)S(1)} all-to-all(f32[32,1,128]{2,1,0:T(1,128)S(1)} %bitcast.18), channel_id=1, replica_groups=mesh['grp'=8,'z'=8,'xl'=2,'xh'=2,'c'=2] {'z','xh','xl'}, dimensions={0} | all-to-all | bytes 32768 | tf_op jit(solution)/shard_map/all_to_all | solution.py:352
  135.1 0.7 shard_map.151
  (2 shorter events, 0.0 us)
Async XLA Ops:
  6.5 102.6 %all-gather.3.cloned.1.call-start = ((), (), s32[]{:S(2)}) async-start(), calls=%async_computation.5 | async-start | bytes 4325376 | tf_op jit(solution)/shard_map/all_gather | solution.py:288
  8.7 37.8 %copy-start = (bf16[4096,128]{1,0:T(8,128)(2,1)S(1)}, bf16[4096,128]{1,0:T(8,128)(2,1)}, u32[]{:S(2)}) copy-start(bf16[4096,128]{1,0:T(8,128)(2,1)} %up0_ref.1) | copy-start | bytes 3145732
  12.0 34.5 %all-to-all-start = ((bf16[32,72,128]{2,1,0:T(8,128)(2,1)}), bf16[32,72,128]{2,1,0:T(8,128)(2,1)S(1)}, u32[]{:S(2)}, u32[]{:S(2)}) async-start(bf16[32,72,128]{2,1,0:T(8,128)(2,1)} %get-tuple-element.10), calls=%async_computation | async-start | bytes 1179648 | tf_op jit(solution)/shard_map/all_to_all | solution.py:308
  25.2 31.4 %copy-start.3 = (bf16[64,2048]{1,0:T(8,128)(2,1)S(1)}, bf16[64,2048]{1,0:T(8,128)(2,1)}, u32[]{:S(2)}) copy-start(bf16[64,2048]{1,0:T(8,128)(2,1)} %proj0_ref.1) | copy-start | bytes 786436
  25.2 4.9 %collective-permute-start = (bf16[4096,128]{1,0:T(8,128)(2,1)}, bf16[4096,128]{1,0:T(8,128)(2,1)S(1)}, u32[]{:S(2)}, u32[]{:S(2)}) collective-permute-start(bf16[4096,128]{1,0:T(8,128)(2,1)} %up0_ref.1), channel_id=1, source_target_pairs={{0,1},{1,0},{2,3},{3,2},{4,5},{5,4},{6,7},{7,6},{8,9},{9,8},{10,11... | collective-permute-start | bytes 3145736 | tf_op jit(solution)/shard_map/ppermute | solution.py:309
  27.3 5.0 %collective-permute-start.1 = (bf16[128,4096]{1,0:T(8,128)(2,1)}, bf16[128,4096]{1,0:T(8,128)(2,1)}, u32[]{:S(2)}, u32[]{:S(2)}) collective-permute-start(bf16[128,4096]{1,0:T(8,128)(2,1)} %down0_ref.1), channel_id=1, source_target_pairs={{0,1},{1,0},{2,3},{3,2},{4,5},{5,4},{6,7},{7,6},{8,9},{9,8},{10,11... | collective-permute-start | bytes 3145736 | tf_op jit(solution)/shard_map/ppermute | solution.py:309
  49.7 43.5 %copy-start.4 = (s32[32]{0:T(128)S(1)}, s32[32]{0:T(128)}, u32[]{:S(2)}) copy-start(s32[32]{0:T(128)} %param.23) | copy-start | bytes 388
  49.7 43.5 %copy-start.5 = (s32[32]{0:T(128)S(1)}, s32[32]{0:T(128)}, u32[]{:S(2)}) copy-start(s32[32]{0:T(128)} %param.22) | copy-start | bytes 388
  49.8 49.4 %copy-start.7 = (bf16[2048]{0:T(1024)(128)(2,1)S(1)}, bf16[2048]{0:T(1024)(128)(2,1)}, u32[]{:S(2)}) copy-start(bf16[2048]{0:T(1024)(128)(2,1)} %param.26) | copy-start | bytes 12292
  49.8 49.4 %copy-start.6 = (bf16[2048,12]{0,1:T(8,128)(2,1)S(1)}, bf16[2048,12]{0,1:T(8,128)(2,1)}, u32[]{:S(2)}) copy-start(bf16[2048,12]{0,1:T(8,128)(2,1)} %param.27) | copy-start | bytes 147460
  49.8 21.6 %all-to-all-start.1 = ((bf16[32,64,128]{2,1,0:T(8,128)(2,1)}), bf16[32,64,128]{2,1,0:T(8,128)(2,1)S(1)}, u32[]{:S(2)}, u32[]{:S(2)}) async-start(bf16[32,64,128]{2,1,0:T(8,128)(2,1)} %shard_map.147), calls=%async_computation.1 | async-start | bytes 1048576 | tf_op jit(solution)/shard_map/all_to_all | solution.py:318
  54.5 54.6 %copy-start.1 = (bf16[2048,128]{1,0:T(8,128)(2,1)S(1)}, bf16[2048,128]{1,0:T(8,128)(2,1)}, u32[]{:S(2)}) copy-start(bf16[2048,128]{1,0:T(8,128)(2,1)} %cross_u_ref.1) | copy-start | bytes 1572868
  54.5 54.6 %copy-start.2 = (bf16[128,2048]{1,0:T(8,128)(2,1)S(1)}, bf16[128,2048]{1,0:T(8,128)(2,1)}, u32[]{:S(2)}) copy-start(bf16[128,2048]{1,0:T(8,128)(2,1)} %cross_v_ref.1) | copy-start | bytes 1572868
  54.5 44.7 %collective-permute-start.3 = (bf16[3,2048,128]{2,1,0:T(8,128)(2,1)}, bf16[3,2048,128]{2,1,0:T(8,128)(2,1)}, u32[]{:S(2)}, u32[]{:S(2)}) collective-permute-start(bf16[3,2048,128]{2,1,0:T(8,128)(2,1)} %w0_ref.1), channel_id=1, source_target_pairs={{0,1},{1,0},{2,3},{3,2},{4,5},{5,4},{6,7},{7,6},{8,9},{9,8},{10,11... | collective-permute-start | bytes 4718600 | tf_op jit(solution)/shard_map/ppermute | solution.py:309
  56.6 3.7 %collective-permute-start.2 = (bf16[64,2048]{1,0:T(8,128)(2,1)S(1)}, bf16[64,2048]{1,0:T(8,128)(2,1)S(1)}, u32[]{:S(2)}, u32[]{:S(2)}) collective-permute-start(bf16[64,2048]{1,0:T(8,128)(2,1)S(1)} %copy-done.3), channel_id=1, source_target_pairs={{0,1},{1,0},{2,3},{3,2},{4,5},{5,4},{6,7},{7,6},{8,9},{9,8},{10,11... | collective-permute-start | bytes 786440 | tf_op jit(solution)/shard_map/ppermute | solution.py:309
  94.0 15.1 %all-to-all-start.3 = ((f32[64,2,128]{2,1,0:T(2,128)}), f32[64,2,128]{2,1,0:T(2,128)S(1)}, u32[]{:S(2)}, u32[]{:S(2)}) async-start(f32[64,2,128]{2,1,0:T(2,128)} %bitcast.6), calls=%async_computation.3 | async-start | bytes 131072 | tf_op jit(solution)/shard_map/all_to_all | solution.py:335
Sparse Core Ops, SparseCore 0:
  10.5 96.8 all-gather.2

commit v5 on v4

--- a/solution.py
+++ b/solution.py
@@ -14,8 +14,9 @@
 HIST = 32
 epsilon = 1e-05
 
-CHIPS = ("z", "xh", "xl")
-ALL = ("z", "xh", "xl", "c")
+CHIPS = ("zh", "zl", "xh", "xl")
+ALL = ("zh", "zl", "xh", "xl", "c")
+HOLDERS = ("zh", "xh", "xl")
 N_CHIPS = 32
 F32 = jnp.float32
 BF16 = jnp.bfloat16
@@ -166,29 +167,30 @@
     out_ref[...] = jnp.where(rows((128, 128)) % 2 == 0, user, slots)
 
 
-SLOTS = 1024
+SLOTS = 512
 STEP = 256
 
 
 def score_kernel(
-    got_ref, cand_ref, own_task_ref, pair_ref, cross_u_ref, cross_v_ref, bias_ref, gate_ref, w0_ref, w1_ref,
-    out_ref, gates_ref, users, x, cross_u, cross_v, w, sems,
+    got_ref, cand_ref, own_task_ref, pair_ref, near_ref, cross_u_ref, cross_v_ref, bias_ref, gate_ref, w0_ref, w1_ref,
+    w2_ref, w3_ref, out_ref, gates_ref, users, x, cross_u, cross_v, w, sems,
 ):
     core = lax.axis_index("c")
-    chip_here = lax.axis_index("z") * 4 + lax.axis_index("xh") * 2 + lax.axis_index("xl")
+    zl = lax.axis_index("zl")
+    place = lax.axis_index("zh") * 4 + lax.axis_index("xh") * 2 + lax.axis_index("xl")
 
     def piece(i):
         part = slice(STEP * i, STEP * i + STEP)
         return pltpu.make_async_copy(cand_ref.at[part, :], x.at[part, :], sems.at[i])
 
-    arrivals = [piece(i) for i in range(4)]
+    arrivals = [piece(i) for i in range(2)]
     get_u = pltpu.make_async_copy(cross_u_ref, cross_u, sems.at[4])
     get_v = pltpu.make_async_copy(cross_v_ref, cross_v.at[0:128, :], sems.at[5])
     get_w = []
     for k in range(EXPERTS):
-        for i, source in enumerate((w0_ref, w1_ref)):
-            start = 256 * k + 128 * i
-            get_w.append(pltpu.make_async_copy(source.at[k], w.at[:, start : start + 128], sems.at[6 + 2 * k + i]))
+        for i, source in enumerate((w0_ref, w1_ref, w2_ref, w3_ref)):
+            start = 512 * k + 128 * i
+            get_w.append(pltpu.make_async_copy(source.at[k], w.at[:, start : start + 128], sems.at[6 + 4 * k + i]))
     for copy in (arrivals[0], get_u, get_v, *arrivals[1:], *get_w):
         copy.start()
     row = rows((16, 128))
@@ -207,11 +209,11 @@
         ).astype(BF16)
     quarter = lanes((1, 128)) // 32
     owners, tasks = [], []
-    for b in range(8):
+    for b in range(4):
         owner = jnp.zeros((1, 128), F32)
         task = jnp.zeros((1, 128), F32)
         for q in range(4):
-            slots = got_ref[pl.ds(4 * (4 * b + q) + 2 * core + 1, 1), :]
+            slots = got_ref[pl.ds(4 * (8 * b + 4 * zl + q) + 2 * core + 1, 1), :]
             turned = turn(slots, 32)
             owner = jnp.where(quarter == q, (slots, turned)[q % 2], owner)
             task = jnp.where(quarter == q, (turned, slots)[q % 2], task)
@@ -219,14 +221,16 @@
         tasks.append(task)
     owners = jnp.concatenate(owners, axis=1)
     tasks = jnp.concatenate(tasks, axis=1)
-    heads = jnp.concatenate([pair_ref[core, 144:160, :], pair_ref[1 - core, 144:160, :]], axis=1)
+    heads = jnp.concatenate(
+        [ref[which, 144:160, :] for ref in (pair_ref, near_ref) for which in (core, 1 - core)], axis=1
+    )
     row = rows((16, 2048))
     bias = bias_ref[...].astype(F32)
     cross_v[128:144, :] = jnp.where(row == 0, bias, jnp.where(row == 1, 1.0, 0.0)).astype(BF16)
     cross_v[144:256, :] = jnp.zeros((112, 2048), BF16)
     ones = jnp.where(lanes((STEP, 128)) < 2, 1.0, 0.0).astype(BF16)
     row = rows((16, STEP))
-    for i in range(4):
+    for i in range(2):
         part = slice(STEP * i, STEP * i + STEP)
         hot = jnp.where((row % 4).astype(F32) == owners[:, part], 1.0, 0.0).T.astype(BF16)
         arrivals[i].wait()
@@ -246,7 +250,7 @@
             cols = slice(256 * j, 256 * j + 256)
             cross = jnp.dot(left, cross_v[:, cols], preferred_element_type=F32)
             x[part, cols] = (x[part, cols].astype(F32) * cross).astype(BF16)
-    own = x[pl.ds(pl.multiple_of(chip_here * 32, 32), 32), :]
+    own = x[pl.ds(pl.multiple_of(place * 32, 32), 32), :]
     logits = lax.dot_general(gate_ref[...], own, ROW_BY_ROW, preferred_element_type=F32)
     row = rows((16, 32))
     picked = jnp.where(row // EXPERTS == own_task_ref[...], jax.nn.sigmoid(logits), 0.0)
@@ -256,15 +260,16 @@
         gate = widen(jnp.sum(jnp.where(row % EXPERTS == k, gates, 0.0), axis=0, keepdims=True))
         row_of = row_of + (gate if k == 0 else turn(gate, 32 * k))
     gates_ref[...] = row_of
-    for copy in get_w:
-        copy.wait()
-    active = jax.nn.relu(jnp.dot(x[...], w[...], preferred_element_type=F32)).astype(BF16)
     row = rows((16, SLOTS)).astype(F32)
     outs = []
     for k in range(EXPERTS):
-        terms = lax.dot_general(heads, active[:, 256 * k : 256 * k + 256], ROW_BY_ROW, preferred_element_type=F32)
+        for copy in get_w[4 * k : 4 * k + 4]:
+            copy.wait()
+        active = jnp.dot(x[...], w[:, 512 * k : 512 * k + 512], preferred_element_type=F32)
+        active = jax.nn.relu(active).astype(BF16)
+        terms = lax.dot_general(heads, active, ROW_BY_ROW, preferred_element_type=F32)
         outs.append(jnp.sum(jnp.where(row == tasks * EXPERTS + k, terms, 0.0), axis=0, keepdims=True))
-    for b in range(8):
+    for b in range(4):
         stack = jnp.concatenate([o[:, 128 * b : 128 * b + 128] for o in outs] + [jnp.zeros((5, 128), F32)], axis=0)
         turns = [stack] + [pltpu.roll(stack, 32 * q, 1) for q in range(1, 4)]
         for q in range(4):
@@ -285,7 +290,7 @@
     hist, tower_gain, up_w, down_w, query, proj_w, cand, owner, task, cross_u, cross_v, cross_bias, gate_w, expert_w, head_w,
 ):
     owner, task = owner[None, :], task[None, :]
-    everyone = lax.all_gather(cand, CHIPS, axis=0, tiled=True)
+    everyone = lax.all_gather(cand, HOLDERS, axis=0, tiled=True)
     message = pl.pallas_call(
         pack_kernel,
         out_shape=jax.ShapeDtypeStruct((160, 128), BF16),
@@ -333,23 +338,28 @@
         compiler_params=params(12288),
     )(values, owner, task)
     users = lax.all_to_all(user, ALL, 0, 0, tiled=True)
+    near = lambda x: lax.ppermute(x, "zl", [(0, 1), (1, 0)])
+    expert_near = near(expert_w)
     gate_rows = jnp.pad(gate_w.T, ((0, 4), (0, 0)))
     part, gates = pl.pallas_call(
         score_kernel,
-        out_shape=(jax.ShapeDtypeStruct((N_CHIPS, 128), F32), jax.ShapeDtypeStruct((1, 128), F32)),
-        in_specs=[VMEM, HBM, VMEM, VMEM, HBM, HBM, VMEM, VMEM, HBM, HBM],
+        out_shape=(jax.ShapeDtypeStruct((16, 128), F32), jax.ShapeDtypeStruct((1, 128), F32)),
+        in_specs=[VMEM, HBM, VMEM, VMEM, VMEM, HBM, HBM, VMEM, VMEM, HBM, HBM, HBM, HBM],
         out_specs=(VMEM,) * 2,
         scratch_shapes=[
             pltpu.VMEM((16, 2048), BF16),
             pltpu.VMEM((SLOTS, 2048), BF16),
             pltpu.VMEM((2048, 128), BF16),
             pltpu.VMEM((256, 2048), BF16),
-            pltpu.VMEM((2048, 768), BF16),
-            pltpu.SemaphoreType.DMA((12,)),
+            pltpu.VMEM((2048, 1536), BF16),
+            pltpu.SemaphoreType.DMA((18,)),
         ],
-        compiler_params=params(11700),
-    )(users, everyone, task, pair, cross_u, cross_v, cross_bias[None, :], gate_rows, expert_w, swap(expert_w))
-    back = lax.all_to_all(part, CHIPS, 0, 0, tiled=True)
+        compiler_params=params(11900),
+    )(
+        users, everyone, task, pair, near(pair), cross_u, cross_v, cross_bias[None, :], gate_rows,
+        expert_w, swap(expert_w), expert_near, swap(expert_near),
+    )
+    back = lax.all_to_all(part, HOLDERS, 0, 0, tiled=True)
     score = pl.pallas_call(
         home_kernel,
         out_shape=jax.ShapeDtypeStruct((1, 32), F32),
@@ -361,8 +371,8 @@
 
 
 def solution(mesh):
-    fine = Mesh(mesh.devices.reshape(mesh.devices.shape[0], 8, 2, 2, 2), ("grp", "z", "xl", "xh", "c"))
-    t = ("z", "xl", "xh", "c")
+    fine = Mesh(mesh.devices.reshape(mesh.devices.shape[0], 4, 2, 2, 2, 2), ("grp", "zh", "zl", "xl", "xh", "c"))
+    t = ("zh", "zl", "xl", "xh", "c")
     in_specs = (
         P("grp", t),
         P(None, t),

time: 144 us -> 176 us (1.22)
  waiting for transfers between devices: 39.8 us -> 66.4 us
  starting transfers between devices: 31.9 us -> 42.4 us
  blocking collectives: 38.7 us -> 36.1 us
  Pallas kernels: 18.6 us -> 16.6 us
    all_to_all x1, waiting for transfers between devices: 14.2 us -> 49.1 us  [body(): tokens = lax.all_to_all(spread, CHIPS, 0, 0, tiled=True)]
    ppermute x0 -> x2, starting transfers between devices: none -> 7.75 us  [body(): near = lambda x: lax.ppermute(x, 'zl', [(0, 1), (1, 0)])]
    all_to_all x1, waiting for transfers between devices: 9.89 us -> 3.43 us  [body(): users = lax.all_to_all(user, ALL, 0, 0, tiled=True)]
    all_to_all x1, waiting for transfers between devices: 11.1 us -> 5.93 us  [body(): summed = lax.all_to_all(parts, CHIPS, 0, 0, tiled=True)]
    ppermute x0 -> x2, waiting for transfers between devices: none -> 2.98 us  [body(): near = lambda x: lax.ppermute(x, 'zl', [(0, 1), (1, 0)])]
    all_to_all x1, blocking collectives: 21.1 us -> 18.2 us  [body(): values = lax.all_to_all(values, CHIPS, 0, 0, tiled=True)]
    all_to_all x1, starting transfers between devices: 4.68 us -> 6.95 us  [body(): summed = lax.all_to_all(parts, CHIPS, 0, 0, tiled=True)]
    pallas_call x1, Pallas kernels: 10.7 us -> 8.66 us  [body(): pl.pallas_call(score_kernel, out_shape=(jax.ShapeDtypeStruct((16, 128), F...]
  transfers between devices with their start and end apart: 8 -> 11, of which waited for: 6 -> 7; matrix products, arithmetic and copies ran while one was open for 0% -> 0% of each run, Pallas kernels for 5% -> 4%
where the time goes in v5:
time: 176 us; the launch traced here: 175 us
  waiting for transfers between devices  66.4 us (38%)
  starting transfers between devices  42.4 us (24%)
  blocking collectives  36.1 us (21%)
  Pallas kernels  16.6 us (9%)
  between operations  13.6 us (8%)
    all_to_all x1, waiting for transfers between devices, body(): tokens = lax.all_to_all(spread, CHIPS, 0, 0, tiled=True)  49.1 us
    all_to_all x1, blocking collectives, body(): values = lax.all_to_all(values, CHIPS, 0, 0, tiled=True)  18.2 us
    all_to_all x1, blocking collectives, body(): back = lax.all_to_all(part, HOLDERS, 0, 0, tiled=True)  15.7 us
    all_to_all x1, starting transfers between devices, body(): tokens = lax.all_to_all(spread, CHIPS, 0, 0, tiled=True)  12.3 us
    ppermute x5, starting transfers between devices, body(): swap = lambda x: lax.ppermute(x, 'c', [(0, 1), (1, 0)])  10.8 us
    pallas_call x1, Pallas kernels, body(): pl.pallas_call(score_kernel, out_shape=(jax.ShapeDtypeStruct((16, 128), F...  8.66 us
    ppermute x2, starting transfers between devices, body(): near = lambda x: lax.ppermute(x, 'zl', [(0, 1), (1, 0)])  7.75 us
    all_to_all x1, starting transfers between devices, body(): summed = lax.all_to_all(parts, CHIPS, 0, 0, tiled=True)  6.95 us
  transfers between devices with their start and end apart: 11, of which 7 were waited for; matrix products, arithmetic and copies ran while one was open for 0% of the time, Pallas kernels for 4%

profile of v5, /device:TPU:56, one launch (start us, length us, event | category | flops | bytes accessed | tf_op | source)
XLA Modules:
  0.0 175.1 jit_solution(16996894127578285098)
XLA Ops:
  6.5 0.0 all-gather.3.cloned.1.call-start
  6.5 0.7 all-gather.3.cloned.1.call-update
  7.3 4.3 %collective-permute-start.5 = (bf16[3,2048,128]{2,1,0:T(8,128)(2,1)}, bf16[3,2048,128]{2,1,0:T(8,128)(2,1)}, u32[]{:S(2)}, u32[]{:S(2)}) collective-permute-start(bf16[3,2048,128]{2,1,0:T(8,128)(2,1)} %w0_ref.1), channel_id=1, source_target_pairs={{0,8},{8,0},{1,9},{9,1},{2,10},{10,2},{3,11},{11,3},{4,12},{12,4},... | collective-permute-start | bytes 4718600 | tf_op jit(solution)/shard_map/ppermute | solution.py:341
  11.5 1.5 shard_map.145
  13.0 0.0 copy-start
  13.0 2.2 %all-gather = bf16[320,128]{1,0:T(8,128)(2,1)S(1)} all-gather(bf16[160,128]{1,0:T(8,128)(2,1)} %shard_map.145), channel_id=2, replica_groups=mesh['grp'=8,'zh'=4,'zl'=2,'xl'=2,'xh'=2,'c'=2] {'c'}, dimensions={0}, use_global_device_ids=true | all-gather | bytes 122880 | tf_op jit(solution)/shard_map/all_gather | solution.py:301
  15.2 1.1 shard_map.146
  16.3 12.3 %all-to-all-start = ((bf16[32,72,128]{2,1,0:T(8,128)(2,1)}), bf16[32,72,128]{2,1,0:T(8,128)(2,1)S(1)}, u32[]{:S(2)}, u32[]{:S(2)}) async-start(bf16[32,72,128]{2,1,0:T(8,128)(2,1)} %get-tuple-element.10), calls=%async_computation | async-start | bytes 1179648 | tf_op jit(solution)/shard_map/all_to_all | solution.py:313
  28.6 0.0 copy-start.3
  28.6 2.1 %collective-permute-start = (bf16[4096,128]{1,0:T(8,128)(2,1)}, bf16[4096,128]{1,0:T(8,128)(2,1)S(1)}, u32[]{:S(2)}, u32[]{:S(2)}) collective-permute-start(bf16[4096,128]{1,0:T(8,128)(2,1)} %up0_ref.1), channel_id=1, source_target_pairs={{0,1},{1,0},{2,3},{3,2},{4,5},{5,4},{6,7},{7,6},{8,9},{9,8},{10,11... | collective-permute-start | bytes 3145736 | tf_op jit(solution)/shard_map/ppermute | solution.py:314
  30.6 2.4 %collective-permute-start.1 = (bf16[128,4096]{1,0:T(8,128)(2,1)}, bf16[128,4096]{1,0:T(8,128)(2,1)}, u32[]{:S(2)}, u32[]{:S(2)}) collective-permute-start(bf16[128,4096]{1,0:T(8,128)(2,1)} %down0_ref.1), channel_id=1, source_target_pairs={{0,1},{1,0},{2,3},{3,2},{4,5},{5,4},{6,7},{7,6},{8,9},{9,8},{10,11... | collective-permute-start | bytes 3145736 | tf_op jit(solution)/shard_map/ppermute | solution.py:314
  33.1 0.4 collective-permute-done.up1_ref
  33.5 2.2 %collective-permute-done.1.down1_ref = bf16[128,4096]{1,0:T(8,128)(2,1)} collective-permute-done((bf16[128,4096]{1,0:T(8,128)(2,1)}, bf16[128,4096]{1,0:T(8,128)(2,1)}, u32[]{:S(2)}, u32[]{:S(2)}) %collective-permute-start.1) | collective-permute-done | bytes 1048608 | tf_op jit(solution)/shard_map/ppermute | solution.py:314
  35.7 49.1 %all-to-all-done.got_ref = bf16[32,72,128]{2,1,0:T(8,128)(2,1)S(1)} async-done(((bf16[32,72,128]{2,1,0:T(8,128)(2,1)}), bf16[32,72,128]{2,1,0:T(8,128)(2,1)S(1)}, u32[]{:S(2)}, u32[]{:S(2)}) %all-to-all-start) | async-done | bytes 589856 | tf_op jit(solution)/shard_map/all_to_all | solution.py:313
  84.7 0.0 copy-done
  84.7 3.3 %shard_map.147 = bf16[32,64,128]{2,1,0:T(8,128)(2,1)} custom-call(bf16[32,72,128]{2,1,0:T(8,128)(2,1)S(1)} %all-to-all-done.got_ref, bf16[4096,128]{1,0:T(8,128)(2,1)S(1)} %copy-done, bf16[4096,128]{1,0:T(8,128)(2,1)S(1)} %collective-permute-done.up1_ref, bf16[128,4096]{1,0:T(8,128)(2,1)} %down0_ref.1, bf16[128,4096]{1,0:T(8,128)(2,1)} %collective-permute-done.1.down1_ref), custom_call_target="tpu_custom_call" | custom-call | tf_op jit(solution)/shard_map/pallas_call | solution.py:315
  88.0 0.0 copy-start.4
  88.0 0.0 copy-start.5
  88.0 0.0 copy-start.7
  88.0 0.0 copy-start.6
  88.0 7.0 %all-to-all-start.1 = ((bf16[32,64,128]{2,1,0:T(8,128)(2,1)}), bf16[32,64,128]{2,1,0:T(8,128)(2,1)S(1)}, u32[]{:S(2)}, u32[]{:S(2)}) async-start(bf16[32,64,128]{2,1,0:T(8,128)(2,1)} %shard_map.147), calls=%async_computation.1 | async-start | bytes 1048576 | tf_op jit(solution)/shard_map/all_to_all | solution.py:323
  95.0 0.0 copy-start.1
  95.0 0.0 copy-start.2
  95.0 2.1 %collective-permute-start.4 = (bf16[3,2048,128]{2,1,0:T(8,128)(2,1)}, bf16[3,2048,128]{2,1,0:T(8,128)(2,1)}, u32[]{:S(2)}, u32[]{:S(2)}) collective-permute-start(bf16[3,2048,128]{2,1,0:T(8,128)(2,1)} %w0_ref.1), channel_id=1, source_target_pairs={{0,1},{1,0},{2,3},{3,2},{4,5},{5,4},{6,7},{7,6},{8,9},{9,8},{10,11... | collective-permute-start | bytes 4718600 | tf_op jit(solution)/shard_map/ppermute | solution.py:314
  97.1 0.0 collective-permute-done.5.w2_ref
  97.1 2.4 %collective-permute-start.6 = (bf16[3,2048,128]{2,1,0:T(8,128)(2,1)}, bf16[3,2048,128]{2,1,0:T(8,128)(2,1)}, u32[]{:S(2)}, u32[]{:S(2)}) collective-permute-start(bf16[3,2048,128]{2,1,0:T(8,128)(2,1)} %collective-permute-done.5.w2_ref), channel_id=1, source_target_pairs={{0,1},{1,0},{2,3},{3,2},{4,5},{5,4},{6,7},{7,6},{8,9},{9,8},{10,11... | collective-permute-start | bytes 4718600 | tf_op jit(solution)/shard_map/ppermute | solution.py:314
  99.5 0.0 copy-done.3
  99.5 1.9 %collective-permute-start.2 = (bf16[64,2048]{1,0:T(8,128)(2,1)S(1)}, bf16[64,2048]{1,0:T(8,128)(2,1)S(1)}, u32[]{:S(2)}, u32[]{:S(2)}) collective-permute-start(bf16[64,2048]{1,0:T(8,128)(2,1)S(1)} %copy-done.3), channel_id=1, source_target_pairs={{0,1},{1,0},{2,3},{3,2},{4,5},{5,4},{6,7},{7,6},{8,9},{9,8},{10,11... | collective-permute-start | bytes 786440 | tf_op jit(solution)/shard_map/ppermute | solution.py:314
  101.5 1.6 collective-permute-done.2.proj1_ref
  103.1 5.9 %all-to-all-done.1.got_ref = bf16[32,64,128]{2,1,0:T(8,128)(2,1)S(1)} async-done(((bf16[32,64,128]{2,1,0:T(8,128)(2,1)}), bf16[32,64,128]{2,1,0:T(8,128)(2,1)S(1)}, u32[]{:S(2)}, u32[]{:S(2)}) %all-to-all-start.1) | async-done | bytes 524320 | tf_op jit(solution)/shard_map/all_to_all | solution.py:323
  109.0 0.7 shard_map.148
  109.7 18.2 %all_to_all.37.got_ref = bf16[32,40,128]{2,1,0:T(8,128)(2,1)S(1)} all-to-all(bf16[32,40,128]{2,1,0:T(8,128)(2,1)S(1)} %shard_map.148), channel_id=1, replica_groups=mesh['grp'=8,'zh'=4,'zl'=2,'xl'=2,'xh'=2,'c'=2] {'zh','zl','xh','xl'}, dimensions={0} | all-to-all | bytes 655360 | tf_op jit(solution)/shard_map/all_to_all | solution.py:332
  128.0 0.0 copy-done.4
  128.0 0.0 copy-done.5
  128.0 0.8 shard_map.149
  128.8 4.6 %all-to-all-start.3 = ((f32[64,2,128]{2,1,0:T(2,128)}), f32[64,2,128]{2,1,0:T(2,128)S(1)}, u32[]{:S(2)}, u32[]{:S(2)}) async-start(f32[64,2,128]{2,1,0:T(2,128)} %bitcast.6), calls=%async_computation.3 | async-start | bytes 131072 | tf_op jit(solution)/shard_map/all_to_all | solution.py:340
  133.3 3.5 %collective-permute-start.3 = (bf16[2,160,128]{2,1,0:T(8,128)(2,1)S(1)}, bf16[2,160,128]{2,1,0:T(8,128)(2,1)S(1)}, u32[]{:S(2)}, u32[]{:S(2)}) collective-permute-start(bf16[2,160,128]{2,1,0:T(8,128)(2,1)S(1)} %bitcast.15), channel_id=1, source_target_pairs={{0,8},{8,0},{1,9},{9,1},{2,10},{10,2},{3,11},{11,3},{4,12},{12,4},... | collective-permute-start | bytes 245768 | tf_op jit(solution)/shard_map/ppermute | solution.py:341
  136.8 0.0 copy-done.7
  136.8 0.0 copy-done.6
  136.9 3.0 %collective-permute-done.3.near_ref = bf16[2,160,128]{2,1,0:T(8,128)(2,1)S(1)} collective-permute-done((bf16[2,160,128]{2,1,0:T(8,128)(2,1)S(1)}, bf16[2,160,128]{2,1,0:T(8,128)(2,1)S(1)}, u32[]{:S(2)}, u32[]{:S(2)}) %collective-permute-start.3) | collective-permute-done | bytes 81952 | tf_op jit(solution)/shard_map/ppermute | solution.py:341
  139.8 0.0 collective-permute-done.4.w1_ref
  139.9 3.4 %all-to-all-done.3 = f32[64,2,128]{2,1,0:T(2,128)S(1)} async-done(((f32[64,2,128]{2,1,0:T(2,128)}), f32[64,2,128]{2,1,0:T(2,128)S(1)}, u32[]{:S(2)}, u32[]{:S(2)}) %all-to-all-start.3) | async-done | bytes 65568 | tf_op jit(solution)/shard_map/all_to_all | solution.py:340
  143.3 0.0 collective-permute-done.6.w3_ref
  143.3 0.0 copy-done.1
  143.3 0.0 copy-done.2
  143.3 8.7 %shard_map.150 = (f32[16,128]{1,0:T(8,128)S(1)}, f32[1,128]{1,0:T(1,128)S(1)}) custom-call(f32[128,128]{1,0:T(8,128)S(1)} %bitcast.17, bf16[512,2048]{1,0:T(8,128)(2,1)} %all-gather.3.cloned.1.call-done.cand_ref, s32[1,32]{1,0:T(1,128)S(1)} %bitcast.21, bf16[2,160,128]{2,1,0:T(8,128)(2,1)S(1)} %bitcast.16, ...), custom_call_target="tpu_custom_call" | custom-call | tf_op jit(solution)/shard_map/pallas_call | solution.py:344
  152.0 15.7 %all_to_all.38 = f32[16,1,128]{2,1,0:T(1,128)S(1)} all-to-all(f32[16,1,128]{2,1,0:T(1,128)S(1)} %bitcast.19), channel_id=1, replica_groups=mesh['grp'=8,'zh'=4,'zl'=2,'xl'=2,'xh'=2,'c'=2] {'zh','xh','xl'}, dimensions={0} | all-to-all | bytes 16384 | tf_op jit(solution)/shard_map/all_to_all | solution.py:362
  167.6 0.7 shard_map.151
  (3 shorter events, 0.0 us)
Async XLA Ops:
  6.5 136.7 %all-gather.3.cloned.1.call-start = ((), (), s32[]{:S(2)}) async-start(), calls=%async_computation.5 | async-start | bytes 2228224 | tf_op jit(solution)/shard_map/all_gather | solution.py:293
  7.3 89.8 %collective-permute-start.5 = (bf16[3,2048,128]{2,1,0:T(8,128)(2,1)}, bf16[3,2048,128]{2,1,0:T(8,128)(2,1)}, u32[]{:S(2)}, u32[]{:S(2)}) collective-permute-start(bf16[3,2048,128]{2,1,0:T(8,128)(2,1)} %w0_ref.1), channel_id=1, source_target_pairs={{0,8},{8,0},{1,9},{9,1},{2,10},{10,2},{3,11},{11,3},{4,12},{12,4},... | collective-permute-start | bytes 4718600 | tf_op jit(solution)/shard_map/ppermute | solution.py:341
  13.0 71.7 %copy-start = (bf16[4096,128]{1,0:T(8,128)(2,1)S(1)}, bf16[4096,128]{1,0:T(8,128)(2,1)}, u32[]{:S(2)}) copy-start(bf16[4096,128]{1,0:T(8,128)(2,1)} %up0_ref.1) | copy-start | bytes 3145732
  16.3 68.4 %all-to-all-start = ((bf16[32,72,128]{2,1,0:T(8,128)(2,1)}), bf16[32,72,128]{2,1,0:T(8,128)(2,1)S(1)}, u32[]{:S(2)}, u32[]{:S(2)}) async-start(bf16[32,72,128]{2,1,0:T(8,128)(2,1)} %get-tuple-element.10), calls=%async_computation | async-start | bytes 1179648 | tf_op jit(solution)/shard_map/all_to_all | solution.py:313
  28.6 71.0 %copy-start.3 = (bf16[64,2048]{1,0:T(8,128)(2,1)S(1)}, bf16[64,2048]{1,0:T(8,128)(2,1)}, u32[]{:S(2)}) copy-start(bf16[64,2048]{1,0:T(8,128)(2,1)} %proj0_ref.1) | copy-start | bytes 786436
  28.6 4.9 %collective-permute-start = (bf16[4096,128]{1,0:T(8,128)(2,1)}, bf16[4096,128]{1,0:T(8,128)(2,1)S(1)}, u32[]{:S(2)}, u32[]{:S(2)}) collective-permute-start(bf16[4096,128]{1,0:T(8,128)(2,1)} %up0_ref.1), channel_id=1, source_target_pairs={{0,1},{1,0},{2,3},{3,2},{4,5},{5,4},{6,7},{7,6},{8,9},{9,8},{10,11... | collective-permute-start | bytes 3145736 | tf_op jit(solution)/shard_map/ppermute | solution.py:314
  30.6 5.0 %collective-permute-start.1 = (bf16[128,4096]{1,0:T(8,128)(2,1)}, bf16[128,4096]{1,0:T(8,128)(2,1)}, u32[]{:S(2)}, u32[]{:S(2)}) collective-permute-start(bf16[128,4096]{1,0:T(8,128)(2,1)} %down0_ref.1), channel_id=1, source_target_pairs={{0,1},{1,0},{2,3},{3,2},{4,5},{5,4},{6,7},{7,6},{8,9},{9,8},{10,11... | collective-permute-start | bytes 3145736 | tf_op jit(solution)/shard_map/ppermute | solution.py:314
  88.0 40.0 %copy-start.4 = (s32[32]{0:T(128)S(1)}, s32[32]{0:T(128)}, u32[]{:S(2)}) copy-start(s32[32]{0:T(128)} %param.23) | copy-start | bytes 388
  88.0 40.0 %copy-start.5 = (s32[32]{0:T(128)S(1)}, s32[32]{0:T(128)}, u32[]{:S(2)}) copy-start(s32[32]{0:T(128)} %param.22) | copy-start | bytes 388
  88.0 48.8 %copy-start.7 = (bf16[2048]{0:T(1024)(128)(2,1)S(1)}, bf16[2048]{0:T(1024)(128)(2,1)}, u32[]{:S(2)}) copy-start(bf16[2048]{0:T(1024)(128)(2,1)} %param.26) | copy-start | bytes 12292
  88.0 48.8 %copy-start.6 = (bf16[2048,12]{0,1:T(8,128)(2,1)S(1)}, bf16[2048,12]{0,1:T(8,128)(2,1)}, u32[]{:S(2)}) copy-start(bf16[2048,12]{0,1:T(8,128)(2,1)} %param.27) | copy-start | bytes 147460
  88.0 21.0 %all-to-all-start.1 = ((bf16[32,64,128]{2,1,0:T(8,128)(2,1)}), bf16[32,64,128]{2,1,0:T(8,128)(2,1)S(1)}, u32[]{:S(2)}, u32[]{:S(2)}) async-start(bf16[32,64,128]{2,1,0:T(8,128)(2,1)} %shard_map.147), calls=%async_computation.1 | async-start | bytes 1048576 | tf_op jit(solution)/shard_map/all_to_all | solution.py:323
  95.0 48.3 %copy-start.1 = (bf16[2048,128]{1,0:T(8,128)(2,1)S(1)}, bf16[2048,128]{1,0:T(8,128)(2,1)}, u32[]{:S(2)}) copy-start(bf16[2048,128]{1,0:T(8,128)(2,1)} %cross_u_ref.1) | copy-start | bytes 1572868
  95.0 48.3 %copy-start.2 = (bf16[128,2048]{1,0:T(8,128)(2,1)S(1)}, bf16[128,2048]{1,0:T(8,128)(2,1)}, u32[]{:S(2)}) copy-start(bf16[128,2048]{1,0:T(8,128)(2,1)} %cross_v_ref.1) | copy-start | bytes 1572868
  95.0 44.8 %collective-permute-start.4 = (bf16[3,2048,128]{2,1,0:T(8,128)(2,1)}, bf16[3,2048,128]{2,1,0:T(8,128)(2,1)}, u32[]{:S(2)}, u32[]{:S(2)}) collective-permute-start(bf16[3,2048,128]{2,1,0:T(8,128)(2,1)} %w0_ref.1), channel_id=1, source_target_pairs={{0,1},{1,0},{2,3},{3,2},{4,5},{5,4},{6,7},{7,6},{8,9},{9,8},{10,11... | collective-permute-start | bytes 4718600 | tf_op jit(solution)/shard_map/ppermute | solution.py:314
  97.1 46.2 %collective-permute-start.6 = (bf16[3,2048,128]{2,1,0:T(8,128)(2,1)}, bf16[3,2048,128]{2,1,0:T(8,128)(2,1)}, u32[]{:S(2)}, u32[]{:S(2)}) collective-permute-start(bf16[3,2048,128]{2,1,0:T(8,128)(2,1)} %collective-permute-done.5.w2_ref), channel_id=1, source_target_pairs={{0,1},{1,0},{2,3},{3,2},{4,5},{5,4},{6,7},{7,6},{8,9},{9,8},{10,11... | collective-permute-start | bytes 4718600 | tf_op jit(solution)/shard_map/ppermute | solution.py:314
  99.5 3.6 %collective-permute-start.2 = (bf16[64,2048]{1,0:T(8,128)(2,1)S(1)}, bf16[64,2048]{1,0:T(8,128)(2,1)S(1)}, u32[]{:S(2)}, u32[]{:S(2)}) collective-permute-start(bf16[64,2048]{1,0:T(8,128)(2,1)S(1)} %copy-done.3), channel_id=1, source_target_pairs={{0,1},{1,0},{2,3},{3,2},{4,5},{5,4},{6,7},{7,6},{8,9},{9,8},{10,11... | collective-permute-start | bytes 786440 | tf_op jit(solution)/shard_map/ppermute | solution.py:314
  128.8 14.5 %all-to-all-start.3 = ((f32[64,2,128]{2,1,0:T(2,128)}), f32[64,2,128]{2,1,0:T(2,128)S(1)}, u32[]{:S(2)}, u32[]{:S(2)}) async-start(f32[64,2,128]{2,1,0:T(2,128)} %bitcast.6), calls=%async_computation.3 | async-start | bytes 131072 | tf_op jit(solution)/shard_map/all_to_all | solution.py:340
  133.3 6.5 %collective-permute-start.3 = (bf16[2,160,128]{2,1,0:T(8,128)(2,1)S(1)}, bf16[2,160,128]{2,1,0:T(8,128)(2,1)S(1)}, u32[]{:S(2)}, u32[]{:S(2)}) collective-permute-start(bf16[2,160,128]{2,1,0:T(8,128)(2,1)S(1)} %bitcast.15), channel_id=1, source_target_pairs={{0,8},{8,0},{1,9},{9,1},{2,10},{10,2},{3,11},{11,3},{4,12},{12,4},... | collective-permute-start | bytes 245768 | tf_op jit(solution)/shard_map/ppermute | solution.py:341
Sparse Core Ops, SparseCore 0:
  10.4 79.9 all-gather.2

commit v6 on v4

--- a/solution.py
+++ b/solution.py
@@ -232,13 +232,11 @@
         arrivals[i].wait()
         if i == 0:
             get_u.wait()
-        low = jnp.zeros((STEP, 128), F32)
         for j in range(8):
             cols = slice(256 * j, 256 * j + 256)
             added = jnp.dot(hot, users[:, cols], preferred_element_type=F32)
-            x0 = (x[part, cols].astype(F32) + added).astype(BF16)
-            x[part, cols] = x0
-            low = low + jnp.dot(x0, cross_u[cols, :], preferred_element_type=F32)
+            x[part, cols] = (x[part, cols].astype(F32) + added).astype(BF16)
+        low = jnp.dot(x[part, :], cross_u[...], preferred_element_type=F32)
         left = jnp.concatenate([low.astype(BF16), ones], axis=1)
         if i == 0:
             get_v.wait()

time: 144 us -> 143 us (level)
  no operation moved by 1% of the time
where the time goes in v6:
time: 143 us; the launch traced here: 142 us
  waiting for transfers between devices  40 us (28%)
  blocking collectives  38.8 us (27%)
  starting transfers between devices  31.7 us (22%)
  Pallas kernels  17.8 us (12%)
  between operations  13.6 us (10%)
    all_to_all x1, blocking collectives, body(): values = lax.all_to_all(values, CHIPS, 0, 0, tiled=True)  21.1 us
    all_to_all x1, blocking collectives, body(): back = lax.all_to_all(part, CHIPS, 0, 0, tiled=True)  15.4 us
    all_to_all x1, waiting for transfers between devices, body(): tokens = lax.all_to_all(spread, CHIPS, 0, 0, tiled=True)  14.2 us
    all_to_all x1, starting transfers between devices, body(): tokens = lax.all_to_all(spread, CHIPS, 0, 0, tiled=True)  13.2 us
    all_to_all x1, waiting for transfers between devices, body(): summed = lax.all_to_all(parts, CHIPS, 0, 0, tiled=True)  11.1 us
    all_to_all x1, waiting for transfers between devices, body(): users = lax.all_to_all(user, ALL, 0, 0, tiled=True)  10.1 us
    pallas_call x1, Pallas kernels, body(): pl.pallas_call(score_kernel, out_shape=(jax.ShapeDtypeStruct((N_CHIPS, 12...  9.88 us
    ppermute x4, starting transfers between devices, body(): swap = lambda x: lax.ppermute(x, 'c', [(0, 1), (1, 0)])  8.93 us
  transfers between devices with their start and end apart: 8, of which 6 were waited for; matrix products, arithmetic and copies ran while one was open for 0% of the time, Pallas kernels for 5%

profile of v6, /device:TPU:56, one launch (start us, length us, event | category | flops | bytes accessed | tf_op | source)
XLA Modules:
  0.0 142.0 jit_solution(10228701818658872249)
XLA Ops:
  6.5 0.0 all-gather.3.cloned.1.call-start
  6.5 0.7 all-gather.3.cloned.1.call-update
  7.3 1.5 %shard_map.145 = bf16[160,128]{1,0:T(8,128)(2,1)} custom-call(bf16[64,128]{1,0:T(8,128)(2,1)} %bitcast.24, bf16[1,64]{1,0:T(2,128)(2,1)} %gain_ref.1, bf16[1,64]{1,0:T(2,128)(2,1)} %bitcast.26, bf16[3,4,128]{2,1,0:T(4,128)(2,1)} %bitcast.25), custom_call_target="tpu_custom_call" | custom-call | tf_op jit(solution)/shard_map/pallas_call | solution.py:287
  8.7 0.0 copy-start
  8.7 2.2 %all-gather = bf16[320,128]{1,0:T(8,128)(2,1)S(1)} all-gather(bf16[160,128]{1,0:T(8,128)(2,1)} %shard_map.145), channel_id=2, replica_groups=mesh['grp'=8,'z'=8,'xl'=2,'xh'=2,'c'=2] {'c'}, dimensions={0}, use_global_device_ids=true | all-gather | bytes 122880 | tf_op jit(solution)/shard_map/all_gather | solution.py:294
  10.9 1.1 shard_map.146
  12.0 13.2 %all-to-all-start = ((bf16[32,72,128]{2,1,0:T(8,128)(2,1)}), bf16[32,72,128]{2,1,0:T(8,128)(2,1)S(1)}, u32[]{:S(2)}, u32[]{:S(2)}) async-start(bf16[32,72,128]{2,1,0:T(8,128)(2,1)} %get-tuple-element.10), calls=%async_computation | async-start | bytes 1179648 | tf_op jit(solution)/shard_map/all_to_all | solution.py:306
  25.2 0.0 copy-start.3
  25.2 2.1 %collective-permute-start = (bf16[4096,128]{1,0:T(8,128)(2,1)}, bf16[4096,128]{1,0:T(8,128)(2,1)S(1)}, u32[]{:S(2)}, u32[]{:S(2)}) collective-permute-start(bf16[4096,128]{1,0:T(8,128)(2,1)} %up0_ref.1), channel_id=1, source_target_pairs={{0,1},{1,0},{2,3},{3,2},{4,5},{5,4},{6,7},{7,6},{8,9},{9,8},{10,11... | collective-permute-start | bytes 3145736 | tf_op jit(solution)/shard_map/ppermute | solution.py:307
  27.3 2.4 %collective-permute-start.1 = (bf16[128,4096]{1,0:T(8,128)(2,1)}, bf16[128,4096]{1,0:T(8,128)(2,1)}, u32[]{:S(2)}, u32[]{:S(2)}) collective-permute-start(bf16[128,4096]{1,0:T(8,128)(2,1)} %down0_ref.1), channel_id=1, source_target_pairs={{0,1},{1,0},{2,3},{3,2},{4,5},{5,4},{6,7},{7,6},{8,9},{9,8},{10,11... | collective-permute-start | bytes 3145736 | tf_op jit(solution)/shard_map/ppermute | solution.py:307
  29.7 0.4 collective-permute-done.up1_ref
  30.1 2.2 %collective-permute-done.1.down1_ref = bf16[128,4096]{1,0:T(8,128)(2,1)} collective-permute-done((bf16[128,4096]{1,0:T(8,128)(2,1)}, bf16[128,4096]{1,0:T(8,128)(2,1)}, u32[]{:S(2)}, u32[]{:S(2)}) %collective-permute-start.1) | collective-permute-done | bytes 1048608 | tf_op jit(solution)/shard_map/ppermute | solution.py:307
  32.3 14.2 %all-to-all-done.got_ref = bf16[32,72,128]{2,1,0:T(8,128)(2,1)S(1)} async-done(((bf16[32,72,128]{2,1,0:T(8,128)(2,1)}), bf16[32,72,128]{2,1,0:T(8,128)(2,1)S(1)}, u32[]{:S(2)}, u32[]{:S(2)}) %all-to-all-start) | async-done | bytes 589856 | tf_op jit(solution)/shard_map/all_to_all | solution.py:306
  46.5 0.0 copy-done
  46.5 3.2 %shard_map.147 = bf16[32,64,128]{2,1,0:T(8,128)(2,1)} custom-call(bf16[32,72,128]{2,1,0:T(8,128)(2,1)S(1)} %all-to-all-done.got_ref, bf16[4096,128]{1,0:T(8,128)(2,1)S(1)} %copy-done, bf16[4096,128]{1,0:T(8,128)(2,1)S(1)} %collective-permute-done.up1_ref, bf16[128,4096]{1,0:T(8,128)(2,1)} %down0_ref.1, bf16[128,4096]{1,0:T(8,128)(2,1)} %collective-permute-done.1.down1_ref), custom_call_target="tpu_custom_call" | custom-call | tf_op jit(solution)/shard_map/pallas_call | solution.py:308
  49.7 0.0 copy-start.4
  49.7 0.0 copy-start.5
  49.8 0.0 copy-start.7
  49.8 0.0 copy-start.6
  49.8 4.7 %all-to-all-start.1 = ((bf16[32,64,128]{2,1,0:T(8,128)(2,1)}), bf16[32,64,128]{2,1,0:T(8,128)(2,1)S(1)}, u32[]{:S(2)}, u32[]{:S(2)}) async-start(bf16[32,64,128]{2,1,0:T(8,128)(2,1)} %shard_map.147), calls=%async_computation.1 | async-start | bytes 1048576 | tf_op jit(solution)/shard_map/all_to_all | solution.py:316
  54.5 0.0 copy-start.1
  54.5 0.0 copy-start.2
  54.5 2.1 %collective-permute-start.3 = (bf16[3,2048,128]{2,1,0:T(8,128)(2,1)}, bf16[3,2048,128]{2,1,0:T(8,128)(2,1)}, u32[]{:S(2)}, u32[]{:S(2)}) collective-permute-start(bf16[3,2048,128]{2,1,0:T(8,128)(2,1)} %w0_ref.1), channel_id=1, source_target_pairs={{0,1},{1,0},{2,3},{3,2},{4,5},{5,4},{6,7},{7,6},{8,9},{9,8},{10,11... | collective-permute-start | bytes 4718600 | tf_op jit(solution)/shard_map/ppermute | solution.py:307
  56.5 0.0 copy-done.3
  56.6 2.4 %collective-permute-start.2 = (bf16[64,2048]{1,0:T(8,128)(2,1)S(1)}, bf16[64,2048]{1,0:T(8,128)(2,1)S(1)}, u32[]{:S(2)}, u32[]{:S(2)}) collective-permute-start(bf16[64,2048]{1,0:T(8,128)(2,1)S(1)} %copy-done.3), channel_id=1, source_target_pairs={{0,1},{1,0},{2,3},{3,2},{4,5},{5,4},{6,7},{7,6},{8,9},{9,8},{10,11... | collective-permute-start | bytes 786440 | tf_op jit(solution)/shard_map/ppermute | solution.py:307
  59.0 1.3 collective-permute-done.2.proj1_ref
  60.3 11.1 %all-to-all-done.1.got_ref = bf16[32,64,128]{2,1,0:T(8,128)(2,1)S(1)} async-done(((bf16[32,64,128]{2,1,0:T(8,128)(2,1)}), bf16[32,64,128]{2,1,0:T(8,128)(2,1)S(1)}, u32[]{:S(2)}, u32[]{:S(2)}) %all-to-all-start.1) | async-done | bytes 524320 | tf_op jit(solution)/shard_map/all_to_all | solution.py:316
  71.4 0.7 shard_map.148
  72.1 21.1 %all_to_all.37.got_ref = bf16[32,40,128]{2,1,0:T(8,128)(2,1)S(1)} all-to-all(bf16[32,40,128]{2,1,0:T(8,128)(2,1)S(1)} %shard_map.148), channel_id=1, replica_groups=mesh['grp'=8,'z'=8,'xl'=2,'xh'=2,'c'=2] {'z','xh','xl'}, dimensions={0} | all-to-all | bytes 655360 | tf_op jit(solution)/shard_map/all_to_all | solution.py:325
  93.2 0.0 copy-done.4
  93.2 0.0 copy-done.5
  93.3 0.8 shard_map.149
  94.0 5.0 %all-to-all-start.3 = ((f32[64,2,128]{2,1,0:T(2,128)}), f32[64,2,128]{2,1,0:T(2,128)S(1)}, u32[]{:S(2)}, u32[]{:S(2)}) async-start(f32[64,2,128]{2,1,0:T(2,128)} %bitcast.6), calls=%async_computation.3 | async-start | bytes 131072 | tf_op jit(solution)/shard_map/all_to_all | solution.py:333
  99.0 0.0 copy-done.7
  99.0 0.0 copy-done.6
  99.0 0.0 collective-permute-done.3.w1_ref
  99.1 10.1 %all-to-all-done.3 = f32[64,2,128]{2,1,0:T(2,128)S(1)} async-done(((f32[64,2,128]{2,1,0:T(2,128)}), f32[64,2,128]{2,1,0:T(2,128)S(1)}, u32[]{:S(2)}, u32[]{:S(2)}) %all-to-all-start.3) | async-done | bytes 65568 | tf_op jit(solution)/shard_map/all_to_all | solution.py:333
  109.1 0.0 all-gather.3.cloned.1.call-done.cand_ref
  109.1 0.0 copy-done.1
  109.2 0.0 copy-done.2
  109.2 9.9 %shard_map.150 = (f32[32,128]{1,0:T(8,128)S(1)}, f32[1,128]{1,0:T(1,128)S(1)}) custom-call(f32[128,128]{1,0:T(8,128)S(1)} %bitcast.16, bf16[1024,2048]{1,0:T(8,128)(2,1)} %all-gather.3.cloned.1.call-done.cand_ref, s32[1,32]{1,0:T(1,128)S(1)} %bitcast.20, bf16[2,160,128]{2,1,0:T(8,128)(2,1)S(1)} %bitcast.15, bf16[2048,128]{1,0:T(8,128)(2,1)S(1)} %copy-done.1, ...), custom_call_target="tpu_custom_call" | custom-call | tf_op jit(solution)/shard_map/pallas_call | solution.py:335
  119.0 15.4 %all_to_all.38 = f32[32,1,128]{2,1,0:T(1,128)S(1)} all-to-all(f32[32,1,128]{2,1,0:T(1,128)S(1)} %bitcast.18), channel_id=1, replica_groups=mesh['grp'=8,'z'=8,'xl'=2,'xh'=2,'c'=2] {'z','xh','xl'}, dimensions={0} | all-to-all | bytes 32768 | tf_op jit(solution)/shard_map/all_to_all | solution.py:350
  134.5 0.7 shard_map.151
  (2 shorter events, 0.0 us)
Async XLA Ops:
  6.5 102.6 %all-gather.3.cloned.1.call-start = ((), (), s32[]{:S(2)}) async-start(), calls=%async_computation.5 | async-start | bytes 4325376 | tf_op jit(solution)/shard_map/all_gather | solution.py:286
  8.7 37.8 %copy-start = (bf16[4096,128]{1,0:T(8,128)(2,1)S(1)}, bf16[4096,128]{1,0:T(8,128)(2,1)}, u32[]{:S(2)}) copy-start(bf16[4096,128]{1,0:T(8,128)(2,1)} %up0_ref.1) | copy-start | bytes 3145732
  12.0 34.5 %all-to-all-start = ((bf16[32,72,128]{2,1,0:T(8,128)(2,1)}), bf16[32,72,128]{2,1,0:T(8,128)(2,1)S(1)}, u32[]{:S(2)}, u32[]{:S(2)}) async-start(bf16[32,72,128]{2,1,0:T(8,128)(2,1)} %get-tuple-element.10), calls=%async_computation | async-start | bytes 1179648 | tf_op jit(solution)/shard_map/all_to_all | solution.py:306
  25.2 31.4 %copy-start.3 = (bf16[64,2048]{1,0:T(8,128)(2,1)S(1)}, bf16[64,2048]{1,0:T(8,128)(2,1)}, u32[]{:S(2)}) copy-start(bf16[64,2048]{1,0:T(8,128)(2,1)} %proj0_ref.1) | copy-start | bytes 786436
  25.2 4.9 %collective-permute-start = (bf16[4096,128]{1,0:T(8,128)(2,1)}, bf16[4096,128]{1,0:T(8,128)(2,1)S(1)}, u32[]{:S(2)}, u32[]{:S(2)}) collective-permute-start(bf16[4096,128]{1,0:T(8,128)(2,1)} %up0_ref.1), channel_id=1, source_target_pairs={{0,1},{1,0},{2,3},{3,2},{4,5},{5,4},{6,7},{7,6},{8,9},{9,8},{10,11... | collective-permute-start | bytes 3145736 | tf_op jit(solution)/shard_map/ppermute | solution.py:307
  27.3 5.0 %collective-permute-start.1 = (bf16[128,4096]{1,0:T(8,128)(2,1)}, bf16[128,4096]{1,0:T(8,128)(2,1)}, u32[]{:S(2)}, u32[]{:S(2)}) collective-permute-start(bf16[128,4096]{1,0:T(8,128)(2,1)} %down0_ref.1), channel_id=1, source_target_pairs={{0,1},{1,0},{2,3},{3,2},{4,5},{5,4},{6,7},{7,6},{8,9},{9,8},{10,11... | collective-permute-start | bytes 3145736 | tf_op jit(solution)/shard_map/ppermute | solution.py:307
  49.7 43.5 %copy-start.4 = (s32[32]{0:T(128)S(1)}, s32[32]{0:T(128)}, u32[]{:S(2)}) copy-start(s32[32]{0:T(128)} %param.23) | copy-start | bytes 388
  49.7 43.5 %copy-start.5 = (s32[32]{0:T(128)S(1)}, s32[32]{0:T(128)}, u32[]{:S(2)}) copy-start(s32[32]{0:T(128)} %param.22) | copy-start | bytes 388
  49.8 49.2 %copy-start.7 = (bf16[2048]{0:T(1024)(128)(2,1)S(1)}, bf16[2048]{0:T(1024)(128)(2,1)}, u32[]{:S(2)}) copy-start(bf16[2048]{0:T(1024)(128)(2,1)} %param.26) | copy-start | bytes 12292
  49.8 49.3 %copy-start.6 = (bf16[2048,12]{0,1:T(8,128)(2,1)S(1)}, bf16[2048,12]{0,1:T(8,128)(2,1)}, u32[]{:S(2)}) copy-start(bf16[2048,12]{0,1:T(8,128)(2,1)} %param.27) | copy-start | bytes 147460
  49.8 21.6 %all-to-all-start.1 = ((bf16[32,64,128]{2,1,0:T(8,128)(2,1)}), bf16[32,64,128]{2,1,0:T(8,128)(2,1)S(1)}, u32[]{:S(2)}, u32[]{:S(2)}) async-start(bf16[32,64,128]{2,1,0:T(8,128)(2,1)} %shard_map.147), calls=%async_computation.1 | async-start | bytes 1048576 | tf_op jit(solution)/shard_map/all_to_all | solution.py:316
  54.5 54.7 %copy-start.1 = (bf16[2048,128]{1,0:T(8,128)(2,1)S(1)}, bf16[2048,128]{1,0:T(8,128)(2,1)}, u32[]{:S(2)}) copy-start(bf16[2048,128]{1,0:T(8,128)(2,1)} %cross_u_ref.1) | copy-start | bytes 1572868
  54.5 54.7 %copy-start.2 = (bf16[128,2048]{1,0:T(8,128)(2,1)S(1)}, bf16[128,2048]{1,0:T(8,128)(2,1)}, u32[]{:S(2)}) copy-start(bf16[128,2048]{1,0:T(8,128)(2,1)} %cross_v_ref.1) | copy-start | bytes 1572868
  54.5 44.6 %collective-permute-start.3 = (bf16[3,2048,128]{2,1,0:T(8,128)(2,1)}, bf16[3,2048,128]{2,1,0:T(8,128)(2,1)}, u32[]{:S(2)}, u32[]{:S(2)}) collective-permute-start(bf16[3,2048,128]{2,1,0:T(8,128)(2,1)} %w0_ref.1), channel_id=1, source_target_pairs={{0,1},{1,0},{2,3},{3,2},{4,5},{5,4},{6,7},{7,6},{8,9},{9,8},{10,11... | collective-permute-start | bytes 4718600 | tf_op jit(solution)/shard_map/ppermute | solution.py:307
  56.6 3.7 %collective-permute-start.2 = (bf16[64,2048]{1,0:T(8,128)(2,1)S(1)}, bf16[64,2048]{1,0:T(8,128)(2,1)S(1)}, u32[]{:S(2)}, u32[]{:S(2)}) collective-permute-start(bf16[64,2048]{1,0:T(8,128)(2,1)S(1)} %copy-done.3), channel_id=1, source_target_pairs={{0,1},{1,0},{2,3},{3,2},{4,5},{5,4},{6,7},{7,6},{8,9},{9,8},{10,11... | collective-permute-start | bytes 786440 | tf_op jit(solution)/shard_map/ppermute | solution.py:307
  94.0 15.1 %all-to-all-start.3 = ((f32[64,2,128]{2,1,0:T(2,128)}), f32[64,2,128]{2,1,0:T(2,128)S(1)}, u32[]{:S(2)}, u32[]{:S(2)}) async-start(f32[64,2,128]{2,1,0:T(2,128)} %bitcast.6), calls=%async_computation.3 | async-start | bytes 131072 | tf_op jit(solution)/shard_map/all_to_all | solution.py:333
Sparse Core Ops, SparseCore 0:
  10.5 96.9 all-gather.2

commit v7 on v6

--- a/solution.py
+++ b/solution.py
@@ -189,7 +189,7 @@
         for i, source in enumerate((w0_ref, w1_ref)):
             start = 256 * k + 128 * i
             get_w.append(pltpu.make_async_copy(source.at[k], w.at[:, start : start + 128], sems.at[6 + 2 * k + i]))
-    for copy in (arrivals[0], get_u, get_v, *arrivals[1:], *get_w):
+    for copy in (arrivals[0], get_u, get_v, *arrivals[1:]):
         copy.start()
     row = rows((16, 128))
     low_half = lanes((1, 128)) < 64
@@ -232,6 +232,9 @@
         arrivals[i].wait()
         if i == 0:
             get_u.wait()
+        if i == 1:
+            for copy in get_w:
+                copy.start()
         for j in range(8):
             cols = slice(256 * j, 256 * j + 256)
             added = jnp.dot(hot, users[:, cols], preferred_element_type=F32)

time: 143 us -> 143 us (level)
  no operation moved by 1% of the time
where the time goes in v7:
time: 143 us; the launch traced here: 142 us
  waiting for transfers between devices  40 us (28%)
  blocking collectives  38.8 us (27%)
  starting transfers between devices  31.7 us (22%)
  Pallas kernels  17.8 us (12%)
  between operations  13.6 us (10%)
    all_to_all x1, blocking collectives, body(): values = lax.all_to_all(values, CHIPS, 0, 0, tiled=True)  21.1 us
    all_to_all x1, blocking collectives, body(): back = lax.all_to_all(part, CHIPS, 0, 0, tiled=True)  15.4 us
    all_to_all x1, waiting for transfers between devices, body(): tokens = lax.all_to_all(spread, CHIPS, 0, 0, tiled=True)  14.2 us
    all_to_all x1, starting transfers between devices, body(): tokens = lax.all_to_all(spread, CHIPS, 0, 0, tiled=True)  13.2 us
    all_to_all x1, waiting for transfers between devices, body(): summed = lax.all_to_all(parts, CHIPS, 0, 0, tiled=True)  11.1 us
    all_to_all x1, waiting for transfers between devices, body(): users = lax.all_to_all(user, ALL, 0, 0, tiled=True)  10.1 us
    pallas_call x1, Pallas kernels, body(): pl.pallas_call(score_kernel, out_shape=(jax.ShapeDtypeStruct((N_CHIPS, 12...  9.88 us
    ppermute x4, starting transfers between devices, body(): swap = lambda x: lax.ppermute(x, 'c', [(0, 1), (1, 0)])  8.93 us
  transfers between devices with their start and end apart: 8, of which 6 were waited for; matrix products, arithmetic and copies ran while one was open for 0% of the time, Pallas kernels for 5%

profile of v7, /device:TPU:56, one launch (start us, length us, event | category | flops | bytes accessed | tf_op | source)
XLA Modules:
  0.0 142.0 jit_solution(2079834910364086859)
XLA Ops:
  6.5 0.0 all-gather.3.cloned.1.call-start
  6.5 0.7 all-gather.3.cloned.1.call-update
  7.3 1.5 %shard_map.145 = bf16[160,128]{1,0:T(8,128)(2,1)} custom-call(bf16[64,128]{1,0:T(8,128)(2,1)} %bitcast.24, bf16[1,64]{1,0:T(2,128)(2,1)} %gain_ref.1, bf16[1,64]{1,0:T(2,128)(2,1)} %bitcast.26, bf16[3,4,128]{2,1,0:T(4,128)(2,1)} %bitcast.25), custom_call_target="tpu_custom_call" | custom-call | tf_op jit(solution)/shard_map/pallas_call | solution.py:290
  8.7 0.0 copy-start
  8.7 2.2 %all-gather = bf16[320,128]{1,0:T(8,128)(2,1)S(1)} all-gather(bf16[160,128]{1,0:T(8,128)(2,1)} %shard_map.145), channel_id=2, replica_groups=mesh['grp'=8,'z'=8,'xl'=2,'xh'=2,'c'=2] {'c'}, dimensions={0}, use_global_device_ids=true | all-gather | bytes 122880 | tf_op jit(solution)/shard_map/all_gather | solution.py:297
  10.9 1.1 shard_map.146
  12.0 13.2 %all-to-all-start = ((bf16[32,72,128]{2,1,0:T(8,128)(2,1)}), bf16[32,72,128]{2,1,0:T(8,128)(2,1)S(1)}, u32[]{:S(2)}, u32[]{:S(2)}) async-start(bf16[32,72,128]{2,1,0:T(8,128)(2,1)} %get-tuple-element.10), calls=%async_computation | async-start | bytes 1179648 | tf_op jit(solution)/shard_map/all_to_all | solution.py:309
  25.2 0.0 copy-start.3
  25.2 2.1 %collective-permute-start = (bf16[4096,128]{1,0:T(8,128)(2,1)}, bf16[4096,128]{1,0:T(8,128)(2,1)S(1)}, u32[]{:S(2)}, u32[]{:S(2)}) collective-permute-start(bf16[4096,128]{1,0:T(8,128)(2,1)} %up0_ref.1), channel_id=1, source_target_pairs={{0,1},{1,0},{2,3},{3,2},{4,5},{5,4},{6,7},{7,6},{8,9},{9,8},{10,11... | collective-permute-start | bytes 3145736 | tf_op jit(solution)/shard_map/ppermute | solution.py:310
  27.3 2.4 %collective-permute-start.1 = (bf16[128,4096]{1,0:T(8,128)(2,1)}, bf16[128,4096]{1,0:T(8,128)(2,1)}, u32[]{:S(2)}, u32[]{:S(2)}) collective-permute-start(bf16[128,4096]{1,0:T(8,128)(2,1)} %down0_ref.1), channel_id=1, source_target_pairs={{0,1},{1,0},{2,3},{3,2},{4,5},{5,4},{6,7},{7,6},{8,9},{9,8},{10,11... | collective-permute-start | bytes 3145736 | tf_op jit(solution)/shard_map/ppermute | solution.py:310
  29.7 0.4 collective-permute-done.up1_ref
  30.1 2.2 %collective-permute-done.1.down1_ref = bf16[128,4096]{1,0:T(8,128)(2,1)} collective-permute-done((bf16[128,4096]{1,0:T(8,128)(2,1)}, bf16[128,4096]{1,0:T(8,128)(2,1)}, u32[]{:S(2)}, u32[]{:S(2)}) %collective-permute-start.1) | collective-permute-done | bytes 1048608 | tf_op jit(solution)/shard_map/ppermute | solution.py:310
  32.3 14.2 %all-to-all-done.got_ref = bf16[32,72,128]{2,1,0:T(8,128)(2,1)S(1)} async-done(((bf16[32,72,128]{2,1,0:T(8,128)(2,1)}), bf16[32,72,128]{2,1,0:T(8,128)(2,1)S(1)}, u32[]{:S(2)}, u32[]{:S(2)}) %all-to-all-start) | async-done | bytes 589856 | tf_op jit(solution)/shard_map/all_to_all | solution.py:309
  46.5 0.0 copy-done
  46.5 3.2 %shard_map.147 = bf16[32,64,128]{2,1,0:T(8,128)(2,1)} custom-call(bf16[32,72,128]{2,1,0:T(8,128)(2,1)S(1)} %all-to-all-done.got_ref, bf16[4096,128]{1,0:T(8,128)(2,1)S(1)} %copy-done, bf16[4096,128]{1,0:T(8,128)(2,1)S(1)} %collective-permute-done.up1_ref, bf16[128,4096]{1,0:T(8,128)(2,1)} %down0_ref.1, bf16[128,4096]{1,0:T(8,128)(2,1)} %collective-permute-done.1.down1_ref), custom_call_target="tpu_custom_call" | custom-call | tf_op jit(solution)/shard_map/pallas_call | solution.py:311
  49.7 0.0 copy-start.4
  49.7 0.0 copy-start.5
  49.8 0.0 copy-start.7
  49.8 0.0 copy-start.6
  49.8 4.7 %all-to-all-start.1 = ((bf16[32,64,128]{2,1,0:T(8,128)(2,1)}), bf16[32,64,128]{2,1,0:T(8,128)(2,1)S(1)}, u32[]{:S(2)}, u32[]{:S(2)}) async-start(bf16[32,64,128]{2,1,0:T(8,128)(2,1)} %shard_map.147), calls=%async_computation.1 | async-start | bytes 1048576 | tf_op jit(solution)/shard_map/all_to_all | solution.py:319
  54.5 0.0 copy-start.1
  54.5 0.0 copy-start.2
  54.5 2.1 %collective-permute-start.3 = (bf16[3,2048,128]{2,1,0:T(8,128)(2,1)}, bf16[3,2048,128]{2,1,0:T(8,128)(2,1)}, u32[]{:S(2)}, u32[]{:S(2)}) collective-permute-start(bf16[3,2048,128]{2,1,0:T(8,128)(2,1)} %w0_ref.1), channel_id=1, source_target_pairs={{0,1},{1,0},{2,3},{3,2},{4,5},{5,4},{6,7},{7,6},{8,9},{9,8},{10,11... | collective-permute-start | bytes 4718600 | tf_op jit(solution)/shard_map/ppermute | solution.py:310
  56.5 0.0 copy-done.3
  56.6 2.4 %collective-permute-start.2 = (bf16[64,2048]{1,0:T(8,128)(2,1)S(1)}, bf16[64,2048]{1,0:T(8,128)(2,1)S(1)}, u32[]{:S(2)}, u32[]{:S(2)}) collective-permute-start(bf16[64,2048]{1,0:T(8,128)(2,1)S(1)} %copy-done.3), channel_id=1, source_target_pairs={{0,1},{1,0},{2,3},{3,2},{4,5},{5,4},{6,7},{7,6},{8,9},{9,8},{10,11... | collective-permute-start | bytes 786440 | tf_op jit(solution)/shard_map/ppermute | solution.py:310
  59.0 1.3 collective-permute-done.2.proj1_ref
  60.3 11.1 %all-to-all-done.1.got_ref = bf16[32,64,128]{2,1,0:T(8,128)(2,1)S(1)} async-done(((bf16[32,64,128]{2,1,0:T(8,128)(2,1)}), bf16[32,64,128]{2,1,0:T(8,128)(2,1)S(1)}, u32[]{:S(2)}, u32[]{:S(2)}) %all-to-all-start.1) | async-done | bytes 524320 | tf_op jit(solution)/shard_map/all_to_all | solution.py:319
  71.4 0.7 shard_map.148
  72.1 21.1 %all_to_all.37.got_ref = bf16[32,40,128]{2,1,0:T(8,128)(2,1)S(1)} all-to-all(bf16[32,40,128]{2,1,0:T(8,128)(2,1)S(1)} %shard_map.148), channel_id=1, replica_groups=mesh['grp'=8,'z'=8,'xl'=2,'xh'=2,'c'=2] {'z','xh','xl'}, dimensions={0} | all-to-all | bytes 655360 | tf_op jit(solution)/shard_map/all_to_all | solution.py:328
  93.2 0.0 copy-done.4
  93.2 0.0 copy-done.5
  93.3 0.8 shard_map.149
  94.0 5.0 %all-to-all-start.3 = ((f32[64,2,128]{2,1,0:T(2,128)}), f32[64,2,128]{2,1,0:T(2,128)S(1)}, u32[]{:S(2)}, u32[]{:S(2)}) async-start(f32[64,2,128]{2,1,0:T(2,128)} %bitcast.6), calls=%async_computation.3 | async-start | bytes 131072 | tf_op jit(solution)/shard_map/all_to_all | solution.py:336
  99.0 0.0 copy-done.7
  99.0 0.0 copy-done.6
  99.0 0.0 collective-permute-done.3.w1_ref
  99.1 10.1 %all-to-all-done.3 = f32[64,2,128]{2,1,0:T(2,128)S(1)} async-done(((f32[64,2,128]{2,1,0:T(2,128)}), f32[64,2,128]{2,1,0:T(2,128)S(1)}, u32[]{:S(2)}, u32[]{:S(2)}) %all-to-all-start.3) | async-done | bytes 65568 | tf_op jit(solution)/shard_map/all_to_all | solution.py:336
  109.1 0.0 all-gather.3.cloned.1.call-done.cand_ref
  109.1 0.0 copy-done.1
  109.2 0.0 copy-done.2
  109.2 9.9 %shard_map.150 = (f32[32,128]{1,0:T(8,128)S(1)}, f32[1,128]{1,0:T(1,128)S(1)}) custom-call(f32[128,128]{1,0:T(8,128)S(1)} %bitcast.16, bf16[1024,2048]{1,0:T(8,128)(2,1)} %all-gather.3.cloned.1.call-done.cand_ref, s32[1,32]{1,0:T(1,128)S(1)} %bitcast.20, bf16[2,160,128]{2,1,0:T(8,128)(2,1)S(1)} %bitcast.15, bf16[2048,128]{1,0:T(8,128)(2,1)S(1)} %copy-done.1, ...), custom_call_target="tpu_custom_call" | custom-call | tf_op jit(solution)/shard_map/pallas_call | solution.py:338
  119.0 15.4 %all_to_all.38 = f32[32,1,128]{2,1,0:T(1,128)S(1)} all-to-all(f32[32,1,128]{2,1,0:T(1,128)S(1)} %bitcast.18), channel_id=1, replica_groups=mesh['grp'=8,'z'=8,'xl'=2,'xh'=2,'c'=2] {'z','xh','xl'}, dimensions={0} | all-to-all | bytes 32768 | tf_op jit(solution)/shard_map/all_to_all | solution.py:353
  134.5 0.7 shard_map.151
  (2 shorter events, 0.0 us)
Async XLA Ops:
  6.5 102.6 %all-gather.3.cloned.1.call-start = ((), (), s32[]{:S(2)}) async-start(), calls=%async_computation.5 | async-start | bytes 4325376 | tf_op jit(solution)/shard_map/all_gather | solution.py:289
  8.7 37.8 %copy-start = (bf16[4096,128]{1,0:T(8,128)(2,1)S(1)}, bf16[4096,128]{1,0:T(8,128)(2,1)}, u32[]{:S(2)}) copy-start(bf16[4096,128]{1,0:T(8,128)(2,1)} %up0_ref.1) | copy-start | bytes 3145732
  12.0 34.5 %all-to-all-start = ((bf16[32,72,128]{2,1,0:T(8,128)(2,1)}), bf16[32,72,128]{2,1,0:T(8,128)(2,1)S(1)}, u32[]{:S(2)}, u32[]{:S(2)}) async-start(bf16[32,72,128]{2,1,0:T(8,128)(2,1)} %get-tuple-element.10), calls=%async_computation | async-start | bytes 1179648 | tf_op jit(solution)/shard_map/all_to_all | solution.py:309
  25.2 31.4 %copy-start.3 = (bf16[64,2048]{1,0:T(8,128)(2,1)S(1)}, bf16[64,2048]{1,0:T(8,128)(2,1)}, u32[]{:S(2)}) copy-start(bf16[64,2048]{1,0:T(8,128)(2,1)} %proj0_ref.1) | copy-start | bytes 786436
  25.2 4.9 %collective-permute-start = (bf16[4096,128]{1,0:T(8,128)(2,1)}, bf16[4096,128]{1,0:T(8,128)(2,1)S(1)}, u32[]{:S(2)}, u32[]{:S(2)}) collective-permute-start(bf16[4096,128]{1,0:T(8,128)(2,1)} %up0_ref.1), channel_id=1, source_target_pairs={{0,1},{1,0},{2,3},{3,2},{4,5},{5,4},{6,7},{7,6},{8,9},{9,8},{10,11... | collective-permute-start | bytes 3145736 | tf_op jit(solution)/shard_map/ppermute | solution.py:310
  27.3 5.0 %collective-permute-start.1 = (bf16[128,4096]{1,0:T(8,128)(2,1)}, bf16[128,4096]{1,0:T(8,128)(2,1)}, u32[]{:S(2)}, u32[]{:S(2)}) collective-permute-start(bf16[128,4096]{1,0:T(8,128)(2,1)} %down0_ref.1), channel_id=1, source_target_pairs={{0,1},{1,0},{2,3},{3,2},{4,5},{5,4},{6,7},{7,6},{8,9},{9,8},{10,11... | collective-permute-start | bytes 3145736 | tf_op jit(solution)/shard_map/ppermute | solution.py:310
  49.7 43.5 %copy-start.4 = (s32[32]{0:T(128)S(1)}, s32[32]{0:T(128)}, u32[]{:S(2)}) copy-start(s32[32]{0:T(128)} %param.23) | copy-start | bytes 388
  49.7 43.5 %copy-start.5 = (s32[32]{0:T(128)S(1)}, s32[32]{0:T(128)}, u32[]{:S(2)}) copy-start(s32[32]{0:T(128)} %param.22) | copy-start | bytes 388
  49.8 49.2 %copy-start.7 = (bf16[2048]{0:T(1024)(128)(2,1)S(1)}, bf16[2048]{0:T(1024)(128)(2,1)}, u32[]{:S(2)}) copy-start(bf16[2048]{0:T(1024)(128)(2,1)} %param.26) | copy-start | bytes 12292
  49.8 49.3 %copy-start.6 = (bf16[2048,12]{0,1:T(8,128)(2,1)S(1)}, bf16[2048,12]{0,1:T(8,128)(2,1)}, u32[]{:S(2)}) copy-start(bf16[2048,12]{0,1:T(8,128)(2,1)} %param.27) | copy-start | bytes 147460
  49.8 21.6 %all-to-all-start.1 = ((bf16[32,64,128]{2,1,0:T(8,128)(2,1)}), bf16[32,64,128]{2,1,0:T(8,128)(2,1)S(1)}, u32[]{:S(2)}, u32[]{:S(2)}) async-start(bf16[32,64,128]{2,1,0:T(8,128)(2,1)} %shard_map.147), calls=%async_computation.1 | async-start | bytes 1048576 | tf_op jit(solution)/shard_map/all_to_all | solution.py:319
  54.5 54.7 %copy-start.1 = (bf16[2048,128]{1,0:T(8,128)(2,1)S(1)}, bf16[2048,128]{1,0:T(8,128)(2,1)}, u32[]{:S(2)}) copy-start(bf16[2048,128]{1,0:T(8,128)(2,1)} %cross_u_ref.1) | copy-start | bytes 1572868
  54.5 54.7 %copy-start.2 = (bf16[128,2048]{1,0:T(8,128)(2,1)S(1)}, bf16[128,2048]{1,0:T(8,128)(2,1)}, u32[]{:S(2)}) copy-start(bf16[128,2048]{1,0:T(8,128)(2,1)} %cross_v_ref.1) | copy-start | bytes 1572868
  54.5 44.6 %collective-permute-start.3 = (bf16[3,2048,128]{2,1,0:T(8,128)(2,1)}, bf16[3,2048,128]{2,1,0:T(8,128)(2,1)}, u32[]{:S(2)}, u32[]{:S(2)}) collective-permute-start(bf16[3,2048,128]{2,1,0:T(8,128)(2,1)} %w0_ref.1), channel_id=1, source_target_pairs={{0,1},{1,0},{2,3},{3,2},{4,5},{5,4},{6,7},{7,6},{8,9},{9,8},{10,11... | collective-permute-start | bytes 4718600 | tf_op jit(solution)/shard_map/ppermute | solution.py:310
  56.6 3.7 %collective-permute-start.2 = (bf16[64,2048]{1,0:T(8,128)(2,1)S(1)}, bf16[64,2048]{1,0:T(8,128)(2,1)S(1)}, u32[]{:S(2)}, u32[]{:S(2)}) collective-permute-start(bf16[64,2048]{1,0:T(8,128)(2,1)S(1)} %copy-done.3), channel_id=1, source_target_pairs={{0,1},{1,0},{2,3},{3,2},{4,5},{5,4},{6,7},{7,6},{8,9},{9,8},{10,11... | collective-permute-start | bytes 786440 | tf_op jit(solution)/shard_map/ppermute | solution.py:310
  94.0 15.1 %all-to-all-start.3 = ((f32[64,2,128]{2,1,0:T(2,128)}), f32[64,2,128]{2,1,0:T(2,128)S(1)}, u32[]{:S(2)}, u32[]{:S(2)}) async-start(f32[64,2,128]{2,1,0:T(2,128)} %bitcast.6), calls=%async_computation.3 | async-start | bytes 131072 | tf_op jit(solution)/shard_map/all_to_all | solution.py:336
Sparse Core Ops, SparseCore 0:
  10.5 96.9 all-gather.2
